TPU v7x, 32 devices: a whole 2x2x4 slice. The times are simulated.
32 devices in a mesh: gx: 8 (over y, x, core), gy: 4 (over z).
Axes of the slice: x: 2, y: 2, z: 4, core: 2. Of those that a mesh axis runs over, the one named last changes fastest.
Arguments:
- velocity: float32 [3, 128, 64, 256], P(None, 'gx', 'gy'), may hold values from -6 to 6
- weights: bfloat16 [8, 4, 8, 3, 64, 128], P('gx', 'gy'), may hold values from 0 to 0.015625
- targets: bfloat16 [8, 4, 8, 3, 192], P('gx', 'gy'), may hold values from -5 to 5
- owner_list: int32 [8, 4, 8, 3], P('gx', 'gy'), may hold values from -1 to 511, as said below
- slot_patch: int32 [8, 4, 8, 3], P('gx', 'gy'), may hold values from -1 to 511, as said below
Outputs:
- velocity_new: float32 [3, 128, 64, 256], P(None, 'gx', 'gy')
- marker_force: float32 [8, 4, 8, 3, 192], P('gx', 'gy')
Inputs may be any that keep to these rules, and one draw needn't show every extreme that they name: owner_list[i, j, d, s] is the patch of tile (d, j) that slot s of owner (i, j) addresses, or -1 for an empty slot; every slot from every owner toward the footprint tiles d in [2, 2 + max(1, 1)), j in [1, 1 + max(1, 1)) is live; several slots may address one patch. slot_patch[d, j, i, s] = owner_list[i, j, d, s].
All inputs are finite; a program needn't handle non-finite values.
Results may differ from a plain program's by a relative error of at most 0.0003.
Values may be sent and summed in bfloat16 or wider, within the bound.
No kernel may reach another device: no remote copies, remote signals or barrier semaphores. Data moves between devices by JAX's collectives and lax.ppermute only.
A program may use at most 128 MiB of HBM per device.

v0:
```python
import jax
import jax.numpy as jnp
from jax import lax
from jax.sharding import PartitionSpec as P

time_step = 0.05
viscosity = 0.5
spread_gain = 0.5


def extended(x, sides, width):
    for axis, dim in sides:
        size, length = (lax.axis_size(axis), x.shape[dim])
        up = [(i, (i + 1) % size) for i in range(size)]
        down = [(j, i) for i, j in up]
        last = lax.slice_in_dim(x, length - width, length, axis=dim)
        initial = lax.slice_in_dim(x, 0, width, axis=dim)
        before = lax.ppermute(last, axis, up)
        after = lax.ppermute(initial, axis, down)
        x = jnp.concatenate([before, x, after], axis=dim)
    return x


def advance(padded):
    center = padded[:, 1:-1, 1:-1, 1:-1]
    fore_cell = padded[:, 2:, 1:-1, 1:-1]
    back_cell = padded[:, :-2, 1:-1, 1:-1]
    right_cell = padded[:, 1:-1, 2:, 1:-1]
    left_cell = padded[:, 1:-1, :-2, 1:-1]
    top_cell = padded[:, 1:-1, 1:-1, 2:]
    bottom_cell = padded[:, 1:-1, 1:-1, :-2]
    laplace = fore_cell + back_cell + right_cell + left_cell + top_cell + bottom_cell - 6.0 * center
    advect = (
        center[0:1] * (fore_cell - back_cell) * 0.5
        + center[1:2] * (right_cell - left_cell) * 0.5
        + center[2:3] * (top_cell - bottom_cell) * 0.5
    )
    return center + time_step * (viscosity * laplace - advect)


def forcing(block_w, chosen, target_rows, live):
    count_s = block_w.shape[1]
    markers = block_w.shape[2]
    interp = jnp.einsum("isbp,iscp->iscb", block_w, chosen, preferred_element_type=jnp.float32)
    target = jnp.transpose(
        target_rows.astype(jnp.float32).reshape(block_w.shape[0], 3, count_s, markers), (0, 2, 1, 3)
    )
    force = jnp.where(live[:, :, None, None], (target - interp) / time_step, 0.0)
    force_low = force.astype(jnp.bfloat16)
    spread = jnp.einsum("iscb,isbp->iscp", force_low, block_w, preferred_element_type=jnp.float32)
    spread = jnp.where(live[:, :, None, None], spread, 0.0)
    return (force, spread)


def shards(velocity, weights, targets, owner_list, slot_patch):
    size_y = velocity.shape[2]
    size_z = velocity.shape[3]
    count_d = weights.shape[2]
    count_s = weights.shape[3]
    markers = weights.shape[4]
    layers_z = size_z // 8
    columns_y = size_y // 4
    incoming = slot_patch[0, 0]
    in_live = incoming >= 0
    in_safe = jnp.maximum(incoming, 0).reshape(-1)
    own_ids = owner_list[0, 0]
    own_live = own_ids >= 0
    corner_x = 4 * (in_safe // (columns_y * layers_z))
    corner_y = 4 * (in_safe // layers_z % columns_y)
    corner_z = 8 * (in_safe % layers_z)
    index_x = corner_x[:, None, None, None] + jnp.arange(4, dtype=jnp.int32)[None, :, None, None]
    index_y = corner_y[:, None, None, None] + jnp.arange(4, dtype=jnp.int32)[None, None, :, None]
    index_z = corner_z[:, None, None, None] + jnp.arange(8, dtype=jnp.int32)[None, None, None, :]
    block_w, target_rows = (
        lax.all_to_all(weights[0, 0], "gx", split_axis=0, concat_axis=0, tiled=True),
        lax.all_to_all(targets[0, 0], "gx", split_axis=0, concat_axis=0, tiled=True),
    )
    padded = extended(velocity, (("gx", 1), ("gy", 2)), 1)
    padded = jnp.pad(padded, ((0, 0), (0, 0), (0, 0), (1, 1)))
    predicted = advance(padded)
    windows = predicted[:, index_x, index_y, index_z].astype(jnp.bfloat16)
    chosen = jnp.transpose(windows.reshape(3, count_d, count_s, 128), (1, 2, 0, 3))
    force, spread = forcing(block_w, chosen, target_rows, in_live)
    back_rows = jnp.transpose(force, (0, 2, 1, 3)).reshape(count_d, 3, count_s * markers)
    returned = lax.all_to_all(back_rows, "gx", split_axis=0, concat_axis=0, tiled=True)
    addition = jnp.transpose(spread.reshape(count_d * count_s, 3, 4, 4, 8), (1, 0, 2, 3, 4))
    velocity_new = predicted.at[:, index_x, index_y, index_z].add(
        time_step * spread_gain * addition
    )
    own_mask = jnp.repeat(own_live, markers, axis=1)[:, None, :]
    marker_force = jnp.where(own_mask, returned, 0.0)[None, None]
    return (velocity_new, marker_force)


def solution(mesh):
    return jax.shard_map(
        shards,
        mesh=mesh,
        in_specs=(
            P(None, "gx", "gy", None),
            P("gx", "gy", None, None, None, None),
            P("gx", "gy", None, None, None),
            P("gx", "gy", None, None),
            P("gx", "gy", None, None),
        ),
        out_specs=(P(None, "gx", "gy", None), P("gx", "gy", None, None, None)),
        check_vma=False,
    )
```

profile of v0, /device:TPU:0, one launch (start us, length us, event | category | flops | bytes accessed | tf_op | source)
XLA Modules:
  0.0 147.1 jit_solution(8521462902874299344)
XLA Ops:
  0.6 0.0 copy-start.7
  0.6 0.0 copy-start.8
  0.7 0.0 copy-start
  0.7 1.4 copy.246
  2.1 5.2 %all-to-all-start = ((bf16[8,3,192]{2,1,0:T(4,128)(2,1)}), bf16[8,3,192]{2,1,0:T(4,128)(2,1)S(1)}, u32[]{:S(2)}, u32[]{:S(2)}) async-start(bf16[8,3,192]{2,1,0:T(4,128)(2,1)} %bitcast.51), calls=%async_computation | async-start | bytes 32768 | tf_op jit(solution)/shard_map/all_to_all | solution.py:76
  7.2 0.8 fusion.21
  8.1 2.7 %collective-permute-start = (f32[3,1,16,256]{3,2,1,0:T(8,128)S(1)}, f32[3,1,16,256]{3,2,1,0:T(8,128)S(1)}, u32[]{:S(2)}, u32[]{:S(2)}) collective-permute-start(f32[3,1,16,256]{3,2,1,0:T(8,128)S(1)} %get-tuple-element.21), channel_id=1, source_target_pairs={{4,0},{8,4},{12,8},{16,12},{20,16},{24,20},{28,24},{0,28},{5,1},{9... | collective-permute-start | bytes 147464 | tf_op jit(solution)/shard_map/ppermute | solution.py:19
  10.8 0.0 collective-permute-start.1
  10.8 0.7 broadcast_compare_fusion.1
  11.5 0.7 broadcast_shift-right-logical_fusion.1
  12.2 1.9 %slice_bitcast_fusion.2 = (f32[16,16,256]{2,1,0:T(8,128)S(1)}, f32[16,16,256]{2,1,0:T(8,128)S(1)}, f32[16,16,256]{2,1,0:T(8,128)}) fusion(f32[3,16,16,256]{3,2,1,0:T(8,128)} %param.5), kind=kLoop, calls=%fused_computation.16 | loop fusion | bytes 1572864 | tf_op jit(solution)/shard_map/mul | solution.py:34
  14.0 0.1 copy.201
  14.1 0.1 ne.69
  14.2 0.1 copy.200
  14.3 0.1 ne.67
  14.4 0.1 copy.202
  14.5 0.1 div.28
  14.6 0.1 copy.203
  14.7 0.1 rem.44
  14.7 0.1 copy.204
  14.8 0.1 div.31
  14.9 0.1 copy.212
  15.0 0.1 copy.211
  15.1 0.1 copy.210
  15.2 0.1 fusion.7
  15.4 0.1 fusion.5
  15.5 0.2 or_or_fusion
  15.7 0.1 copy.230
  15.8 0.1 broadcast_in_dim.85
  15.9 0.1 broadcast_in_dim.86
  16.0 0.1 copy.206
  16.1 0.2 copy.205
  16.2 0.2 reshape.173
  16.4 0.2 reshape.167
  16.6 0.0 collective-permute-done.1
  16.7 0.1 constant_dynamic-update-slice_fusion.1
  16.8 0.0 collective-permute-done
  16.8 0.1 fusion.20
  16.9 0.4 copy-done.3
  17.3 0.1 copy-done.1
  17.4 1.6 %collective-permute-start.3 = (f32[3,18,1,256]{3,2,1,0:T(1,128)S(1)}, f32[3,18,1,256]{3,2,1,0:T(1,128)S(1)}, u32[]{:S(2)}, u32[]{:S(2)}) collective-permute-start(f32[3,18,1,256]{3,2,1,0:T(1,128)S(1)} %get-tuple-element.16), channel_id=1, source_target_pairs={{0,1},{1,2},{2,3},{3,0},{4,5},{5,6},{6,7},{7,4},{8,9},{9,10},{10,1... | collective-permute-start | bytes 165896 | tf_op jit(solution)/shard_map/ppermute | solution.py:18
  18.9 2.2 %collective-permute-start.2 = (f32[3,18,1,256]{3,2,1,0:T(1,128)S(1)}, f32[3,18,1,256]{3,2,1,0:T(1,128)S(1)}, u32[]{:S(2)}, u32[]{:S(2)}) collective-permute-start(f32[3,18,1,256]{3,2,1,0:T(1,128)S(1)} %get-tuple-element.17), channel_id=1, source_target_pairs={{1,0},{2,1},{3,2},{0,3},{5,4},{6,5},{7,6},{4,7},{9,8},{10,9},{11,1... | collective-permute-start | bytes 165896 | tf_op jit(solution)/shard_map/ppermute | solution.py:19
  21.2 0.0 all-to-all-done
  21.2 3.5 %all-to-all-start.1 = ((bf16[8,3,64,128]{3,2,1,0:T(8,128)(2,1)}), bf16[8,3,64,128]{3,2,1,0:T(8,128)(2,1)S(1)}, u32[]{:S(2)}, u32[]{:S(2)}) async-start(bf16[8,3,64,128]{3,2,1,0:T(8,128)(2,1)} %bitcast.9), calls=%async_computation.1 | async-start | bytes 786432 | tf_op jit(solution)/shard_map/all_to_all | solution.py:75
  24.7 0.7 reshape.166
  25.4 0.0 collective-permute-done.3
  25.4 0.0 collective-permute-done.2
  25.4 1.0 select_maximum_fusion
  26.4 1.9 %multiply_add_fusion = f32[3,16,16,256]{3,2,1,0:T(8,128)S(1)} fusion(f32[3,16,16,256]{3,2,1,0:T(8,128)S(1)} %copy-done, f32[3,18,18,258]{3,2,1,0:T(8,128)S(1)} %select_maximum_fusion, f32[3,18,16,256]{3,2,1,0:T(8,128)S(1)} %constant_dynamic-update-slice_fusion, f32[3,18,1,256]{3,2,1,0:T(1,128)S(1)} %collective-permute-done.3, ...), kind=kLoop, calls=%fused_computation.13 | loop fusion | flops 4718592 | bytes 5025792 | tf_op jit(solution)/shard_map/add | solution.py:38
  28.3 16.6 %copy.228 = f32[3,16,16,256]{0,3,2,1:T(8,128)} copy(f32[3,16,16,256]{3,2,1,0:T(8,128)S(1)} %multiply_add_fusion) | data formatting | bytes 1572864
  45.0 33.1 %gather_fusion = bf16[3072,3]{1,0:T(8,128)(2,1)S(1)} fusion(f32[3,16,16,256]{0,3,2,1:T(8,128)} %copy.228, s32[3072]{0:T(1024)S(1)} %reshape.167), kind=kCustom, calls=%fused_computation | custom fusion | bytes 73728 | tf_op jit(solution)/shard_map/gather | solution.py:81
  78.0 2.5 %copy.214 = bf16[24,4,4,8,3]{3,2,1,0,4:T(4,128)(2,1)S(1)} copy(bf16[24,4,4,8,3]{4,3,2,1,0:T(8,128)(2,1)S(1)} %bitcast.57) | data formatting | bytes 36864 | tf_op jit(solution)/shard_map/convert_element_type | solution.py:81
  80.6 0.3 convert_element_type.14
  80.9 0.3 fusion.14
  81.2 0.1 fusion.9
  81.3 0.7 reshape.180
  82.1 4.1 %all-to-all-start.2 = ((f32[8,3,192]{2,1,0:T(4,128)}), f32[8,3,192]{2,1,0:T(4,128)S(1)}, u32[]{:S(2)}, u32[]{:S(2)}) async-start(f32[8,3,192]{2,1,0:T(4,128)} %reshape.180), calls=%async_computation.2 | async-start | bytes 65536 | tf_op jit(solution)/shard_map/all_to_all | solution.py:85
  86.2 0.2 fusion.1
  86.4 0.7 mul.103
  87.2 2.3 %copy.229 = f32[24,4,4,8,3]{4,3,2,1,0:T(8,128)S(1)} copy(f32[24,4,4,8,3]{3,2,1,4,0:T(4,128)S(1)} %bitcast.56) | data formatting | bytes 73728 | tf_op jit(solution)/shard_map/mul | solution.py:88
  89.5 36.8 %scatter_fusion = f32[3,65536]{0,1:T(8,128)} fusion(f32[3,65536]{0,1:T(8,128)} %bitcast.53, s32[3072]{0:T(1024)S(1)} %reshape.173, f32[3072,3]{1,0:T(8,128)S(1)} %bitcast.55), kind=kCustom, calls=%fused_computation.1 | custom fusion | flops 9216 | bytes 122880
  126.3 20.2 %copy.226 = f32[3,16,16,256]{3,2,1,0:T(8,128)} copy(f32[3,16,16,256]{0,3,2,1:T(8,128)} %bitcast.54) | data formatting | bytes 1572864
  146.5 0.0 all-to-all-done.2
  146.5 0.6 copy.227
  (28 shorter events, 0.2 us)
Async XLA Ops:
  0.6 14.6 %copy-start.7 = (s32[3]{0:T(128)S(1)}, s32[3]{0:T(128)}, u32[]{:S(2)}) copy-start(s32[3]{0:T(128)} %constant.91) | copy-start | bytes 40
  0.6 14.7 %copy-start.8 = (s32[3]{0:T(128)S(1)}, s32[3]{0:T(128)}, u32[]{:S(2)}) copy-start(s32[3]{0:T(128)} %constant.88) | copy-start | bytes 40
  0.7 16.0 %copy-start = (f32[3,16,16,256]{3,2,1,0:T(8,128)S(1)}, f32[3,16,16,256]{3,2,1,0:T(8,128)}, u32[]{:S(2)}) copy-start(f32[3,16,16,256]{3,2,1,0:T(8,128)} %param.5) | copy-start | bytes 2359300
  0.7 15.0 %copy-start.6 = (s32[1,1,8,3]{2,1,3,0:T(1,128)S(1)}, s32[1,1,8,3]{2,1,3,0:T(1,128)}, u32[]{:S(2)}) copy-start(s32[1,1,8,3]{2,1,3,0:T(1,128)} %param.8) | copy-start | bytes 292
  2.1 19.1 %all-to-all-start = ((bf16[8,3,192]{2,1,0:T(4,128)(2,1)}), bf16[8,3,192]{2,1,0:T(4,128)(2,1)S(1)}, u32[]{:S(2)}, u32[]{:S(2)}) async-start(bf16[8,3,192]{2,1,0:T(4,128)(2,1)} %bitcast.51), calls=%async_computation | async-start | bytes 32768 | tf_op jit(solution)/shard_map/all_to_all | solution.py:76
  8.1 8.7 %collective-permute-start = (f32[3,1,16,256]{3,2,1,0:T(8,128)S(1)}, f32[3,1,16,256]{3,2,1,0:T(8,128)S(1)}, u32[]{:S(2)}, u32[]{:S(2)}) collective-permute-start(f32[3,1,16,256]{3,2,1,0:T(8,128)S(1)} %get-tuple-element.21), channel_id=1, source_target_pairs={{4,0},{8,4},{12,8},{16,12},{20,16},{24,20},{28,24},{0,28},{5,1},{9... | collective-permute-start | bytes 147464 | tf_op jit(solution)/shard_map/ppermute | solution.py:19
  10.8 5.9 %collective-permute-start.1 = (f32[3,1,16,256]{3,2,1,0:T(8,128)S(1)}, f32[3,1,16,256]{3,2,1,0:T(8,128)S(1)}, u32[]{:S(2)}, u32[]{:S(2)}) collective-permute-start(f32[3,1,16,256]{3,2,1,0:T(8,128)S(1)} %get-tuple-element.22), channel_id=1, source_target_pairs={{0,4},{4,8},{8,12},{12,16},{16,20},{20,24},{24,28},{28,0},{1,5},{5... | collective-permute-start | bytes 147464 | tf_op jit(solution)/shard_map/ppermute | solution.py:18
  16.7 0.6 copy-start.3
  16.8 0.6 copy-start.1
  17.4 8.0 %collective-permute-start.3 = (f32[3,18,1,256]{3,2,1,0:T(1,128)S(1)}, f32[3,18,1,256]{3,2,1,0:T(1,128)S(1)}, u32[]{:S(2)}, u32[]{:S(2)}) collective-permute-start(f32[3,18,1,256]{3,2,1,0:T(1,128)S(1)} %get-tuple-element.16), channel_id=1, source_target_pairs={{0,1},{1,2},{2,3},{3,0},{4,5},{5,6},{6,7},{7,4},{8,9},{9,10},{10,1... | collective-permute-start | bytes 165896 | tf_op jit(solution)/shard_map/ppermute | solution.py:18
  18.9 6.4 %collective-permute-start.2 = (f32[3,18,1,256]{3,2,1,0:T(1,128)S(1)}, f32[3,18,1,256]{3,2,1,0:T(1,128)S(1)}, u32[]{:S(2)}, u32[]{:S(2)}) collective-permute-start(f32[3,18,1,256]{3,2,1,0:T(1,128)S(1)} %get-tuple-element.17), channel_id=1, source_target_pairs={{1,0},{2,1},{3,2},{0,3},{5,4},{6,5},{7,6},{4,7},{9,8},{10,9},{11,1... | collective-permute-start | bytes 165896 | tf_op jit(solution)/shard_map/ppermute | solution.py:19
  21.2 59.7 %all-to-all-start.1 = ((bf16[8,3,64,128]{3,2,1,0:T(8,128)(2,1)}), bf16[8,3,64,128]{3,2,1,0:T(8,128)(2,1)S(1)}, u32[]{:S(2)}, u32[]{:S(2)}) async-start(bf16[8,3,64,128]{3,2,1,0:T(8,128)(2,1)} %bitcast.9), calls=%async_computation.1 | async-start | bytes 786432 | tf_op jit(solution)/shard_map/all_to_all | solution.py:75
  25.4 1.0 copy-start.2
  25.4 1.1 copy-start.4
  45.0 36.3 %copy-start.5 = (f32[8,3,3,64]{3,2,0,1:T(4,128)S(1)}, f32[8,3,3,64]{3,2,0,1:T(4,128)}, u32[]{:S(2)}) copy-start(f32[8,3,3,64]{3,2,0,1:T(4,128)} %reshape.166) | copy-start | bytes 55300
  82.1 64.4 %all-to-all-start.2 = ((f32[8,3,192]{2,1,0:T(4,128)}), f32[8,3,192]{2,1,0:T(4,128)S(1)}, u32[]{:S(2)}, u32[]{:S(2)}) async-start(f32[8,3,192]{2,1,0:T(4,128)} %reshape.180), calls=%async_computation.2 | async-start | bytes 65536 | tf_op jit(solution)/shard_map/all_to_all | solution.py:85
where the time goes:
time: 148 us; the launch traced here: 147 us
  local copies, waits for them, and re-layouts  84.7 us (57%)
  other arithmetic  41.7 us (28%)
  starting transfers between devices  19.3 us (13%)
    unnamed x27, local copies, waits for them, and re-layouts  39.8 us
    unnamed x4, other arithmetic  37 us
    gather x1, local copies, waits for them, and re-layouts, shards(): windows = predicted[:, index_x, index_y, index_z].astype(jnp.bfloat16)  33.1 us
    all_to_all x1, starting transfers between devices, shards(): lax.all_to_all(targets[0, 0], 'gx', split_axis=0, concat_axis=0, tiled=True)  5.17 us
    ppermute x2, starting transfers between devices, extended(): after = lax.ppermute(initial, axis, down)  4.96 us
    all_to_all x1, starting transfers between devices, shards(): lax.all_to_all(back_rows, 'gx', split_axis=0, concat_axis=0, tiled=True)  4.14 us
    all_to_all x1, starting transfers between devices, shards(): lax.all_to_all(weights[0, 0], 'gx', split_axis=0, concat_axis=0, tiled=True)  3.45 us
    mul x2, local copies, waits for them, and re-layouts, shards(): time_step * spread_gain * addition  3.04 us
  transfers between devices with their start and end apart: 7, of which 0 were waited for; matrix products, arithmetic and copies ran while one was open for 84% of the time, Pallas kernels for 0%

commit v1 on v0

v1 whole, which is shorter than its diff:
```python
import functools

import jax
import jax.numpy as jnp
from jax import lax
from jax.experimental import pallas as pl
from jax.experimental.pallas import tpu as pltpu
from jax.sharding import PartitionSpec as P

time_step = 0.05
viscosity = 0.5
spread_gain = 0.5

VMEM = pltpu.VMEM
F32 = jnp.float32
BF16 = jnp.bfloat16


def each(count, body):
    if count <= 8:
        for i in range(count):
            body(i)
    else:

        def step(i, carry):
            body(i)
            return carry

        lax.fori_loop(0, count, step, 0)


def pack_kernel(dims, vel, w, t, chunk, x_first, x_last, y_first, y_last, held, rows, packed, sems):
    size_x, size_y, count_d, width = dims
    move_w = pltpu.make_async_copy(w, chunk.at[:, pl.ds(0, width), :], sems.at[0])
    halves = held.shape[0]
    moves = [
        pltpu.make_async_copy(vel.at[:, pl.ds(part * 128, 128)], held.at[part], sems.at[2 + part])
        for part in range(halves)
    ]
    for move in moves:
        move.start()
    move_w.start()
    rows[...] = jnp.zeros_like(rows)

    def one(i):
        values = t[i].astype(F32)
        rows[i, 0:3, :] = values[:, 0:128]
        rows[i, 8:11, 0 : width - 128] = values[:, 128:width]

    each(count_d, one)
    packed[...] = rows[...].astype(BF16)
    move_t = pltpu.make_async_copy(packed, chunk.at[:, pl.ds(width, 16), :], sems.at[1])
    move_t.start()
    plane = size_x * size_y
    for part in range(halves):
        moves[part].wait()
        lanes = pl.ds(part * 128, 128)
        for c in range(3):
            x_first[c, :, lanes] = held[part, pl.ds(c * plane, size_y), :]
            x_last[c, :, lanes] = held[part, pl.ds(c * plane + plane - size_y, size_y), :]
            y_first[c, :, lanes] = held[part, pl.ds(c * plane, size_x, stride=size_y), :]
            y_last[c, :, lanes] = held[part, pl.ds(c * plane + size_y - 1, size_x, stride=size_y), :]
    move_t.wait()
    move_w.wait()


def main_kernel(
    dims, slots, vel, x_before, x_after, y_before, y_after, chunk, out, force_out,
    held, field, blocks, chosen, sems,
):
    size_x, size_y, size_z, count_d, count_s, width = dims
    move_v = pltpu.make_async_copy(vel, held, sems.at[0])
    move_w = pltpu.make_async_copy(chunk, blocks, sems.at[1])
    move_v.start()
    move_w.start()
    columns_y = size_y // 4
    layers_z = size_z // 8
    markers = width // count_s

    row = lax.broadcasted_iota(jnp.int32, (size_y, size_z), 0)
    col = lax.broadcasted_iota(jnp.int32, (size_y, size_z), 1)
    move_v.wait()
    for x in range(size_x):
        center, fore, back, right, left, top, bottom = [], [], [], [], [], [], []
        for c in range(3):
            base = (c * size_x + x) * size_y
            here = held[pl.ds(base, size_y), :]
            center.append(here)
            fore.append(x_after[c] if x == size_x - 1 else held[pl.ds(base + size_y, size_y), :])
            back.append(x_before[c] if x == 0 else held[pl.ds(base - size_y, size_y), :])
            right.append(
                jnp.where(row == size_y - 1, y_after[c, pl.ds(x, 1), :], pltpu.roll(here, size_y - 1, 0))
            )
            left.append(jnp.where(row == 0, y_before[c, pl.ds(x, 1), :], pltpu.roll(here, 1, 0)))
            top.append(jnp.where(col == size_z - 1, 0.0, pltpu.roll(here, size_z - 1, 1)))
            bottom.append(jnp.where(col == 0, 0.0, pltpu.roll(here, 1, 1)))
        for c in range(3):
            laplace = fore[c] + back[c] + right[c] + left[c] + top[c] + bottom[c] - 6.0 * center[c]
            advect = (
                center[0] * (fore[c] - back[c]) * 0.5
                + center[1] * (right[c] - left[c]) * 0.5
                + center[2] * (top[c] - bottom[c]) * 0.5
            )
            base = (c * size_x + x) * size_y
            field[pl.ds(base, size_y), :] = center[c] + time_step * (viscosity * laplace - advect)

    lane = lax.broadcasted_iota(jnp.int32, (8, 128), 1)
    sub = lax.broadcasted_iota(jnp.int32, (8, 128), 0)
    lane_x = lane // 32
    sub_half = jnp.where((lane // 8) % 4 == sub % 4, sub // 4, -1)
    odd = sub % 2 == 1
    upper = sub % 4 >= 2

    def place(i, s):
        safe = jnp.maximum(slots[0, 0, i, s], 0)
        qx = safe // (columns_y * layers_z)
        qy = safe // layers_z % columns_y
        qz = safe % layers_z
        first = qx * (4 * size_y) + (qy // 2) * 8
        half = qy % 2
        lanes = pl.ds(pl.multiple_of((qz // 16) * 128, 128), 128)
        shift = 8 * (qz % 16)
        return first, half, lanes, shift

    def spot(first, c, ax, lanes):
        return pl.ds(pl.multiple_of(first + (c * size_x + ax) * size_y, 8), 8), lanes

    def gather(i):
        for s in range(count_s):
            first, half, lanes, shift = place(i, s)
            wanted = sub_half == half
            picked = jnp.zeros((8, 128), F32)
            for c in range(3):
                merged = None
                for ax in range(4):
                    piece = field[spot(first, c, ax, lanes)]
                    piece = pltpu.roll(piece, (128 + 32 * ax - shift) % 128, 1)
                    merged = piece if ax == 0 else jnp.where(lane_x == ax, piece, merged)
                merged = jnp.where(odd, pltpu.roll(merged, 8, 1), merged)
                merged = jnp.where(upper, pltpu.roll(merged, 16, 1), merged)
                line = jnp.sum(jnp.where(wanted, merged, 0.0), axis=0, keepdims=True)
                picked = jnp.where(sub == c, line, picked)
            chosen[i, pl.ds(8 * s, 8), :] = picked

    each(count_d, gather)
    move_w.wait()
    slot_of = lax.broadcasted_iota(jnp.int32, (8, width), 1) // markers

    def force_and_spread(i):
        block_w = blocks[i, 0:width, :]
        tail = blocks[i, width : width + 16, :].astype(F32)
        target = jnp.concatenate([tail[0:8, :], tail[8:16, 0 : width - 128]], axis=1)
        product = lax.dot_general(
            chosen[i].astype(BF16), block_w, (((1,), (1,)), ((), ())), preferred_element_type=F32
        )
        interp = product[0:8]
        live = jnp.full((8, width), slots[0, 0, i, 0], jnp.int32)
        for s in range(1, count_s):
            interp = jnp.where(slot_of == s, product[8 * s : 8 * s + 8], interp)
            live = jnp.where(slot_of == s, slots[0, 0, i, s], live)
        force = jnp.where(live >= 0, (target - interp) / time_step, 0.0)
        force_out[i] = force[0:3, :]
        rows = jnp.concatenate([jnp.where(slot_of == s, force, 0.0) for s in range(count_s)], axis=0)
        chosen[i] = jnp.dot(rows.astype(BF16), block_w, preferred_element_type=F32)

    each(count_d, force_and_spread)

    def scatter(i):
        for s in range(count_s):
            first, half, lanes, shift = place(i, s)
            wanted = sub_half == half
            rows = chosen[i, pl.ds(8 * s, 8), :] * (time_step * spread_gain)
            for c in range(3):
                line = jnp.where(wanted, rows[c : c + 1, :], 0.0)
                line = jnp.where(odd, pltpu.roll(line, 120, 1), line)
                line = jnp.where(upper, pltpu.roll(line, 112, 1), line)
                for ax in range(4):
                    piece = jnp.where(lane_x == ax, line, 0.0)
                    piece = pltpu.roll(piece, (128 + shift - 32 * ax) % 128, 1)
                    at = spot(first, c, ax, lanes)
                    field[at] = field[at] + piece

    each(count_d, scatter)
    pltpu.sync_copy(field, out)


def shards(velocity, weights, targets, owner_list, slot_patch):
    size_x, size_y, size_z = velocity.shape[1:]
    count_d, count_s, markers = weights.shape[2:5]
    width = count_s * markers
    cells = 3 * size_x * size_y
    vel = velocity.reshape(cells, size_z)
    block_w = weights.reshape(count_d, width, 128)
    anywhere = pl.BlockSpec(memory_space=pl.ANY)
    inside = pl.BlockSpec(memory_space=VMEM)
    face_x = jax.ShapeDtypeStruct((3, size_y, size_z), F32)
    face_y = jax.ShapeDtypeStruct((3, size_x, size_z), F32)
    chunk, x_first, x_last, y_first, y_last = pl.pallas_call(
        functools.partial(pack_kernel, (size_x, size_y, count_d, width)),
        out_shape=(
            jax.ShapeDtypeStruct((count_d, width + 16, 128), BF16),
            face_x, face_x, face_y, face_y,
        ),
        in_specs=[anywhere, anywhere, inside],
        out_specs=(anywhere, inside, inside, inside, inside),
        scratch_shapes=[
            VMEM((size_z // 128, cells, 128), F32),
            VMEM((count_d, 16, 128), F32),
            VMEM((count_d, 16, 128), BF16),
            pltpu.SemaphoreType.DMA((2 + size_z // 128,)),
        ],
        compiler_params=pltpu.CompilerParams(vmem_limit_bytes=16 * 2**20),
        name="pack",
    )(vel, block_w, targets.reshape(count_d, 3, width))

    def ring(x, axis, step):
        size = lax.axis_size(axis)
        return lax.ppermute(x, axis, [(i, (i + step) % size) for i in range(size)])

    y_before = ring(y_last, "gy", 1)
    y_after = ring(y_first, "gy", -1)
    x_before = ring(x_last, "gx", 1)
    x_after = ring(x_first, "gx", -1)
    arrived = lax.all_to_all(chunk, "gx", split_axis=0, concat_axis=0, tiled=True)
    out, force = pl.pallas_call(
        functools.partial(main_kernel, (size_x, size_y, size_z, count_d, count_s, width)),
        out_shape=(
            jax.ShapeDtypeStruct((cells, size_z), F32),
            jax.ShapeDtypeStruct((count_d, 3, width), F32),
        ),
        in_specs=[
            pl.BlockSpec(memory_space=pltpu.SMEM),
            anywhere, inside, inside, inside, inside, anywhere,
        ],
        out_specs=(anywhere, inside),
        scratch_shapes=[
            VMEM((cells, size_z), F32),
            VMEM((cells, size_z), F32),
            VMEM((count_d, width + 16, 128), BF16),
            VMEM((count_d, 8 * count_s, 128), F32),
            pltpu.SemaphoreType.DMA((2,)),
        ],
        compiler_params=pltpu.CompilerParams(vmem_limit_bytes=16 * 2**20),
        name="main",
    )(slot_patch, vel, x_before, x_after, y_before, y_after, arrived)
    returned = lax.all_to_all(force, "gx", split_axis=0, concat_axis=0, tiled=True)
    return out.reshape(velocity.shape), returned[None, None]


def solution(mesh):
    return jax.shard_map(
        shards,
        mesh=mesh,
        in_specs=(
            P(None, "gx", "gy", None),
            P("gx", "gy", None, None, None, None),
            P("gx", "gy", None, None, None),
            P("gx", "gy", None, None),
            P("gx", "gy", None, None),
        ),
        out_specs=(P(None, "gx", "gy", None), P("gx", "gy", None, None, None)),
        check_vma=False,
    )
```

time: 148 us -> 40.7 us (0.28)
  local copies, waits for them, and re-layouts: 84.7 us -> 3.54 us
  other arithmetic: 41.7 us -> 0 us
  Pallas kernels: 0 us -> 14.2 us
  starting transfers between devices: 19.3 us -> 11.7 us
  blocking collectives: 0 us -> 7.48 us
  waiting for transfers between devices: 0.02 us -> 2.63 us
    unnamed x4 -> x0, other arithmetic: 37 us -> none
    unnamed x27 -> x11, local copies, waits for them, and re-layouts: 39.8 us -> 3.54 us
    gather x1 -> x0, local copies, waits for them, and re-layouts: 33.1 us -> none  [shards(): windows = predicted[:, index_x, index_y, index_z].astype(jnp.bfloat16)]
    pallas_call x0 -> x2, Pallas kernels: none -> 14.2 us  [the longest x1 13.4 us: shards(): pl.pallas_call(functools.partial(main_kernel, (size_x, size_y, size_z, co...]
    all_to_all x3 -> x1, starting transfers between devices: 12.8 us -> 5.18 us  [shards(): lax.all_to_all(chunk, 'gx', split_axis=0, concat_axis=0, tiled=True)]
    all_to_all x0 -> x1, blocking collectives: none -> 7.48 us  [shards(): lax.all_to_all(force, 'gx', split_axis=0, concat_axis=0, tiled=True)]
    mul x3 -> x0, local copies, waits for them, and re-layouts: 4.9 us -> none  [the longest x2 3.04 us: shards(): time_step * spread_gain * addition]
    convert_element_type x2 -> x0, local copies, waits for them, and re-layouts: 2.88 us -> none  [shards(): windows = predicted[:, index_x, index_y, index_z].astype(jnp.bfloat16)]
  transfers between devices with their start and end apart: 7 -> 5, of which waited for: 0 -> 1; matrix products, arithmetic and copies ran while one was open for 84% -> 0% of each run, Pallas kernels for 0% -> 0%
where the time goes in v1:
time: 40.7 us; the launch traced here: 40.3 us
  Pallas kernels  14.2 us (35%)
  starting transfers between devices  11.7 us (29%)
  blocking collectives  7.48 us (18%)
  local copies, waits for them, and re-layouts  3.54 us (9%)
  waiting for transfers between devices  2.63 us (6%)
  between operations  0.68 us (2%)
    pallas_call x1, Pallas kernels, shards(): pl.pallas_call(functools.partial(main_kernel, (size_x, size_y, size_z, co...  13.4 us
    all_to_all x1, blocking collectives, shards(): lax.all_to_all(force, 'gx', split_axis=0, concat_axis=0, tiled=True)  7.48 us
    ppermute x4, starting transfers between devices, ring(): return lax.ppermute(x, axis, [(i, (i + step) % size) for i in range(size)])  6.56 us
    all_to_all x1, starting transfers between devices, shards(): lax.all_to_all(chunk, 'gx', split_axis=0, concat_axis=0, tiled=True)  5.18 us
    unnamed x11, local copies, waits for them, and re-layouts  3.54 us
    ppermute x4, waiting for transfers between devices, ring(): return lax.ppermute(x, axis, [(i, (i + step) % size) for i in range(size)])  2.63 us
    pallas_call x1, Pallas kernels, shards(): pl.pallas_call(functools.partial(pack_kernel, (size_x, size_y, count_d, w...  0.83 us
  transfers between devices with their start and end apart: 5, of which 1 were waited for; matrix products, arithmetic and copies ran while one was open for 0% of the time, Pallas kernels for 0%

profile of v1, /device:TPU:0, one launch (start us, length us, event | category | flops | bytes accessed | tf_op | source)
XLA Modules:
  0.0 40.3 jit_solution(268592916880485444)
XLA Ops:
  0.6 0.7 %copy.10 = bf16[1,1,8,3,192]{4,3,2,1,0:T(4,128)(2,1)S(1)} copy(bf16[1,1,8,3,192]{4,2,3,1,0:T(8,128)(2,1)} %param.7) | data formatting | bytes 18432 | tf_op args[2]
  1.3 0.0 copy-start
  1.3 1.1 %copy-done = f32[3,16,16,256]{3,2,1,0:T(8,128)S(1)} copy-done((f32[3,16,16,256]{3,2,1,0:T(8,128)S(1)}, f32[3,16,16,256]{3,2,1,0:T(8,128)}, u32[]{:S(2)}) %copy-start) | copy-done | bytes 786456
  2.5 0.0 copy-start.2
  2.5 1.0 %copy-done.2 = bf16[1,1,8,3,64,128]{5,4,3,2,1,0:T(8,128)(2,1)S(1)} copy-done((bf16[1,1,8,3,64,128]{5,4,3,2,1,0:T(8,128)(2,1)S(1)}, bf16[1,1,8,3,64,128]{5,4,3,2,1,0:T(8,128)(2,1)}, u32[]{:S(2)}) %copy-start.2) | copy-done | bytes 393240
  3.5 0.0 copy-start.1
  3.5 0.8 %pack.1 = (bf16[8,208,128]{2,1,0:T(8,128)(2,1)}, f32[3,16,256]{2,1,0:T(8,128)S(1)}, f32[3,16,256]{2,1,0:T(8,128)S(1)}, f32[3,16,256]{2,1,0:T(8,128)S(1)}, f32[3,16,256]{2,1,0:T(8,128)S(1)}) custom-call(f32[768,256]{1,0:T(8,128)S(1)} %bitcast.7, bf16[8,192,128]{2,1,0:T(8,128)(2,1)S(1)} %bitcast.9, bf16[8,3,192]{2,1,0:T(4,128)(2,1)S(1)} %bitcast.10), custom_call_target="tpu_custom_call" | custom-call | tf_op jit(solution)/shard_map/pack/pallas_call | solution.py:198
  4.3 5.2 %all-to-all-start = ((bf16[8,208,128]{2,1,0:T(8,128)(2,1)}), bf16[8,208,128]{2,1,0:T(8,128)(2,1)S(1)}, u32[]{:S(2)}, u32[]{:S(2)}) async-start(bf16[8,208,128]{2,1,0:T(8,128)(2,1)} %get-tuple-element.13), calls=%async_computation | async-start | bytes 851968 | tf_op jit(solution)/shard_map/all_to_all | solution.py:224
  9.5 0.5 %collective-permute-start = (f32[3,16,256]{2,1,0:T(8,128)S(1)}, f32[3,16,256]{2,1,0:T(8,128)S(1)}, u32[]{:S(2)}, u32[]{:S(2)}) collective-permute-start(f32[3,16,256]{2,1,0:T(8,128)S(1)} %get-tuple-element.9), channel_id=1, source_target_pairs={{0,4},{4,8},{8,12},{12,16},{16,20},{20,24},{24,28},{28,0},{1,5},{5... | collective-permute-start | bytes 147464 | tf_op jit(solution)/shard_map/ppermute | solution.py:218
  10.0 0.0 copy-start.3
  10.0 2.2 %collective-permute-start.1 = (f32[3,16,256]{2,1,0:T(8,128)S(1)}, f32[3,16,256]{2,1,0:T(8,128)S(1)}, u32[]{:S(2)}, u32[]{:S(2)}) collective-permute-start(f32[3,16,256]{2,1,0:T(8,128)S(1)} %get-tuple-element.10), channel_id=1, source_target_pairs={{0,28},{4,0},{8,4},{12,8},{16,12},{20,16},{24,20},{28,24},{1,29},{... | collective-permute-start | bytes 147464 | tf_op jit(solution)/shard_map/ppermute | solution.py:218
  12.2 1.6 %collective-permute-start.2 = (f32[3,16,256]{2,1,0:T(8,128)S(1)}, f32[3,16,256]{2,1,0:T(8,128)S(1)}, u32[]{:S(2)}, u32[]{:S(2)}) collective-permute-start(f32[3,16,256]{2,1,0:T(8,128)S(1)} %get-tuple-element.11), channel_id=1, source_target_pairs={{0,1},{1,2},{2,3},{3,0},{4,5},{5,6},{6,7},{7,4},{8,9},{9,10},{10,1... | collective-permute-start | bytes 147464 | tf_op jit(solution)/shard_map/ppermute | solution.py:218
  13.8 2.2 %collective-permute-start.3 = (f32[3,16,256]{2,1,0:T(8,128)S(1)}, f32[3,16,256]{2,1,0:T(8,128)S(1)}, u32[]{:S(2)}, u32[]{:S(2)}) collective-permute-start(f32[3,16,256]{2,1,0:T(8,128)S(1)} %get-tuple-element.12), channel_id=1, source_target_pairs={{0,3},{1,0},{2,1},{3,2},{4,7},{5,4},{6,5},{7,6},{8,11},{9,8},{10,9... | collective-permute-start | bytes 147464 | tf_op jit(solution)/shard_map/ppermute | solution.py:218
  16.1 0.0 copy-done.3
  16.1 0.1 copy.7.slots
  16.1 2.6 %collective-permute-done.x_before = f32[3,16,256]{2,1,0:T(8,128)S(1)} collective-permute-done((f32[3,16,256]{2,1,0:T(8,128)S(1)}, f32[3,16,256]{2,1,0:T(8,128)S(1)}, u32[]{:S(2)}, u32[]{:S(2)}) %collective-permute-start) | collective-permute-done | bytes 49184 | tf_op jit(solution)/shard_map/ppermute | solution.py:218
  18.8 0.0 collective-permute-done.1.x_after
  18.8 0.0 collective-permute-done.2.y_before
  18.8 0.0 collective-permute-done.3.y_after
  18.8 0.0 all-to-all-done.chunk
  18.8 0.0 copy-done.1
  18.8 13.4 %main.1 = (f32[768,256]{1,0:T(8,128)}, f32[8,3,192]{2,1,0:T(4,128)S(1)}) custom-call(s32[1,1,8,3]{3,2,1,0:T(8,128)S(1)} %copy.7.slots, f32[768,256]{1,0:T(8,128)S(1)} %bitcast.8, f32[3,16,256]{2,1,0:T(8,128)S(1)} %collective-permute-done.x_before, f32[3,16,256]{2,1,0:T(8,128)S(1)} %collective-permute-done.1.x_after, ...), custom_call_target="tpu_custom_call" | custom-call | tf_op jit(solution)/shard_map/main/pallas_call | solution.py:225
  32.2 7.5 %all_to_all.10 = f32[8,3,192]{2,1,0:T(4,128)S(1)} all-to-all(f32[8,3,192]{2,1,0:T(4,128)S(1)} %get-tuple-element.15), channel_id=1, replica_groups=mesh['gx'=8,'gy'=4] {'gx'}, dimensions={0} | all-to-all | bytes 36864 | tf_op jit(solution)/shard_map/all_to_all | solution.py:246
  39.7 0.6 %copy.8 = f32[1,1,8,3,192]{4,2,3,1,0:T(8,128)} copy(f32[1,1,8,3,192]{4,3,2,1,0:T(4,128)S(1)} %bitcast.11) | data formatting | bytes 36864
Async XLA Ops:
  1.3 1.1 %copy-start = (f32[3,16,16,256]{3,2,1,0:T(8,128)S(1)}, f32[3,16,16,256]{3,2,1,0:T(8,128)}, u32[]{:S(2)}) copy-start(f32[3,16,16,256]{3,2,1,0:T(8,128)} %param.5) | copy-start | bytes 2359300
  2.5 1.0 %copy-start.2 = (bf16[1,1,8,3,64,128]{5,4,3,2,1,0:T(8,128)(2,1)S(1)}, bf16[1,1,8,3,64,128]{5,4,3,2,1,0:T(8,128)(2,1)}, u32[]{:S(2)}) copy-start(bf16[1,1,8,3,64,128]{5,4,3,2,1,0:T(8,128)(2,1)} %param.6) | copy-start | bytes 1179652
  3.5 15.3 %copy-start.1 = (f32[3,16,16,256]{3,2,1,0:T(8,128)S(1)}, f32[3,16,16,256]{3,2,1,0:T(8,128)}, u32[]{:S(2)}) copy-start(f32[3,16,16,256]{3,2,1,0:T(8,128)} %param.5) | copy-start | bytes 2359300
  4.3 14.5 %all-to-all-start = ((bf16[8,208,128]{2,1,0:T(8,128)(2,1)}), bf16[8,208,128]{2,1,0:T(8,128)(2,1)S(1)}, u32[]{:S(2)}, u32[]{:S(2)}) async-start(bf16[8,208,128]{2,1,0:T(8,128)(2,1)} %get-tuple-element.13), calls=%async_computation | async-start | bytes 851968 | tf_op jit(solution)/shard_map/all_to_all | solution.py:224
  9.5 9.3 %collective-permute-start = (f32[3,16,256]{2,1,0:T(8,128)S(1)}, f32[3,16,256]{2,1,0:T(8,128)S(1)}, u32[]{:S(2)}, u32[]{:S(2)}) collective-permute-start(f32[3,16,256]{2,1,0:T(8,128)S(1)} %get-tuple-element.9), channel_id=1, source_target_pairs={{0,4},{4,8},{8,12},{12,16},{16,20},{20,24},{24,28},{28,0},{1,5},{5... | collective-permute-start | bytes 147464 | tf_op jit(solution)/shard_map/ppermute | solution.py:218
  10.0 6.1 %copy-start.3 = (s32[1,1,8,3]{2,1,3,0:T(1,128)S(1)}, s32[1,1,8,3]{2,1,3,0:T(1,128)}, u32[]{:S(2)}) copy-start(s32[1,1,8,3]{2,1,3,0:T(1,128)} %param.8) | copy-start | bytes 292
  10.0 8.8 %collective-permute-start.1 = (f32[3,16,256]{2,1,0:T(8,128)S(1)}, f32[3,16,256]{2,1,0:T(8,128)S(1)}, u32[]{:S(2)}, u32[]{:S(2)}) collective-permute-start(f32[3,16,256]{2,1,0:T(8,128)S(1)} %get-tuple-element.10), channel_id=1, source_target_pairs={{0,28},{4,0},{8,4},{12,8},{16,12},{20,16},{24,20},{28,24},{1,29},{... | collective-permute-start | bytes 147464 | tf_op jit(solution)/shard_map/ppermute | solution.py:218
  12.2 6.5 %collective-permute-start.2 = (f32[3,16,256]{2,1,0:T(8,128)S(1)}, f32[3,16,256]{2,1,0:T(8,128)S(1)}, u32[]{:S(2)}, u32[]{:S(2)}) collective-permute-start(f32[3,16,256]{2,1,0:T(8,128)S(1)} %get-tuple-element.11), channel_id=1, source_target_pairs={{0,1},{1,2},{2,3},{3,0},{4,5},{5,6},{6,7},{7,4},{8,9},{9,10},{10,1... | collective-permute-start | bytes 147464 | tf_op jit(solution)/shard_map/ppermute | solution.py:218
  13.8 5.0 %collective-permute-start.3 = (f32[3,16,256]{2,1,0:T(8,128)S(1)}, f32[3,16,256]{2,1,0:T(8,128)S(1)}, u32[]{:S(2)}, u32[]{:S(2)}) collective-permute-start(f32[3,16,256]{2,1,0:T(8,128)S(1)} %get-tuple-element.12), channel_id=1, source_target_pairs={{0,3},{1,0},{2,1},{3,2},{4,7},{5,4},{6,5},{7,6},{8,11},{9,8},{10,9... | collective-permute-start | bytes 147464 | tf_op jit(solution)/shard_map/ppermute | solution.py:218

commit v2 on v1

v2 whole, which is shorter than its diff:
```python
import functools

import jax
import jax.numpy as jnp
from jax import lax
from jax.experimental import pallas as pl
from jax.experimental.pallas import tpu as pltpu
from jax.sharding import PartitionSpec as P

time_step = 0.05
viscosity = 0.5
spread_gain = 0.5

VMEM = pltpu.VMEM
F32 = jnp.float32
BF16 = jnp.bfloat16


def each(count, body, flat=False):
    if flat or count == 1:
        for i in range(count):
            body(i)
    else:

        def step(i, carry):
            body(i)
            return carry

        lax.fori_loop(0, count, step, 0)


def pack_kernel(dims, vel, w, t, chunk, x_first, x_last, y_first, y_last, held, rows, sems):
    size_x, size_y, count_d, width = dims
    halves = held.shape[0]
    moves = [
        pltpu.make_async_copy(vel.at[:, pl.ds(part * 128, 128)], held.at[part], sems.at[1 + part])
        for part in range(halves)
    ]
    for move in moves:
        move.start()
    move_w = pltpu.make_async_copy(w, chunk.at[:, pl.ds(0, width), :], sems.at[0])
    move_w.start()
    rows[...] = jnp.zeros_like(rows)
    rest = jnp.zeros((count_d, 256 - width), F32)
    for c in range(3):
        values = t[c].astype(F32)
        rows[pl.ds(c, count_d, stride=16), :] = values[:, 0:128]
        rows[pl.ds(8 + c, count_d, stride=16), :] = jnp.concatenate([values[:, 128:width], rest], axis=1)
    chunk[:, width : width + 16, :] = rows[...].astype(BF16).reshape(count_d, 16, 128)
    plane = size_x * size_y
    for part in range(halves):
        moves[part].wait()
        lanes = pl.ds(part * 128, 128)
        for c in range(3):
            x_first[c, :, lanes] = held[part, pl.ds(c * plane, size_y), :]
            x_last[c, :, lanes] = held[part, pl.ds(c * plane + plane - size_y, size_y), :]
            y_first[c, :, lanes] = held[part, pl.ds(c * plane, size_x, stride=size_y), :]
            y_last[c, :, lanes] = held[part, pl.ds(c * plane + size_y - 1, size_x, stride=size_y), :]
    move_w.wait()


def split(x, size):
    if size & (size - 1) == 0:
        return lax.shift_right_logical(x, size.bit_length() - 1), x & (size - 1)
    return lax.div(x, size), lax.rem(x, size)


def main_kernel(
    dims, slots, vel, x_before, x_after, y_before, y_after, blocks, out, force_out,
    field, stage, chosen,
):
    size_x, size_y, size_z, count_d, count_s, width = dims
    columns_y = size_y // 4
    layers_z = size_z // 8
    markers = width // count_s
    cells = 3 * size_x * size_y
    halves = size_z // 128

    row = lax.broadcasted_iota(jnp.int32, (size_y, size_z), 0)
    col = lax.broadcasted_iota(jnp.int32, (size_y, size_z), 1)

    def stencil(x):
        center, fore, back, right, left, top, bottom = [], [], [], [], [], [], []
        for c in range(3):
            base = (c * size_x + x) * size_y
            here = vel[pl.ds(base, size_y), :]
            center.append(here)
            fore.append(x_after[c] if x == size_x - 1 else vel[pl.ds(base + size_y, size_y), :])
            back.append(x_before[c] if x == 0 else vel[pl.ds(base - size_y, size_y), :])
            right.append(
                jnp.where(row == size_y - 1, y_after[c, pl.ds(x, 1), :], pltpu.roll(here, size_y - 1, 0))
            )
            left.append(jnp.where(row == 0, y_before[c, pl.ds(x, 1), :], pltpu.roll(here, 1, 0)))
            top.append(jnp.where(col == size_z - 1, 0.0, pltpu.roll(here, size_z - 1, 1)))
            bottom.append(jnp.where(col == 0, 0.0, pltpu.roll(here, 1, 1)))
        for c in range(3):
            laplace = fore[c] + back[c] + right[c] + left[c] + top[c] + bottom[c] - 6.0 * center[c]
            advect = (
                center[0] * (fore[c] - back[c]) * 0.5
                + center[1] * (right[c] - left[c]) * 0.5
                + center[2] * (top[c] - bottom[c]) * 0.5
            )
            base = 8 + (c * size_x + x) * size_y
            result = center[c] + time_step * (viscosity * laplace - advect)
            for part in range(halves):
                field[part, pl.ds(base, size_y), :] = result[:, part * 128 : part * 128 + 128]

    each(size_x, stencil, True)

    lane = lax.broadcasted_iota(jnp.int32, (8, 128), 1)
    sub = lax.broadcasted_iota(jnp.int32, (8, 128), 0)
    low_lane = lane < 64
    low_sub = sub < 4
    group = 8 if count_d % 8 == 0 else 1
    lines = group * count_s * 8

    def shifts(rows, columns, piece_axis):
        shape = (rows, columns)
        piece = lax.broadcasted_iota(jnp.int32, shape, piece_axis)
        place = lax.broadcasted_iota(jnp.int32, shape, 1 - piece_axis) & 127
        m = piece & 127
        hit = ((m & 63) < 8) & (place == m + 8 * lax.shift_right_logical(piece, 7))
        return jnp.where(hit, 1.0, 0.0).astype(BF16)

    def place(i, s):
        safe = jnp.maximum(slots[s, 0, i], 0)
        rest, qz = split(safe, layers_z)
        qx, qy = split(rest, columns_y)
        half, layer = split(qz, 16)
        first = 8 + qx * (4 * size_y) + qy * 4
        return half, first, 8 * layer

    def windows(half, first, c):
        return [
            (half, pl.ds(first + ((c * size_x + ax) * size_y - 4 * (ax % 2)), 8)) for ax in range(4)
        ]

    def gather(i, g):
        for s in range(count_s):
            half, first, shift = place(i, s)
            for c in range(3):
                w = [field[k, at, :] for k, at in windows(half, first, c)]
                near = pltpu.roll(jnp.where(low_sub, w[0], w[1]), (128 - shift) & 127, 1)
                far = pltpu.roll(jnp.where(low_sub, w[2], w[3]), (192 - shift) & 127, 1)
                stage[pl.ds(((g * count_s + s) * 8 + c) * 8, 8), :] = jnp.where(low_lane, near, far)

    slot_of = lax.broadcasted_iota(jnp.int32, (8, width), 1) // markers

    def force_and_spread(i, g):
        block_w = blocks[i, 0:width, :]
        tail = blocks[i, width : width + 16, :].astype(F32)
        target = jnp.concatenate([tail[0:8, :], tail[8:16, 0 : width - 128]], axis=1)
        mine = pl.ds(pl.multiple_of(i * (count_s * 8), 8), count_s * 8)
        product = lax.dot_general(
            chosen[mine, :].astype(BF16), block_w, (((1,), (1,)), ((), ())), preferred_element_type=F32
        )
        interp = product[0:8]
        live = jnp.full((8, width), slots[0, 0, i], jnp.int32)
        for s in range(1, count_s):
            interp = jnp.where(slot_of == s, product[8 * s : 8 * s + 8], interp)
            live = jnp.where(slot_of == s, slots[s, 0, i], live)
        force = jnp.where(live >= 0, (target - interp) / time_step, 0.0)
        force_out[i] = force[0:3, :]
        rows = jnp.concatenate([jnp.where(slot_of == s, force, 0.0) for s in range(count_s)], axis=0)
        chosen[mine, :] = jnp.dot(rows.astype(BF16), block_w, preferred_element_type=F32)

    def scatter(i, g):
        for s in range(count_s):
            half, first, shift = place(i, s)
            for c in range(3):
                both = stage[pl.ds(((g * count_s + s) * 8 + c) * 8, 8), :]
                near = pltpu.roll(jnp.where(low_lane, both, 0.0), shift, 1)
                far = pltpu.roll(jnp.where(low_lane, 0.0, both), (shift + 64) & 127, 1)
                spots = windows(half, first, c)
                pieces = [near, near, far, far]
                sums = [
                    field[k, at, :] + jnp.where(low_sub, *((pieces[ax], 0.0) if ax % 2 == 0 else (0.0, pieces[ax])))
                    for ax, (k, at) in enumerate(spots)
                ]
                for (k, at), total in zip(spots, sums):
                    field[k, at, :] = total

    def first_pass(k):
        for g in range(group):
            gather(k * group + g, g)
        picked = jnp.concatenate([stage[pl.ds(r, lines, stride=8), :] for r in range(8)], axis=1)
        picked = jnp.dot(picked.astype(BF16), shifts(1024, 128, 0), preferred_element_type=F32)
        chosen[pl.ds(pl.multiple_of(k * lines, 8), lines), :] = picked
        for g in range(group):
            force_and_spread(k * group + g, g)

    def second_pass(k):
        rows = chosen[pl.ds(pl.multiple_of(k * lines, 8), lines), :] * (time_step * spread_gain)
        high = rows.astype(BF16)
        pair = jnp.concatenate([high, (rows - high.astype(F32)).astype(BF16)], axis=1)
        pieces = jnp.dot(pair, shifts(256, 1024, 1), preferred_element_type=F32)
        for r in range(8):
            stage[pl.ds(r, lines, stride=8), :] = pieces[:, r * 128 : r * 128 + 128]
        for g in range(group):
            scatter(k * group + g, g)

    each(count_d // group, first_pass)
    each(count_d // group, second_pass)
    for part in range(halves):
        out[:, part * 128 : part * 128 + 128] = field[part, pl.ds(8, cells), :]


def run_main(dims, *operands):
    size_x, size_y, size_z, count_d, count_s, width = dims
    cells = 3 * size_x * size_y
    group = 8 if count_d % 8 == 0 else 1
    inside = pl.BlockSpec(memory_space=VMEM)
    return pl.pallas_call(
        functools.partial(main_kernel, dims),
        out_shape=(
            jax.ShapeDtypeStruct((cells, size_z), F32),
            jax.ShapeDtypeStruct((count_d, 3, width), F32),
        ),
        in_specs=[pl.BlockSpec(memory_space=pltpu.SMEM)] + [inside] * 6,
        out_specs=(inside, inside),
        scratch_shapes=[
            VMEM((size_z // 128, cells + 16, 128), F32),
            VMEM((group * count_s * 64, 128), F32),
            VMEM((count_d * count_s * 8, 128), F32),
        ],
        compiler_params=pltpu.CompilerParams(vmem_limit_bytes=24 * 2**20),
        name="main",
    )(*operands)


def shards(velocity, weights, targets, owner_list, slot_patch):
    size_x, size_y, size_z = velocity.shape[1:]
    count_d, count_s, markers = weights.shape[2:5]
    width = count_s * markers
    cells = 3 * size_x * size_y
    vel = velocity.reshape(cells, size_z)
    block_w = weights.reshape(count_d, width, 128)
    anywhere = pl.BlockSpec(memory_space=pl.ANY)
    inside = pl.BlockSpec(memory_space=VMEM)
    face_x = jax.ShapeDtypeStruct((3, size_y, size_z), F32)
    face_y = jax.ShapeDtypeStruct((3, size_x, size_z), F32)
    chunk, x_first, x_last, y_first, y_last = pl.pallas_call(
        functools.partial(pack_kernel, (size_x, size_y, count_d, width)),
        out_shape=(
            jax.ShapeDtypeStruct((count_d, width + 16, 128), BF16),
            face_x, face_x, face_y, face_y,
        ),
        in_specs=[anywhere, anywhere, inside],
        out_specs=(inside,) * 5,
        scratch_shapes=[
            VMEM((size_z // 128, cells, 128), F32),
            VMEM((count_d * 16, 128), F32),
            pltpu.SemaphoreType.DMA((1 + size_z // 128,)),
        ],
        compiler_params=pltpu.CompilerParams(vmem_limit_bytes=56 * 2**20),
        name="pack",
    )(vel, block_w, jnp.transpose(targets[0, 0], (1, 0, 2)))

    def ring(x, axis, step):
        size = lax.axis_size(axis)
        return lax.ppermute(x, axis, [(i, (i + step) % size) for i in range(size)])

    y_before = ring(y_last, "gy", 1)
    y_after = ring(y_first, "gy", -1)
    x_before = ring(x_last, "gx", 1)
    x_after = ring(x_first, "gx", -1)
    arrived = lax.all_to_all(chunk, "gx", split_axis=0, concat_axis=0, tiled=True)
    slots = jnp.transpose(slot_patch[0, 0]).reshape(count_s, 1, count_d)
    dims = (size_x, size_y, size_z, count_d, count_s, width)
    out, force = run_main(dims, slots, vel, x_before, x_after, y_before, y_after, arrived)
    returned = lax.all_to_all(force, "gx", split_axis=0, concat_axis=0, tiled=True)
    return out.reshape(velocity.shape), returned[None, None]


def solution(mesh):
    return jax.shard_map(
        shards,
        mesh=mesh,
        in_specs=(
            P(None, "gx", "gy", None),
            P("gx", "gy", None, None, None, None),
            P("gx", "gy", None, None, None),
            P("gx", "gy", None, None),
            P("gx", "gy", None, None),
        ),
        out_specs=(P(None, "gx", "gy", None), P("gx", "gy", None, None, None)),
        check_vma=False,
    )
```

time: 40.7 us -> 31 us (0.76)
  Pallas kernels: 14.2 us -> 7.24 us
  local copies, waits for them, and re-layouts: 3.54 us -> 0.65 us
    pallas_call x1, Pallas kernels: 13.4 us -> 4.41 us  [run_main(): pl.pallas_call(functools.partial(main_kernel, dims), out_shape=(jax.Shape...]
    unnamed x11 -> x14, local copies, waits for them, and re-layouts: 3.54 us -> 0.64 us
    pallas_call x1, Pallas kernels: 0.83 us -> 2.83 us  [shards(): pl.pallas_call(functools.partial(pack_kernel, (size_x, size_y, count_d, w...]
where the time goes in v2:
time: 31 us; the launch traced here: 30.6 us
  starting transfers between devices  11.9 us (38%)
  blocking collectives  7.48 us (24%)
  Pallas kernels  7.24 us (23%)
  waiting for transfers between devices  2.68 us (9%)
  between operations  0.71 us (2%)
  local copies, waits for them, and re-layouts  0.65 us (2%)
    all_to_all x1, blocking collectives, shards(): lax.all_to_all(force, 'gx', split_axis=0, concat_axis=0, tiled=True)  7.48 us
    ppermute x4, starting transfers between devices, ring(): return lax.ppermute(x, axis, [(i, (i + step) % size) for i in range(size)])  6.57 us
    all_to_all x1, starting transfers between devices, shards(): lax.all_to_all(chunk, 'gx', split_axis=0, concat_axis=0, tiled=True)  5.31 us
    pallas_call x1, Pallas kernels, run_main(): pl.pallas_call(functools.partial(main_kernel, dims), out_shape=(jax.Shape...  4.41 us
    pallas_call x1, Pallas kernels, shards(): pl.pallas_call(functools.partial(pack_kernel, (size_x, size_y, count_d, w...  2.83 us
    ppermute x4, waiting for transfers between devices, ring(): return lax.ppermute(x, axis, [(i, (i + step) % size) for i in range(size)])  2.67 us
    unnamed x14, local copies, waits for them, and re-layouts  0.64 us
  transfers between devices with their start and end apart: 5, of which 1 were waited for; matrix products, arithmetic and copies ran while one was open for 0% of the time, Pallas kernels for 0%

profile of v2, /device:TPU:0, one launch (start us, length us, event | category | flops | bytes accessed | tf_op | source)
XLA Modules:
  0.0 30.6 jit_solution(15939130877176050347)
XLA Ops:
  0.6 0.0 copy-start
  0.6 2.8 %pack.1 = (bf16[8,208,128]{2,1,0:T(8,128)(2,1)}, f32[3,16,256]{2,1,0:T(8,128)}, f32[3,16,256]{2,1,0:T(8,128)}, f32[3,16,256]{2,1,0:T(8,128)}, f32[3,16,256]{2,1,0:T(8,128)}) custom-call(f32[768,256]{1,0:T(8,128)} %bitcast.14, bf16[8,192,128]{2,1,0:T(8,128)(2,1)} %bitcast.16, bf16[3,8,192]{2,1,0:T(8,128)(2,1)} %bitcast.18), custom_call_target="tpu_custom_call" | custom-call | tf_op jit(solution)/shard_map/pack/pallas_call | solution.py:242
  3.5 0.0 copy-start.5
  3.5 0.0 copy-start.4
  3.5 0.0 copy-start.3
  3.5 0.0 copy-start.2
  3.5 5.3 %all-to-all-start = ((bf16[8,208,128]{2,1,0:T(8,128)(2,1)}), bf16[8,208,128]{2,1,0:T(8,128)(2,1)S(1)}, u32[]{:S(2)}, u32[]{:S(2)}) async-start(bf16[8,208,128]{2,1,0:T(8,128)(2,1)} %get-tuple-element.13), calls=%async_computation | async-start | bytes 851968 | tf_op jit(solution)/shard_map/all_to_all | solution.py:267
  8.8 0.0 copy-done.5
  8.8 0.5 %collective-permute-start = (f32[3,16,256]{2,1,0:T(8,128)S(1)}, f32[3,16,256]{2,1,0:T(8,128)S(1)}, u32[]{:S(2)}, u32[]{:S(2)}) collective-permute-start(f32[3,16,256]{2,1,0:T(8,128)S(1)} %copy-done.5), channel_id=1, source_target_pairs={{0,4},{4,8},{8,12},{12,16},{16,20},{20,24},{24,28},{28,0},{1,5},{5... | collective-permute-start | bytes 147464 | tf_op jit(solution)/shard_map/ppermute | solution.py:261
  9.3 0.0 copy-done.4
  9.3 0.0 copy-start.1
  9.3 2.2 %collective-permute-start.1 = (f32[3,16,256]{2,1,0:T(8,128)S(1)}, f32[3,16,256]{2,1,0:T(8,128)S(1)}, u32[]{:S(2)}, u32[]{:S(2)}) collective-permute-start(f32[3,16,256]{2,1,0:T(8,128)S(1)} %copy-done.4), channel_id=1, source_target_pairs={{0,28},{4,0},{8,4},{12,8},{16,12},{20,16},{24,20},{28,24},{1,29},{... | collective-permute-start | bytes 147464 | tf_op jit(solution)/shard_map/ppermute | solution.py:261
  11.6 0.0 copy-done.3
  11.6 1.6 %collective-permute-start.2 = (f32[3,16,256]{2,1,0:T(8,128)S(1)}, f32[3,16,256]{2,1,0:T(8,128)S(1)}, u32[]{:S(2)}, u32[]{:S(2)}) collective-permute-start(f32[3,16,256]{2,1,0:T(8,128)S(1)} %copy-done.3), channel_id=1, source_target_pairs={{0,1},{1,2},{2,3},{3,0},{4,5},{5,6},{6,7},{7,4},{8,9},{9,10},{10,1... | collective-permute-start | bytes 147464 | tf_op jit(solution)/shard_map/ppermute | solution.py:261
  13.2 0.0 copy-done.2
  13.2 2.2 %collective-permute-start.3 = (f32[3,16,256]{2,1,0:T(8,128)S(1)}, f32[3,16,256]{2,1,0:T(8,128)S(1)}, u32[]{:S(2)}, u32[]{:S(2)}) collective-permute-start(f32[3,16,256]{2,1,0:T(8,128)S(1)} %copy-done.2), channel_id=1, source_target_pairs={{0,3},{1,0},{2,1},{3,2},{4,7},{5,4},{6,5},{7,6},{8,11},{9,8},{10,9... | collective-permute-start | bytes 147464 | tf_op jit(solution)/shard_map/ppermute | solution.py:261
  15.4 0.0 copy-done.1
  15.4 2.7 %collective-permute-done.x_before = f32[3,16,256]{2,1,0:T(8,128)S(1)} collective-permute-done((f32[3,16,256]{2,1,0:T(8,128)S(1)}, f32[3,16,256]{2,1,0:T(8,128)S(1)}, u32[]{:S(2)}, u32[]{:S(2)}) %collective-permute-start) | collective-permute-done | bytes 49184 | tf_op jit(solution)/shard_map/ppermute | solution.py:261
  18.1 0.0 collective-permute-done.1.x_after
  18.1 0.0 collective-permute-done.2.y_before
  18.1 0.0 collective-permute-done.3.y_after
  18.1 0.0 all-to-all-done.blocks
  18.1 0.0 copy-done
  18.1 4.4 %main.1 = (f32[768,256]{1,0:T(8,128)}, f32[8,3,192]{2,1,0:T(4,128)S(1)}) custom-call(s32[3,1,8]{2,1,0:T(1,128)S(1)} %copy.6.slots, f32[768,256]{1,0:T(8,128)S(1)} %bitcast.15, f32[3,16,256]{2,1,0:T(8,128)S(1)} %collective-permute-done.x_before, f32[3,16,256]{2,1,0:T(8,128)S(1)} %collective-permute-done.1.x_after, ...), custom_call_target="tpu_custom_call" | custom-call | tf_op jit(solution)/shard_map/main/pallas_call | solution.py:213
  22.5 7.5 %all_to_all.10 = f32[8,3,192]{2,1,0:T(4,128)S(1)} all-to-all(f32[8,3,192]{2,1,0:T(4,128)S(1)} %get-tuple-element.15), channel_id=1, replica_groups=mesh['gx'=8,'gy'=4] {'gx'}, dimensions={0} | all-to-all | bytes 36864 | tf_op jit(solution)/shard_map/all_to_all | solution.py:271
  30.0 0.6 %copy.7 = f32[1,1,8,3,192]{4,2,3,1,0:T(8,128)} copy(f32[1,1,8,3,192]{4,3,2,1,0:T(4,128)S(1)} %bitcast.17) | data formatting | bytes 36864
  (2 shorter events, 0.0 us)
Async XLA Ops:
  0.6 17.5 %copy-start = (f32[3,16,16,256]{3,2,1,0:T(8,128)S(1)}, f32[3,16,16,256]{3,2,1,0:T(8,128)}, u32[]{:S(2)}) copy-start(f32[3,16,16,256]{3,2,1,0:T(8,128)} %param.5) | copy-start | bytes 2359300
  3.5 5.4 %copy-start.5 = (f32[3,16,256]{2,1,0:T(8,128)S(1)}, f32[3,16,256]{2,1,0:T(8,128)}, u32[]{:S(2)}) copy-start(f32[3,16,256]{2,1,0:T(8,128)} %get-tuple-element.9) | copy-start | bytes 147460
  3.5 5.9 %copy-start.4 = (f32[3,16,256]{2,1,0:T(8,128)S(1)}, f32[3,16,256]{2,1,0:T(8,128)}, u32[]{:S(2)}) copy-start(f32[3,16,256]{2,1,0:T(8,128)} %get-tuple-element.10) | copy-start | bytes 147460
  3.5 8.1 %copy-start.3 = (f32[3,16,256]{2,1,0:T(8,128)S(1)}, f32[3,16,256]{2,1,0:T(8,128)}, u32[]{:S(2)}) copy-start(f32[3,16,256]{2,1,0:T(8,128)} %get-tuple-element.11) | copy-start | bytes 147460
  3.5 9.7 %copy-start.2 = (f32[3,16,256]{2,1,0:T(8,128)S(1)}, f32[3,16,256]{2,1,0:T(8,128)}, u32[]{:S(2)}) copy-start(f32[3,16,256]{2,1,0:T(8,128)} %get-tuple-element.12) | copy-start | bytes 147460
  3.5 14.6 %all-to-all-start = ((bf16[8,208,128]{2,1,0:T(8,128)(2,1)}), bf16[8,208,128]{2,1,0:T(8,128)(2,1)S(1)}, u32[]{:S(2)}, u32[]{:S(2)}) async-start(bf16[8,208,128]{2,1,0:T(8,128)(2,1)} %get-tuple-element.13), calls=%async_computation | async-start | bytes 851968 | tf_op jit(solution)/shard_map/all_to_all | solution.py:267
  8.8 9.3 %collective-permute-start = (f32[3,16,256]{2,1,0:T(8,128)S(1)}, f32[3,16,256]{2,1,0:T(8,128)S(1)}, u32[]{:S(2)}, u32[]{:S(2)}) collective-permute-start(f32[3,16,256]{2,1,0:T(8,128)S(1)} %copy-done.5), channel_id=1, source_target_pairs={{0,4},{4,8},{8,12},{12,16},{16,20},{20,24},{24,28},{28,0},{1,5},{5... | collective-permute-start | bytes 147464 | tf_op jit(solution)/shard_map/ppermute | solution.py:261
  9.3 6.1 %copy-start.1 = (s32[1,1,8,3]{2,1,3,0:T(1,128)S(1)}, s32[1,1,8,3]{2,1,3,0:T(1,128)}, u32[]{:S(2)}) copy-start(s32[1,1,8,3]{2,1,3,0:T(1,128)} %param.8) | copy-start | bytes 292
  9.3 8.8 %collective-permute-start.1 = (f32[3,16,256]{2,1,0:T(8,128)S(1)}, f32[3,16,256]{2,1,0:T(8,128)S(1)}, u32[]{:S(2)}, u32[]{:S(2)}) collective-permute-start(f32[3,16,256]{2,1,0:T(8,128)S(1)} %copy-done.4), channel_id=1, source_target_pairs={{0,28},{4,0},{8,4},{12,8},{16,12},{20,16},{24,20},{28,24},{1,29},{... | collective-permute-start | bytes 147464 | tf_op jit(solution)/shard_map/ppermute | solution.py:261
  11.6 6.5 %collective-permute-start.2 = (f32[3,16,256]{2,1,0:T(8,128)S(1)}, f32[3,16,256]{2,1,0:T(8,128)S(1)}, u32[]{:S(2)}, u32[]{:S(2)}) collective-permute-start(f32[3,16,256]{2,1,0:T(8,128)S(1)} %copy-done.3), channel_id=1, source_target_pairs={{0,1},{1,2},{2,3},{3,0},{4,5},{5,6},{6,7},{7,4},{8,9},{9,10},{10,1... | collective-permute-start | bytes 147464 | tf_op jit(solution)/shard_map/ppermute | solution.py:261
  13.2 4.9 %collective-permute-start.3 = (f32[3,16,256]{2,1,0:T(8,128)S(1)}, f32[3,16,256]{2,1,0:T(8,128)S(1)}, u32[]{:S(2)}, u32[]{:S(2)}) collective-permute-start(f32[3,16,256]{2,1,0:T(8,128)S(1)} %copy-done.2), channel_id=1, source_target_pairs={{0,3},{1,0},{2,1},{3,2},{4,7},{5,4},{6,5},{7,6},{8,11},{9,8},{10,9... | collective-permute-start | bytes 147464 | tf_op jit(solution)/shard_map/ppermute | solution.py:261

commit v3 on v2

v3 whole, which is shorter than its diff:
```python
import functools

import jax
import jax.numpy as jnp
from jax import lax
from jax.experimental import pallas as pl
from jax.experimental.pallas import tpu as pltpu
from jax.sharding import PartitionSpec as P

time_step = 0.05
viscosity = 0.5
spread_gain = 0.5

VMEM = pltpu.VMEM
F32 = jnp.float32
BF16 = jnp.bfloat16


def each(count, body, flat=False):
    if flat or count == 1:
        for i in range(count):
            body(i)
    else:

        def step(i, carry):
            body(i)
            return carry

        lax.fori_loop(0, count, step, 0)


def faces_kernel(dims, vel, x_first, x_last, y_first, y_last, held, sems):
    size_x, size_y = dims
    halves = held.shape[0]
    moves = [
        pltpu.make_async_copy(vel.at[:, pl.ds(part * 128, 128)], held.at[part], sems.at[part])
        for part in range(halves)
    ]
    for move in moves:
        move.start()
    plane = size_x * size_y
    for part in range(halves):
        moves[part].wait()
        lanes = pl.ds(part * 128, 128)
        for c in range(3):
            x_first[c, :, lanes] = held[part, pl.ds(c * plane, size_y), :]
            x_last[c, :, lanes] = held[part, pl.ds(c * plane + plane - size_y, size_y), :]
            y_first[c, :, lanes] = held[part, pl.ds(c * plane, size_x, stride=size_y), :]
            y_last[c, :, lanes] = held[part, pl.ds(c * plane + size_y - 1, size_x, stride=size_y), :]


def pack_kernel(dims, w, t, slots, own, chunk, slots_out, own_out, rows, sem):
    slots_out[...] = slots[...]
    own_out[...] = own[...]
    count_d, width = dims
    move_w = pltpu.make_async_copy(w, chunk.at[:, pl.ds(0, width), :], sem)
    move_w.start()
    rows[...] = jnp.zeros_like(rows)
    rest = jnp.zeros((count_d, 256 - width), F32)
    for c in range(3):
        values = t[c].astype(F32)
        rows[pl.ds(c, count_d, stride=16), :] = values[:, 0:128]
        rows[pl.ds(8 + c, count_d, stride=16), :] = jnp.concatenate([values[:, 128:width], rest], axis=1)
    chunk[:, width : width + 16, :] = rows[...].astype(BF16).reshape(count_d, 16, 128)
    move_w.wait()


def split(x, size):
    if size & (size - 1) == 0:
        return lax.shift_right_logical(x, size.bit_length() - 1), x & (size - 1)
    return lax.div(x, size), lax.rem(x, size)


def shifts(rows, columns, piece_axis):
    shape = (rows, columns)
    piece = lax.broadcasted_iota(jnp.int32, shape, piece_axis)
    place = lax.broadcasted_iota(jnp.int32, shape, 1 - piece_axis) & 127
    m = piece & 127
    hit = ((m & 63) < 8) & (place == m + 8 * lax.shift_right_logical(piece, 7))
    return jnp.where(hit, 1.0, 0.0).astype(BF16)


def locate(dims, slots, i, s):
    size_x, size_y, size_z = dims[:3]
    safe = jnp.maximum(slots[0, s, 0, i], 0)
    rest, qz = split(safe, size_z // 8)
    qx, qy = split(rest, size_y // 4)
    half, layer = split(qz, 16)
    first = 8 + qx * (4 * size_y) + qy * 4
    return half, first, 8 * layer


def windows(dims, half, first, c):
    size_x, size_y = dims[:2]
    return [(half, pl.ds(first + ((c * size_x + ax) * size_y - 4 * (ax % 2)), 8)) for ax in range(4)]


def low_halves():
    lane = lax.broadcasted_iota(jnp.int32, (8, 128), 1)
    sub = lax.broadcasted_iota(jnp.int32, (8, 128), 0)
    return lane < 64, sub < 4


def select_slots(product, slot_of, count_s):
    interp = product[0:8]
    for s in range(1, count_s):
        interp = jnp.where(slot_of == s, product[8 * s : 8 * s + 8], interp)
    return interp


def predict_kernel(
    dims, slots, me_ref, vel, x_before, x_after, y_before, y_after, field, keep, give, stage,
):
    size_x, size_y, size_z, count_d, count_s, width = dims
    halves = size_z // 128
    me = me_ref[0]

    row = lax.broadcasted_iota(jnp.int32, (size_y, size_z), 0)
    col = lax.broadcasted_iota(jnp.int32, (size_y, size_z), 1)

    def stencil(x):
        center, fore, back, right, left, top, bottom = [], [], [], [], [], [], []
        for c in range(3):
            base = (c * size_x + x) * size_y
            here = vel[pl.ds(base, size_y), :]
            center.append(here)
            fore.append(x_after[c] if x == size_x - 1 else vel[pl.ds(base + size_y, size_y), :])
            back.append(x_before[c] if x == 0 else vel[pl.ds(base - size_y, size_y), :])
            right.append(
                jnp.where(row == size_y - 1, y_after[c, pl.ds(x, 1), :], pltpu.roll(here, size_y - 1, 0))
            )
            left.append(jnp.where(row == 0, y_before[c, pl.ds(x, 1), :], pltpu.roll(here, 1, 0)))
            top.append(jnp.where(col == size_z - 1, 0.0, pltpu.roll(here, size_z - 1, 1)))
            bottom.append(jnp.where(col == 0, 0.0, pltpu.roll(here, 1, 1)))
        for c in range(3):
            laplace = fore[c] + back[c] + right[c] + left[c] + top[c] + bottom[c] - 6.0 * center[c]
            advect = (
                center[0] * (fore[c] - back[c]) * 0.5
                + center[1] * (right[c] - left[c]) * 0.5
                + center[2] * (top[c] - bottom[c]) * 0.5
            )
            base = 8 + (c * size_x + x) * size_y
            result = center[c] + time_step * (viscosity * laplace - advect)
            for part in range(halves):
                field[part, pl.ds(base, size_y), :] = result[:, part * 128 : part * 128 + 128]

    each(size_x, stencil, True)

    low_lane, low_sub = low_halves()
    group = 8 if count_d % 8 == 0 else count_d
    lines = group * count_s * 8
    tail = jnp.zeros((keep.shape[1] - count_s * 8, 128), F32)

    def gather(i, g):
        for s in range(count_s):
            half, first, shift = locate(dims, slots, i, s)
            for c in range(3):
                w = [field[k, at, :] for k, at in windows(dims, half, first, c)]
                near = pltpu.roll(jnp.where(low_sub, w[0], w[1]), (128 - shift) & 127, 1)
                far = pltpu.roll(jnp.where(low_sub, w[2], w[3]), (192 - shift) & 127, 1)
                stage[pl.ds(((g * count_s + s) * 8 + c) * 8, 8), :] = jnp.where(low_lane, near, far)

    def batch(k):
        for g in range(group):
            gather(me ^ (k * group + g), g)
        picked = jnp.concatenate([stage[pl.ds(r, lines, stride=8), :] for r in range(8)], axis=1)
        picked = jnp.dot(picked.astype(BF16), shifts(1024, 128, 0), preferred_element_type=F32)
        for g in range(group):
            mine = picked[g * count_s * 8 : (g + 1) * count_s * 8]
            block = jnp.concatenate([mine, tail], axis=0).astype(BF16)
            (give if g % 2 else keep)[k * (group // 2) + g // 2] = block

    each(count_d // group, batch)


def spread_kernel(dims, slots, me_ref, before, keep, give, blocks, out, token, field, stage, chosen):
    size_x, size_y, size_z, count_d, count_s, width = dims
    cells = 3 * size_x * size_y
    halves = size_z // 128
    me = me_ref[0]
    low_lane, low_sub = low_halves()
    group = 8 if count_d % 8 == 0 else count_d
    lines = group * count_s * 8
    slot_of = lax.broadcasted_iota(jnp.int32, (8, width), 1) // (width // count_s)
    field[...] = before[...]
    token[...] = jnp.zeros_like(token)

    def force(i, g, block):
        block_w = blocks[i, 0:width, :]
        tail = blocks[i, width : width + 16, :].astype(F32)
        target = jnp.concatenate([tail[0:8, :], tail[8:16, 0 : width - 128]], axis=1)
        product = lax.dot_general(
            block, block_w, (((1,), (1,)), ((), ())), preferred_element_type=F32
        )
        interp = select_slots(product, slot_of, count_s)
        live = jnp.full((8, width), slots[0, 0, 0, i], jnp.int32)
        for s in range(1, count_s):
            live = jnp.where(slot_of == s, slots[0, s, 0, i], live)
        value = jnp.where(live >= 0, (target - interp) / time_step, 0.0)
        rows = jnp.concatenate([jnp.where(slot_of == s, value, 0.0) for s in range(count_s)], axis=0)
        chosen[pl.ds(g * count_s * 8, count_s * 8), :] = jnp.dot(
            rows.astype(BF16), block_w, preferred_element_type=F32
        )

    def scatter(i, g):
        for s in range(count_s):
            half, first, shift = locate(dims, slots, i, s)
            for c in range(3):
                both = stage[pl.ds(((g * count_s + s) * 8 + c) * 8, 8), :]
                near = pltpu.roll(jnp.where(low_lane, both, 0.0), shift, 1)
                far = pltpu.roll(jnp.where(low_lane, 0.0, both), (shift + 64) & 127, 1)
                spots = windows(dims, half, first, c)
                pieces = [
                    jnp.where(low_sub, near, 0.0), jnp.where(low_sub, 0.0, near),
                    jnp.where(low_sub, far, 0.0), jnp.where(low_sub, 0.0, far),
                ]
                sums = [field[k, at, :] + piece for (k, at), piece in zip(spots, pieces)]
                for (k, at), total in zip(spots, sums):
                    field[k, at, :] = total

    def batch(k):
        for g in range(group):
            block = (give if g % 2 else keep)[k * (group // 2) + g // 2]
            force(me ^ (k * group + g), g, block)
        rows = chosen[...] * (time_step * spread_gain)
        high = rows.astype(BF16)
        pair = jnp.concatenate([high, (rows - high.astype(F32)).astype(BF16)], axis=1)
        pieces = jnp.dot(pair, shifts(256, 1024, 1), preferred_element_type=F32)
        for r in range(8):
            stage[pl.ds(r, lines, stride=8), :] = pieces[:, r * 128 : r * 128 + 128]
        for g in range(group):
            scatter(me ^ (k * group + g), g)

    each(count_d // group, batch)
    for part in range(halves):
        out[:, part * 128 : part * 128 + 128] = field[part, pl.ds(8, cells), :]


def owner_kernel(dims, slots, me_ref, token, targets, block_w, keep, first, *rest):
    size_x, size_y, size_z, count_d, count_s, width = dims
    received, out, picked = rest[:-2], rest[-2], rest[-1]
    me = me_ref[0]
    group = 8 if count_d % 8 == 0 else count_d
    slot_of = lax.broadcasted_iota(jnp.int32, (8, width), 1) // (width // count_s)
    row = lax.broadcasted_iota(jnp.int32, (group, width), 0)
    column_slot = lax.broadcasted_iota(jnp.int32, (group, width), 1) // (width // count_s)
    picked[0] = keep[0]
    picked[1] = first[0]
    for k, pair in enumerate(received):
        picked[2 * k + 2] = pair[0]
        picked[2 * k + 3] = pair[1]

    def batch(k):
        interp = [jnp.zeros((group, width), F32) for c in range(3)]
        live = jnp.full((group, width), -1, jnp.int32)
        for g in range(group):
            d = k * group + g
            product = lax.dot_general(
                picked[me ^ d], block_w[d], (((1,), (1,)), ((), ())), preferred_element_type=F32
            )
            lines = select_slots(product, slot_of, count_s)
            for c in range(3):
                interp[c] = jnp.where(row == g, lines[c : c + 1], interp[c])
            for s in range(count_s):
                live = jnp.where((row == g) & (column_slot == s), slots[0, s, 0, d], live)
        for c in range(3):
            at = pl.ds(k * group, group)
            target = targets[c, at, :].astype(F32)
            out[c, at, :] = jnp.where(live >= 0, (target - interp[c]) / time_step, 0.0)

    each(count_d // group, batch)


def shards(velocity, weights, targets, owner_list, slot_patch):
    size_x, size_y, size_z = velocity.shape[1:]
    count_d, count_s, markers = weights.shape[2:5]
    width = count_s * markers
    cells = 3 * size_x * size_y
    vel = velocity.reshape(cells, size_z)
    block_w = weights.reshape(count_d, width, 128)
    wanted = jnp.transpose(targets[0, 0], (1, 0, 2))
    slots = jnp.transpose(slot_patch, (0, 3, 1, 2))
    own = jnp.transpose(owner_list, (0, 3, 1, 2))
    me = jnp.full((1,), lax.axis_index("gx"), jnp.int32)
    dims = (size_x, size_y, size_z, count_d, count_s, width)
    group = 8 if count_d % 8 == 0 else count_d
    high = -(-count_s * 8 // 16) * 16
    anywhere = pl.BlockSpec(memory_space=pl.ANY)
    inside = pl.BlockSpec(memory_space=VMEM)
    scalars = pl.BlockSpec(memory_space=pltpu.SMEM)
    face_x = jax.ShapeDtypeStruct((3, size_y, size_z), F32)
    face_y = jax.ShapeDtypeStruct((3, size_x, size_z), F32)
    half = jax.ShapeDtypeStruct((count_d // 2, high, 128), BF16)
    padded = (size_z // 128, cells + 16, 128)
    params = pltpu.CompilerParams(vmem_limit_bytes=24 * 2**20)
    table = jax.ShapeDtypeStruct(slots.shape, jnp.int32)
    x_first, x_last, y_first, y_last = pl.pallas_call(
        functools.partial(faces_kernel, (size_x, size_y)),
        out_shape=(face_x, face_x, face_y, face_y),
        in_specs=[anywhere],
        out_specs=(inside,) * 4,
        scratch_shapes=[
            VMEM((size_z // 128, cells, 128), F32),
            pltpu.SemaphoreType.DMA((size_z // 128,)),
        ],
        compiler_params=pltpu.CompilerParams(vmem_limit_bytes=24 * 2**20),
        name="faces",
    )(vel)
    chunk, slots, own = pl.pallas_call(
        functools.partial(pack_kernel, (count_d, width)),
        out_shape=(jax.ShapeDtypeStruct((count_d, width + 16, 128), BF16), table, table),
        in_specs=[anywhere, inside, inside, inside],
        out_specs=(inside,) * 3,
        scratch_shapes=[VMEM((count_d * 16, 128), F32), pltpu.SemaphoreType.DMA],
        compiler_params=params,
        name="pack",
    )(block_w, wanted, slots, own)

    def ring(x, axis, step):
        size = lax.axis_size(axis)
        return lax.ppermute(x, axis, [(i, (i + step) % size) for i in range(size)])

    def swap(x, mask):
        return lax.ppermute(x, "gx", [(i, i ^ mask) for i in range(lax.axis_size("gx"))])

    x_before = ring(x_last, "gx", 1)
    x_after = ring(x_first, "gx", -1)
    y_before = ring(y_last, "gy", 1)
    y_after = ring(y_first, "gy", -1)
    arrived = lax.all_to_all(chunk, "gx", split_axis=0, concat_axis=0, tiled=True)
    field, keep, give = pl.pallas_call(
        functools.partial(predict_kernel, dims),
        out_shape=(jax.ShapeDtypeStruct(padded, F32), half, half),
        in_specs=[scalars, scalars] + [inside] * 5,
        out_specs=(inside,) * 3,
        scratch_shapes=[VMEM((group * count_s * 64, 128), F32)],
        compiler_params=params,
        name="predict",
    )(slots, me, vel, x_before, x_after, y_before, y_after)
    first = swap(give, 1)
    received = [swap(jnp.stack([keep[k], first[k]]), 2 * k) for k in range(1, count_d // 2)]
    out, token = pl.pallas_call(
        functools.partial(spread_kernel, dims),
        out_shape=(jax.ShapeDtypeStruct((cells, size_z), F32), jax.ShapeDtypeStruct((8, 128), F32)),
        in_specs=[scalars, scalars] + [inside] * 4,
        out_specs=(inside, inside),
        scratch_shapes=[
            VMEM(padded, F32),
            VMEM((group * count_s * 64, 128), F32),
            VMEM((group * count_s * 8, 128), F32),
        ],
        compiler_params=params,
        cost_estimate=pl.CostEstimate(flops=10**8, bytes_accessed=4 * 10**6, transcendentals=0),
        name="spread",
    )(slots, me, field, keep, give, arrived)
    force = pl.pallas_call(
        functools.partial(owner_kernel, dims),
        out_shape=jax.ShapeDtypeStruct((3, count_d, width), F32),
        in_specs=[scalars, scalars] + [inside] * (4 + count_d // 2),
        out_specs=inside,
        scratch_shapes=[VMEM((count_d, high, 128), BF16)],
        compiler_params=params,
        name="owner",
    )(own, me, token, wanted, block_w, keep, first, *received)
    return out.reshape(velocity.shape), jnp.transpose(force, (1, 0, 2))[None, None]


def solution(mesh):
    return jax.shard_map(
        shards,
        mesh=mesh,
        in_specs=(
            P(None, "gx", "gy", None),
            P("gx", "gy", None, None, None, None),
            P("gx", "gy", None, None, None),
            P("gx", "gy", None, None),
            P("gx", "gy", None, None),
        ),
        out_specs=(P(None, "gx", "gy", None), P("gx", "gy", None, None, None)),
        check_vma=False,
    )
```

time: 31 us -> 28 us (0.903)
  blocking collectives: 7.48 us -> 0 us
  starting transfers between devices: 11.9 us -> 15.2 us
  local copies, waits for them, and re-layouts: 0.65 us -> 1.15 us
  Pallas kernels: 7.24 us -> 7.65 us
  waiting for transfers between devices: 2.68 us -> 3.03 us
    all_to_all x1 -> x0, blocking collectives: 7.48 us -> none  [shards(): lax.all_to_all(force, 'gx', split_axis=0, concat_axis=0, tiled=True)]
    ppermute x0 -> x4, starting transfers between devices: none -> 3.94 us  [swap(): lax.ppermute(x, 'gx', [(i, i ^ mask) for i in range(lax.axis_size('gx'))])]
    ppermute x4, waiting for transfers between devices: 2.67 us -> 0.01 us  [ring(): return lax.ppermute(x, axis, [(i, (i + step) % size) for i in range(size)])]
    all_to_all x1, waiting for transfers between devices: 0.01 us -> 2.15 us  [shards(): lax.all_to_all(chunk, 'gx', split_axis=0, concat_axis=0, tiled=True)]
    all_to_all x1, starting transfers between devices: 5.31 us -> 3.48 us  [shards(): lax.all_to_all(chunk, 'gx', split_axis=0, concat_axis=0, tiled=True)]
    ppermute x4, starting transfers between devices: 6.57 us -> 7.75 us  [ring(): return lax.ppermute(x, axis, [(i, (i + step) % size) for i in range(size)])]
    ppermute x0 -> x4, waiting for transfers between devices: none -> 0.86 us  [swap(): lax.ppermute(x, 'gx', [(i, i ^ mask) for i in range(lax.axis_size('gx'))])]
    unnamed x14 -> x12, local copies, waits for them, and re-layouts: 0.64 us -> 1.15 us
  transfers between devices with their start and end apart: 5 -> 9, of which waited for: 1 -> 2; matrix products, arithmetic and copies ran while one was open for 0% -> 0% of each run, Pallas kernels for 0% -> 22%
where the time goes in v3:
time: 28 us; the launch traced here: 27.8 us
  starting transfers between devices  15.2 us (54%)
  Pallas kernels  7.65 us (27%)
  waiting for transfers between devices  3.03 us (11%)
  local copies, waits for them, and re-layouts  1.15 us (4%)
  between operations  0.75 us (3%)
    ppermute x4, starting transfers between devices, ring(): return lax.ppermute(x, axis, [(i, (i + step) % size) for i in range(size)])  7.75 us
    ppermute x4, starting transfers between devices, swap(): lax.ppermute(x, 'gx', [(i, i ^ mask) for i in range(lax.axis_size('gx'))])  3.94 us
    all_to_all x1, starting transfers between devices, shards(): lax.all_to_all(chunk, 'gx', split_axis=0, concat_axis=0, tiled=True)  3.48 us
    pallas_call x1, Pallas kernels, shards(): pl.pallas_call(functools.partial(spread_kernel, dims), out_shape=(jax.Sha...  3.4 us
    all_to_all x1, waiting for transfers between devices, shards(): lax.all_to_all(chunk, 'gx', split_axis=0, concat_axis=0, tiled=True)  2.15 us
    pallas_call x1, Pallas kernels, shards(): pl.pallas_call(functools.partial(predict_kernel, dims), out_shape=(jax.Sh...  1.78 us
    pallas_call x1, Pallas kernels, shards(): pl.pallas_call(functools.partial(owner_kernel, dims), out_shape=jax.Shape...  1.52 us
    unnamed x12, local copies, waits for them, and re-layouts  1.15 us
  transfers between devices with their start and end apart: 9, of which 2 were waited for; matrix products, arithmetic and copies ran while one was open for 0% of the time, Pallas kernels for 22%

profile of v3, /device:TPU:0, one launch (start us, length us, event | category | flops | bytes accessed | tf_op | source)
XLA Modules:
  0.0 27.8 jit_solution(8536470304096686217)
XLA Ops:
  0.6 0.0 copy-start
  0.6 1.1 %copy-done = f32[3,16,16,256]{3,2,1,0:T(8,128)S(1)} copy-done((f32[3,16,16,256]{3,2,1,0:T(8,128)S(1)}, f32[3,16,16,256]{3,2,1,0:T(8,128)}, u32[]{:S(2)}) %copy-start) | copy-done | bytes 786456
  1.8 0.0 copy-start.2
  1.8 0.0 copy-start.3
  1.8 0.0 copy-start.4
  1.8 0.0 copy-start.5
  1.8 0.1 faces.1
  1.9 0.0 copy-start.1
  1.9 0.5 %collective-permute-start = (f32[3,16,256]{2,1,0:T(8,128)S(1)}, f32[3,16,256]{2,1,0:T(8,128)S(1)}, u32[]{:S(2)}, u32[]{:S(2)}) collective-permute-start(f32[3,16,256]{2,1,0:T(8,128)S(1)} %get-tuple-element.15), channel_id=1, source_target_pairs={{0,4},{4,8},{8,12},{12,16},{16,20},{20,24},{24,28},{28,0},{1,5},{5... | collective-permute-start | bytes 147464 | tf_op jit(solution)/shard_map/ppermute | solution.py:321
  2.4 2.9 %collective-permute-start.1 = (f32[3,16,256]{2,1,0:T(8,128)S(1)}, f32[3,16,256]{2,1,0:T(8,128)S(1)}, u32[]{:S(2)}, u32[]{:S(2)}) collective-permute-start(f32[3,16,256]{2,1,0:T(8,128)S(1)} %get-tuple-element.16), channel_id=1, source_target_pairs={{0,28},{4,0},{8,4},{12,8},{16,12},{20,16},{24,20},{28,24},{1,29},{... | collective-permute-start | bytes 147464 | tf_op jit(solution)/shard_map/ppermute | solution.py:321
  5.4 2.3 %collective-permute-start.2 = (f32[3,16,256]{2,1,0:T(8,128)S(1)}, f32[3,16,256]{2,1,0:T(8,128)S(1)}, u32[]{:S(2)}, u32[]{:S(2)}) collective-permute-start(f32[3,16,256]{2,1,0:T(8,128)S(1)} %get-tuple-element.17), channel_id=1, source_target_pairs={{0,1},{1,2},{2,3},{3,0},{4,5},{5,6},{6,7},{7,4},{8,9},{9,10},{10,1... | collective-permute-start | bytes 147464 | tf_op jit(solution)/shard_map/ppermute | solution.py:321
  7.6 2.0 %collective-permute-start.3 = (f32[3,16,256]{2,1,0:T(8,128)S(1)}, f32[3,16,256]{2,1,0:T(8,128)S(1)}, u32[]{:S(2)}, u32[]{:S(2)}) collective-permute-start(f32[3,16,256]{2,1,0:T(8,128)S(1)} %get-tuple-element.18), channel_id=1, source_target_pairs={{0,3},{1,0},{2,1},{3,2},{4,7},{5,4},{6,5},{7,6},{8,11},{9,8},{10,9... | collective-permute-start | bytes 147464 | tf_op jit(solution)/shard_map/ppermute | solution.py:321
  9.7 0.0 copy-done.2
  9.7 0.0 copy-done.3
  9.7 0.0 copy-done.4
  9.7 0.0 copy-done.5
  9.7 0.8 %pack.1 = (bf16[8,208,128]{2,1,0:T(8,128)(2,1)}, s32[1,3,1,8]{3,2,1,0:T(1,128)S(1)}, s32[1,3,1,8]{3,2,1,0:T(1,128)S(1)}) custom-call(bf16[8,192,128]{2,1,0:T(8,128)(2,1)S(1)} %bitcast.14, bf16[3,8,192]{2,1,0:T(8,128)(2,1)S(1)} %bitcast.16, s32[1,3,1,8]{3,2,1,0:T(1,128)S(1)} %bitcast.18, s32[1,3,1,8]{3,2,1,0:T(1,128)S(1)} %bitcast.19), custom_call_target="tpu_custom_call" | custom-call | tf_op jit(solution)/shard_map/pack/pallas_call | solution.py:309
  10.5 3.5 %all-to-all-start = ((bf16[8,208,128]{2,1,0:T(8,128)(2,1)}), bf16[8,208,128]{2,1,0:T(8,128)(2,1)S(1)}, u32[]{:S(2)}, u32[]{:S(2)}) async-start(bf16[8,208,128]{2,1,0:T(8,128)(2,1)} %get-tuple-element.22), calls=%async_computation | async-start | bytes 851968 | tf_op jit(solution)/shard_map/all_to_all | solution.py:330
  14.0 0.0 collective-permute-done.x_before
  14.0 0.0 collective-permute-done.1.x_after
  14.0 0.0 collective-permute-done.2.y_before
  14.0 0.0 collective-permute-done.3.y_after
  14.0 0.0 copy-done.1
  14.1 1.8 %predict.1 = (f32[2,784,128]{2,1,0:T(8,128)S(1)}, bf16[4,32,128]{2,1,0:T(8,128)(2,1)S(1)}, bf16[4,32,128]{2,1,0:T(8,128)(2,1)S(1)}) custom-call(s32[1,3,1,8]{3,2,1,0:T(1,128)S(1)} %get-tuple-element.14.slots, s32[1]{0:T(128)} %bitcast.5.me_ref, f32[768,256]{1,0:T(8,128)S(1)} %bitcast.13, f32[3,16,256]{2,1,0:T(8,128)S(1)} %collective-permute-done.x_before, ...), custom_call_target="tpu_custom_call" | custom-call | tf_op jit(solution)/shard_map/predict/pallas_call | solution.py:331
  15.8 0.5 %collective-permute-start.4 = (bf16[4,32,128]{2,1,0:T(8,128)(2,1)S(1)}, bf16[4,32,128]{2,1,0:T(8,128)(2,1)S(1)}, u32[]{:S(2)}, u32[]{:S(2)}) collective-permute-start(bf16[4,32,128]{2,1,0:T(8,128)(2,1)S(1)} %get-tuple-element.21.give), channel_id=1, source_target_pairs={{0,4},{4,0},{8,12},{12,8},{16,20},{20,16},{24,28},{28,24},{1,5},{5... | collective-permute-start | bytes 98312 | tf_op jit(solution)/shard_map/ppermute | solution.py:324
  16.3 0.9 %collective-permute-done.4.first = bf16[4,32,128]{2,1,0:T(8,128)(2,1)S(1)} collective-permute-done((bf16[4,32,128]{2,1,0:T(8,128)(2,1)S(1)}, bf16[4,32,128]{2,1,0:T(8,128)(2,1)S(1)}, u32[]{:S(2)}, u32[]{:S(2)}) %collective-permute-start.4) | collective-permute-done | bytes 32800 | tf_op jit(solution)/shard_map/ppermute | solution.py:324
  17.2 1.9 %collective-permute-start.5 = (bf16[2,32,128]{2,1,0:T(8,128)(2,1)S(1)}, bf16[2,32,128]{2,1,0:T(8,128)(2,1)S(1)}, u32[]{:S(2)}, u32[]{:S(2)}) collective-permute-start(bf16[2,32,128]{2,1,0:T(8,128)(2,1)S(1)} %pad_maximum_fusion), channel_id=1, source_target_pairs={{0,8},{4,12},{8,0},{12,4},{16,24},{20,28},{24,16},{28,20},{1,9},{5... | collective-permute-start | bytes 49160 | tf_op jit(solution)/shard_map/ppermute | solution.py:324
  19.0 1.5 %collective-permute-start.6 = (bf16[2,32,128]{2,1,0:T(8,128)(2,1)S(1)}, bf16[2,32,128]{2,1,0:T(8,128)(2,1)S(1)}, u32[]{:S(2)}, u32[]{:S(2)}) collective-permute-start(bf16[2,32,128]{2,1,0:T(8,128)(2,1)S(1)} %pad_maximum_fusion.1), channel_id=1, source_target_pairs={{0,16},{4,20},{8,24},{12,28},{16,0},{20,4},{24,8},{28,12},{1,17},{... | collective-permute-start | bytes 49160 | tf_op jit(solution)/shard_map/ppermute | solution.py:324
  20.5 0.1 collective-permute-start.7
  20.7 2.2 %all-to-all-done.blocks = bf16[8,208,128]{2,1,0:T(8,128)(2,1)S(1)} async-done(((bf16[8,208,128]{2,1,0:T(8,128)(2,1)}), bf16[8,208,128]{2,1,0:T(8,128)(2,1)S(1)}, u32[]{:S(2)}, u32[]{:S(2)}) %all-to-all-start) | async-done | bytes 426016 | tf_op jit(solution)/shard_map/all_to_all | solution.py:330
  22.8 3.4 %spread.1 = (f32[768,256]{1,0:T(8,128)}, f32[8,128]{1,0:T(8,128)S(1)}) custom-call(s32[1,3,1,8]{3,2,1,0:T(1,128)S(1)} %get-tuple-element.14.slots, s32[1]{0:T(128)} %bitcast.5.me_ref, f32[2,784,128]{2,1,0:T(8,128)S(1)} %get-tuple-element.19.before, bf16[4,32,128]{2,1,0:T(8,128)(2,1)S(1)} %get-tuple-element.20.keep, ...), custom_call_target="tpu_custom_call" | custom-call | flops 100000000 | bytes 4000000 | tf_op jit(solution)/shard_map/spread/pallas_call | solution.py:342
  26.2 0.0 collective-permute-done.5.rest_0_
  26.2 0.0 collective-permute-done.6.rest_1_
  26.2 0.0 collective-permute-done.7.rest_2_
  26.2 1.5 %owner.1 = f32[3,8,192]{2,1,0:T(8,128)} custom-call(s32[1,3,1,8]{3,2,1,0:T(1,128)S(1)} %get-tuple-element.24.slots, s32[1]{0:T(128)} %bitcast.5.me_ref, f32[8,128]{1,0:T(8,128)S(1)} %get-tuple-element.25.token, bf16[3,8,192]{2,1,0:T(8,128)(2,1)S(1)} %bitcast.17, bf16[8,192,128]{2,1,0:T(8,128)(2,1)S(1)} %bitcast.15, ...), custom_call_target="tpu_custom_call" | custom-call | tf_op jit(solution)/shard_map/owner/pallas_call | solution.py:356
  (5 shorter events, 0.0 us)
Async XLA Ops:
  0.6 1.1 %copy-start = (f32[3,16,16,256]{3,2,1,0:T(8,128)S(1)}, f32[3,16,16,256]{3,2,1,0:T(8,128)}, u32[]{:S(2)}) copy-start(f32[3,16,16,256]{3,2,1,0:T(8,128)} %param.5) | copy-start | bytes 2359300
  1.8 7.9 %copy-start.2 = (bf16[1,1,8,3,64,128]{5,4,3,2,1,0:T(8,128)(2,1)S(1)}, bf16[1,1,8,3,64,128]{5,4,3,2,1,0:T(8,128)(2,1)}, u32[]{:S(2)}) copy-start(bf16[1,1,8,3,64,128]{5,4,3,2,1,0:T(8,128)(2,1)} %param.6) | copy-start | bytes 1179652
  1.8 7.9 %copy-start.3 = (bf16[1,1,8,3,192]{4,2,3,1,0:T(8,128)(2,1)S(1)}, bf16[1,1,8,3,192]{4,2,3,1,0:T(8,128)(2,1)}, u32[]{:S(2)}) copy-start(bf16[1,1,8,3,192]{4,2,3,1,0:T(8,128)(2,1)} %param.7) | copy-start | bytes 27652
  1.8 7.9 %copy-start.4 = (s32[1,1,8,3]{2,1,3,0:T(1,128)S(1)}, s32[1,1,8,3]{2,1,3,0:T(1,128)}, u32[]{:S(2)}) copy-start(s32[1,1,8,3]{2,1,3,0:T(1,128)} %param.9) | copy-start | bytes 292
  1.8 7.9 %copy-start.5 = (s32[1,1,8,3]{2,1,3,0:T(1,128)S(1)}, s32[1,1,8,3]{2,1,3,0:T(1,128)}, u32[]{:S(2)}) copy-start(s32[1,1,8,3]{2,1,3,0:T(1,128)} %param.8) | copy-start | bytes 292
  1.9 12.1 %copy-start.1 = (f32[3,16,16,256]{3,2,1,0:T(8,128)S(1)}, f32[3,16,16,256]{3,2,1,0:T(8,128)}, u32[]{:S(2)}) copy-start(f32[3,16,16,256]{3,2,1,0:T(8,128)} %param.5) | copy-start | bytes 2359300
  1.9 12.1 %collective-permute-start = (f32[3,16,256]{2,1,0:T(8,128)S(1)}, f32[3,16,256]{2,1,0:T(8,128)S(1)}, u32[]{:S(2)}, u32[]{:S(2)}) collective-permute-start(f32[3,16,256]{2,1,0:T(8,128)S(1)} %get-tuple-element.15), channel_id=1, source_target_pairs={{0,4},{4,8},{8,12},{12,16},{16,20},{20,24},{24,28},{28,0},{1,5},{5... | collective-permute-start | bytes 147464 | tf_op jit(solution)/shard_map/ppermute | solution.py:321
  2.4 11.6 %collective-permute-start.1 = (f32[3,16,256]{2,1,0:T(8,128)S(1)}, f32[3,16,256]{2,1,0:T(8,128)S(1)}, u32[]{:S(2)}, u32[]{:S(2)}) collective-permute-start(f32[3,16,256]{2,1,0:T(8,128)S(1)} %get-tuple-element.16), channel_id=1, source_target_pairs={{0,28},{4,0},{8,4},{12,8},{16,12},{20,16},{24,20},{28,24},{1,29},{... | collective-permute-start | bytes 147464 | tf_op jit(solution)/shard_map/ppermute | solution.py:321
  5.4 8.7 %collective-permute-start.2 = (f32[3,16,256]{2,1,0:T(8,128)S(1)}, f32[3,16,256]{2,1,0:T(8,128)S(1)}, u32[]{:S(2)}, u32[]{:S(2)}) collective-permute-start(f32[3,16,256]{2,1,0:T(8,128)S(1)} %get-tuple-element.17), channel_id=1, source_target_pairs={{0,1},{1,2},{2,3},{3,0},{4,5},{5,6},{6,7},{7,4},{8,9},{9,10},{10,1... | collective-permute-start | bytes 147464 | tf_op jit(solution)/shard_map/ppermute | solution.py:321
  7.6 6.4 %collective-permute-start.3 = (f32[3,16,256]{2,1,0:T(8,128)S(1)}, f32[3,16,256]{2,1,0:T(8,128)S(1)}, u32[]{:S(2)}, u32[]{:S(2)}) collective-permute-start(f32[3,16,256]{2,1,0:T(8,128)S(1)} %get-tuple-element.18), channel_id=1, source_target_pairs={{0,3},{1,0},{2,1},{3,2},{4,7},{5,4},{6,5},{7,6},{8,11},{9,8},{10,9... | collective-permute-start | bytes 147464 | tf_op jit(solution)/shard_map/ppermute | solution.py:321
  10.5 12.3 %all-to-all-start = ((bf16[8,208,128]{2,1,0:T(8,128)(2,1)}), bf16[8,208,128]{2,1,0:T(8,128)(2,1)S(1)}, u32[]{:S(2)}, u32[]{:S(2)}) async-start(bf16[8,208,128]{2,1,0:T(8,128)(2,1)} %get-tuple-element.22), calls=%async_computation | async-start | bytes 851968 | tf_op jit(solution)/shard_map/all_to_all | solution.py:330
  15.8 1.3 %collective-permute-start.4 = (bf16[4,32,128]{2,1,0:T(8,128)(2,1)S(1)}, bf16[4,32,128]{2,1,0:T(8,128)(2,1)S(1)}, u32[]{:S(2)}, u32[]{:S(2)}) collective-permute-start(bf16[4,32,128]{2,1,0:T(8,128)(2,1)S(1)} %get-tuple-element.21.give), channel_id=1, source_target_pairs={{0,4},{4,0},{8,12},{12,8},{16,20},{20,16},{24,28},{28,24},{1,5},{5... | collective-permute-start | bytes 98312 | tf_op jit(solution)/shard_map/ppermute | solution.py:324
  17.2 9.1 %collective-permute-start.5 = (bf16[2,32,128]{2,1,0:T(8,128)(2,1)S(1)}, bf16[2,32,128]{2,1,0:T(8,128)(2,1)S(1)}, u32[]{:S(2)}, u32[]{:S(2)}) collective-permute-start(bf16[2,32,128]{2,1,0:T(8,128)(2,1)S(1)} %pad_maximum_fusion), channel_id=1, source_target_pairs={{0,8},{4,12},{8,0},{12,4},{16,24},{20,28},{24,16},{28,20},{1,9},{5... | collective-permute-start | bytes 49160 | tf_op jit(solution)/shard_map/ppermute | solution.py:324
  19.0 7.2 %collective-permute-start.6 = (bf16[2,32,128]{2,1,0:T(8,128)(2,1)S(1)}, bf16[2,32,128]{2,1,0:T(8,128)(2,1)S(1)}, u32[]{:S(2)}, u32[]{:S(2)}) collective-permute-start(bf16[2,32,128]{2,1,0:T(8,128)(2,1)S(1)} %pad_maximum_fusion.1), channel_id=1, source_target_pairs={{0,16},{4,20},{8,24},{12,28},{16,0},{20,4},{24,8},{28,12},{1,17},{... | collective-permute-start | bytes 49160 | tf_op jit(solution)/shard_map/ppermute | solution.py:324
  20.5 5.7 %collective-permute-start.7 = (bf16[2,32,128]{2,1,0:T(8,128)(2,1)S(1)}, bf16[2,32,128]{2,1,0:T(8,128)(2,1)S(1)}, u32[]{:S(2)}, u32[]{:S(2)}) collective-permute-start(bf16[2,32,128]{2,1,0:T(8,128)(2,1)S(1)} %pad_maximum_fusion.2), channel_id=1, source_target_pairs={{0,24},{4,28},{8,16},{12,20},{16,8},{20,12},{24,0},{28,4},{1,25},{... | collective-permute-start | bytes 49160 | tf_op jit(solution)/shard_map/ppermute | solution.py:324

commit v4 on v3

--- a/solution.py
+++ b/solution.py
@@ -2,6 +2,8 @@
 
 import jax
 import jax.numpy as jnp
+import ml_dtypes
+import numpy as np
 from jax import lax
 from jax.experimental import pallas as pl
 from jax.experimental.pallas import tpu as pltpu
@@ -71,13 +73,11 @@
     return lax.div(x, size), lax.rem(x, size)
 
 
-def shifts(rows, columns, piece_axis):
-    shape = (rows, columns)
-    piece = lax.broadcasted_iota(jnp.int32, shape, piece_axis)
-    place = lax.broadcasted_iota(jnp.int32, shape, 1 - piece_axis) & 127
-    m = piece & 127
-    hit = ((m & 63) < 8) & (place == m + 8 * lax.shift_right_logical(piece, 7))
-    return jnp.where(hit, 1.0, 0.0).astype(BF16)
+def shifts():
+    piece = np.arange(1024)[:, None]
+    m = piece % 128
+    hit = (m % 64 < 8) & (np.arange(128)[None, :] == m + 8 * (piece // 128))
+    return hit.astype(ml_dtypes.bfloat16)
 
 
 def locate(dims, slots, i, s):
@@ -102,18 +102,23 @@
 
 
 def select_slots(product, slot_of, count_s):
-    interp = product[0:8]
-    for s in range(1, count_s):
-        interp = jnp.where(slot_of == s, product[8 * s : 8 * s + 8], interp)
+    interp = None
+    for s in range(count_s):
+        part = product[s // 2 * 8 : s // 2 * 8 + 8]
+        if s % 2:
+            part = pltpu.roll(part, 4, 0)
+        interp = part if s == 0 else jnp.where(slot_of == s, part, interp)
     return interp
 
 
 def predict_kernel(
-    dims, slots, me_ref, vel, x_before, x_after, y_before, y_after, field, keep, give, stage,
+    dims, table, vel, x_before, x_after, y_before, y_after, gathers, field, keep, give, stage, slots, sem,
 ):
     size_x, size_y, size_z, count_d, count_s, width = dims
     halves = size_z // 128
-    me = me_ref[0]
+    me = lax.axis_index("gx")
+    move = pltpu.make_async_copy(table, slots, sem)
+    move.start()
 
     row = lax.broadcasted_iota(jnp.int32, (size_y, size_z), 0)
     col = lax.broadcasted_iota(jnp.int32, (size_y, size_z), 1)
@@ -133,23 +138,23 @@
             top.append(jnp.where(col == size_z - 1, 0.0, pltpu.roll(here, size_z - 1, 1)))
             bottom.append(jnp.where(col == 0, 0.0, pltpu.roll(here, 1, 1)))
         for c in range(3):
-            laplace = fore[c] + back[c] + right[c] + left[c] + top[c] + bottom[c] - 6.0 * center[c]
-            advect = (
-                center[0] * (fore[c] - back[c]) * 0.5
-                + center[1] * (right[c] - left[c]) * 0.5
-                + center[2] * (top[c] - bottom[c]) * 0.5
+            total = (
+                (fore[c] + back[c]) - center[0] * (fore[c] - back[c])
+                + (right[c] + left[c]) - center[1] * (right[c] - left[c])
+                + (top[c] + bottom[c]) - center[2] * (top[c] - bottom[c])
             )
             base = 8 + (c * size_x + x) * size_y
-            result = center[c] + time_step * (viscosity * laplace - advect)
+            result = (1.0 - 6.0 * time_step * viscosity) * center[c] + (0.5 * time_step) * total
             for part in range(halves):
                 field[part, pl.ds(base, size_y), :] = result[:, part * 128 : part * 128 + 128]
 
     each(size_x, stencil, True)
 
+    move.wait()
     low_lane, low_sub = low_halves()
     group = 8 if count_d % 8 == 0 else count_d
-    lines = group * count_s * 8
-    tail = jnp.zeros((keep.shape[1] - count_s * 8, 128), F32)
+    high = keep.shape[1]
+    lines = group * high
 
     def gather(i, g):
         for s in range(count_s):
@@ -158,55 +163,65 @@
                 w = [field[k, at, :] for k, at in windows(dims, half, first, c)]
                 near = pltpu.roll(jnp.where(low_sub, w[0], w[1]), (128 - shift) & 127, 1)
                 far = pltpu.roll(jnp.where(low_sub, w[2], w[3]), (192 - shift) & 127, 1)
-                stage[pl.ds(((g * count_s + s) * 8 + c) * 8, 8), :] = jnp.where(low_lane, near, far)
+                stage[pl.ds((g * high + s * 4 + c) * 8, 8), :] = jnp.where(low_lane, near, far)
 
     def batch(k):
         for g in range(group):
             gather(me ^ (k * group + g), g)
         picked = jnp.concatenate([stage[pl.ds(r, lines, stride=8), :] for r in range(8)], axis=1)
-        picked = jnp.dot(picked.astype(BF16), shifts(1024, 128, 0), preferred_element_type=F32)
+        picked = jnp.dot(picked.astype(BF16), gathers[...], preferred_element_type=F32).astype(BF16)
         for g in range(group):
-            mine = picked[g * count_s * 8 : (g + 1) * count_s * 8]
-            block = jnp.concatenate([mine, tail], axis=0).astype(BF16)
-            (give if g % 2 else keep)[k * (group // 2) + g // 2] = block
-
+            (give if g % 2 else keep)[k * (group // 2) + g // 2] = picked[g * high : (g + 1) * high]
+
+    stage[...] = jnp.zeros_like(stage)
     each(count_d // group, batch)
 
 
-def spread_kernel(dims, slots, me_ref, before, keep, give, blocks, out, token, field, stage, chosen):
+def spread_kernel(
+    dims, table, before, keep, give, blocks, scatters, out, token, field, stage, chosen, slots, sems,
+):
     size_x, size_y, size_z, count_d, count_s, width = dims
     cells = 3 * size_x * size_y
     halves = size_z // 128
-    me = me_ref[0]
+    me = lax.axis_index("gx")
+    move_field = pltpu.make_async_copy(before, field, sems.at[0])
+    move_slots = pltpu.make_async_copy(table, slots, sems.at[1])
+    move_slots.start()
+    move_field.start()
+    token[...] = jnp.zeros_like(token)
     low_lane, low_sub = low_halves()
     group = 8 if count_d % 8 == 0 else count_d
-    lines = group * count_s * 8
+    high = keep.shape[1]
+    lines = group * high
     slot_of = lax.broadcasted_iota(jnp.int32, (8, width), 1) // (width // count_s)
-    field[...] = before[...]
-    token[...] = jnp.zeros_like(token)
-
-    def force(i, g, block):
-        block_w = blocks[i, 0:width, :]
+    low_row = lax.broadcasted_iota(jnp.int32, (8, width), 0) < 4
+
+    def interpolate(i, block):
+        return lax.dot_general(
+            block, blocks[i, 0:width, :], (((1,), (1,)), ((), ())), preferred_element_type=F32
+        )
+
+    def force(i, product):
         tail = blocks[i, width : width + 16, :].astype(F32)
         target = jnp.concatenate([tail[0:8, :], tail[8:16, 0 : width - 128]], axis=1)
-        product = lax.dot_general(
-            block, block_w, (((1,), (1,)), ((), ())), preferred_element_type=F32
-        )
         interp = select_slots(product, slot_of, count_s)
         live = jnp.full((8, width), slots[0, 0, 0, i], jnp.int32)
         for s in range(1, count_s):
             live = jnp.where(slot_of == s, slots[0, s, 0, i], live)
         value = jnp.where(live >= 0, (target - interp) / time_step, 0.0)
-        rows = jnp.concatenate([jnp.where(slot_of == s, value, 0.0) for s in range(count_s)], axis=0)
-        chosen[pl.ds(g * count_s * 8, count_s * 8), :] = jnp.dot(
-            rows.astype(BF16), block_w, preferred_element_type=F32
-        )
+        swapped = pltpu.roll(value, 4, 0)
+        rows = []
+        for first in range(0, high // 4, 2):
+            lower = jnp.where(slot_of == first, value, 0.0)
+            upper = jnp.where(slot_of == first + 1, swapped, 0.0)
+            rows.append(jnp.where(low_row, lower, upper))
+        return jnp.concatenate(rows, axis=0).astype(BF16)
 
     def scatter(i, g):
         for s in range(count_s):
             half, first, shift = locate(dims, slots, i, s)
             for c in range(3):
-                both = stage[pl.ds(((g * count_s + s) * 8 + c) * 8, 8), :]
+                both = stage[pl.ds((g * high + s * 4 + c) * 8, 8), :]
                 near = pltpu.roll(jnp.where(low_lane, both, 0.0), shift, 1)
                 far = pltpu.roll(jnp.where(low_lane, 0.0, both), (shift + 64) & 127, 1)
                 spots = windows(dims, half, first, c)
@@ -219,27 +234,52 @@
                     field[k, at, :] = total
 
     def batch(k):
+        owners = [me ^ (k * group + g) for g in range(group)]
+        products = [
+            interpolate(owners[g], (give if g % 2 else keep)[k * (group // 2) + g // 2])
+            for g in range(group)
+        ]
+        if count_d == group:
+            move_slots.wait()
+        forces = [force(owners[g], products[g]) for g in range(group)]
         for g in range(group):
-            block = (give if g % 2 else keep)[k * (group // 2) + g // 2]
-            force(me ^ (k * group + g), g, block)
+            chosen[pl.ds(g * high, high), :] = jnp.dot(
+                forces[g], blocks[owners[g], 0:width, :], preferred_element_type=F32
+            )
         rows = chosen[...] * (time_step * spread_gain)
-        high = rows.astype(BF16)
-        pair = jnp.concatenate([high, (rows - high.astype(F32)).astype(BF16)], axis=1)
-        pieces = jnp.dot(pair, shifts(256, 1024, 1), preferred_element_type=F32)
+        upper = rows.astype(BF16)
+        lower = (rows - upper.astype(F32)).astype(BF16)
+        pieces = jnp.dot(upper, scatters[...], preferred_element_type=F32)
+        pieces = pieces + jnp.dot(lower, scatters[...], preferred_element_type=F32)
         for r in range(8):
             stage[pl.ds(r, lines, stride=8), :] = pieces[:, r * 128 : r * 128 + 128]
+        if count_d == group:
+            move_field.wait()
         for g in range(group):
-            scatter(me ^ (k * group + g), g)
-
+            scatter(owners[g], g)
+
+    if count_d != group:
+        move_slots.wait()
+        move_field.wait()
     each(count_d // group, batch)
-    for part in range(halves):
-        out[:, part * 128 : part * 128 + 128] = field[part, pl.ds(8, cells), :]
-
-
-def owner_kernel(dims, slots, me_ref, token, targets, block_w, keep, first, *rest):
+    moves = [
+        pltpu.make_async_copy(
+            field.at[part, pl.ds(8, cells), :], out.at[:, pl.ds(part * 128, 128)], sems.at[2 + part]
+        )
+        for part in range(halves)
+    ]
+    for move in moves:
+        move.start()
+    for move in moves:
+        move.wait()
+
+
+def owner_kernel(dims, table, token, targets, block_w, keep, first, *rest):
     size_x, size_y, size_z, count_d, count_s, width = dims
-    received, out, picked = rest[:-2], rest[-2], rest[-1]
-    me = me_ref[0]
+    received, (out, picked, slots, sem) = rest[:-4], rest[-4:]
+    me = lax.axis_index("gx")
+    move = pltpu.make_async_copy(table, slots, sem)
+    move.start()
     group = 8 if count_d % 8 == 0 else count_d
     slot_of = lax.broadcasted_iota(jnp.int32, (8, width), 1) // (width // count_s)
     row = lax.broadcasted_iota(jnp.int32, (group, width), 0)
@@ -249,20 +289,27 @@
     for k, pair in enumerate(received):
         picked[2 * k + 2] = pair[0]
         picked[2 * k + 3] = pair[1]
+    if count_d != group:
+        move.wait()
 
     def batch(k):
+        products = [
+            lax.dot_general(
+                picked[me ^ (k * group + g)], block_w[k * group + g],
+                (((1,), (1,)), ((), ())), preferred_element_type=F32,
+            )
+            for g in range(group)
+        ]
+        if count_d == group:
+            move.wait()
         interp = [jnp.zeros((group, width), F32) for c in range(3)]
         live = jnp.full((group, width), -1, jnp.int32)
         for g in range(group):
-            d = k * group + g
-            product = lax.dot_general(
-                picked[me ^ d], block_w[d], (((1,), (1,)), ((), ())), preferred_element_type=F32
-            )
-            lines = select_slots(product, slot_of, count_s)
+            lines = select_slots(products[g], slot_of, count_s)
             for c in range(3):
                 interp[c] = jnp.where(row == g, lines[c : c + 1], interp[c])
             for s in range(count_s):
-                live = jnp.where((row == g) & (column_slot == s), slots[0, s, 0, d], live)
+                live = jnp.where((row == g) & (column_slot == s), slots[0, s, 0, k * group + g], live)
         for c in range(3):
             at = pl.ds(k * group, group)
             target = targets[c, at, :].astype(F32)
@@ -281,19 +328,18 @@
     wanted = jnp.transpose(targets[0, 0], (1, 0, 2))
     slots = jnp.transpose(slot_patch, (0, 3, 1, 2))
     own = jnp.transpose(owner_list, (0, 3, 1, 2))
-    me = jnp.full((1,), lax.axis_index("gx"), jnp.int32)
     dims = (size_x, size_y, size_z, count_d, count_s, width)
     group = 8 if count_d % 8 == 0 else count_d
-    high = -(-count_s * 8 // 16) * 16
+    high = -(-count_s * 4 // 16) * 16
     anywhere = pl.BlockSpec(memory_space=pl.ANY)
     inside = pl.BlockSpec(memory_space=VMEM)
-    scalars = pl.BlockSpec(memory_space=pltpu.SMEM)
     face_x = jax.ShapeDtypeStruct((3, size_y, size_z), F32)
     face_y = jax.ShapeDtypeStruct((3, size_x, size_z), F32)
     half = jax.ShapeDtypeStruct((count_d // 2, high, 128), BF16)
     padded = (size_z // 128, cells + 16, 128)
     params = pltpu.CompilerParams(vmem_limit_bytes=24 * 2**20)
     table = jax.ShapeDtypeStruct(slots.shape, jnp.int32)
+    staged = (pltpu.SMEM(slots.shape, jnp.int32), pltpu.SemaphoreType.DMA)
     x_first, x_last, y_first, y_last = pl.pallas_call(
         functools.partial(faces_kernel, (size_x, size_y)),
         out_shape=(face_x, face_x, face_y, face_y),
@@ -331,37 +377,39 @@
     field, keep, give = pl.pallas_call(
         functools.partial(predict_kernel, dims),
         out_shape=(jax.ShapeDtypeStruct(padded, F32), half, half),
-        in_specs=[scalars, scalars] + [inside] * 5,
+        in_specs=[inside] * 7,
         out_specs=(inside,) * 3,
-        scratch_shapes=[VMEM((group * count_s * 64, 128), F32)],
+        scratch_shapes=[VMEM((group * high * 8, 128), F32), *staged],
         compiler_params=params,
         name="predict",
-    )(slots, me, vel, x_before, x_after, y_before, y_after)
+    )(slots, vel, x_before, x_after, y_before, y_after, jnp.asarray(shifts()))
     first = swap(give, 1)
     received = [swap(jnp.stack([keep[k], first[k]]), 2 * k) for k in range(1, count_d // 2)]
     out, token = pl.pallas_call(
         functools.partial(spread_kernel, dims),
         out_shape=(jax.ShapeDtypeStruct((cells, size_z), F32), jax.ShapeDtypeStruct((8, 128), F32)),
-        in_specs=[scalars, scalars] + [inside] * 4,
-        out_specs=(inside, inside),
+        in_specs=[inside] * 6,
+        out_specs=(anywhere, inside),
         scratch_shapes=[
             VMEM(padded, F32),
-            VMEM((group * count_s * 64, 128), F32),
-            VMEM((group * count_s * 8, 128), F32),
+            VMEM((group * high * 8, 128), F32),
+            VMEM((group * high, 128), F32),
+            staged[0],
+            pltpu.SemaphoreType.DMA((2 + size_z // 128,)),
         ],
         compiler_params=params,
         cost_estimate=pl.CostEstimate(flops=10**8, bytes_accessed=4 * 10**6, transcendentals=0),
         name="spread",
-    )(slots, me, field, keep, give, arrived)
+    )(slots, field, keep, give, arrived, jnp.asarray(shifts().T))
     force = pl.pallas_call(
         functools.partial(owner_kernel, dims),
         out_shape=jax.ShapeDtypeStruct((3, count_d, width), F32),
-        in_specs=[scalars, scalars] + [inside] * (4 + count_d // 2),
+        in_specs=[inside] * (5 + count_d // 2),
         out_specs=inside,
-        scratch_shapes=[VMEM((count_d, high, 128), BF16)],
+        scratch_shapes=[VMEM((count_d, high, 128), BF16), *staged],
         compiler_params=params,
         name="owner",
-    )(own, me, token, wanted, block_w, keep, first, *received)
+    )(own, token, wanted, block_w, keep, first, *received)
     return out.reshape(velocity.shape), jnp.transpose(force, (1, 0, 2))[None, None]
 
 

time: 28 us -> 26.7 us (0.954)
  Pallas kernels: 7.65 us -> 5.93 us
    pallas_call x1, Pallas kernels: 3.4 us -> 2.18 us  [shards(): pl.pallas_call(functools.partial(spread_kernel, dims), out_shape=(jax.Sha...]
    pallas_call x1, Pallas kernels: 1.78 us -> 1.49 us  [shards(): pl.pallas_call(functools.partial(predict_kernel, dims), out_shape=(jax.Sh...]
    unnamed x12 -> x16, local copies, waits for them, and re-layouts: 1.15 us -> 1.16 us
  transfers between devices with their start and end apart: 9 -> 9, of which waited for: 2 -> 2; matrix products, arithmetic and copies ran while one was open for 0% -> 0% of each run, Pallas kernels for 22% -> 17%
where the time goes in v4:
time: 26.7 us; the launch traced here: 26.4 us
  starting transfers between devices  15.3 us (57%)
  Pallas kernels  5.93 us (22%)
  waiting for transfers between devices  3.23 us (12%)
  local copies, waits for them, and re-layouts  1.17 us (4%)
  between operations  0.79 us (3%)
    ppermute x4, starting transfers between devices, ring(): return lax.ppermute(x, axis, [(i, (i + step) % size) for i in range(size)])  7.75 us
    ppermute x4, starting transfers between devices, swap(): lax.ppermute(x, 'gx', [(i, i ^ mask) for i in range(lax.axis_size('gx'))])  3.95 us
    all_to_all x1, starting transfers between devices, shards(): lax.all_to_all(chunk, 'gx', split_axis=0, concat_axis=0, tiled=True)  3.61 us
    all_to_all x1, waiting for transfers between devices, shards(): lax.all_to_all(chunk, 'gx', split_axis=0, concat_axis=0, tiled=True)  2.37 us
    pallas_call x1, Pallas kernels, shards(): pl.pallas_call(functools.partial(spread_kernel, dims), out_shape=(jax.Sha...  2.18 us
    pallas_call x1, Pallas kernels, shards(): pl.pallas_call(functools.partial(predict_kernel, dims), out_shape=(jax.Sh...  1.49 us
    pallas_call x1, Pallas kernels, shards(): pl.pallas_call(functools.partial(owner_kernel, dims), out_shape=jax.Shape...  1.32 us
    unnamed x16, local copies, waits for them, and re-layouts  1.16 us
  transfers between devices with their start and end apart: 9, of which 2 were waited for; matrix products, arithmetic and copies ran while one was open for 0% of the time, Pallas kernels for 17%

profile of v4, /device:TPU:0, one launch (start us, length us, event | category | flops | bytes accessed | tf_op | source)
XLA Modules:
  0.0 26.4 jit_solution(379950454217793732)
XLA Ops:
  0.6 0.0 copy-start
  0.6 1.1 %copy-done = f32[3,16,16,256]{3,2,1,0:T(8,128)S(1)} copy-done((f32[3,16,16,256]{3,2,1,0:T(8,128)S(1)}, f32[3,16,16,256]{3,2,1,0:T(8,128)}, u32[]{:S(2)}) %copy-start) | copy-done | bytes 786456
  1.8 0.0 copy-start.2
  1.8 0.0 copy-start.5
  1.8 0.0 copy-start.6
  1.8 0.0 copy-start.7
  1.8 0.1 faces.1
  1.9 0.0 copy-start.1
  1.9 0.5 %collective-permute-start = (f32[3,16,256]{2,1,0:T(8,128)S(1)}, f32[3,16,256]{2,1,0:T(8,128)S(1)}, u32[]{:S(2)}, u32[]{:S(2)}) collective-permute-start(f32[3,16,256]{2,1,0:T(8,128)S(1)} %get-tuple-element.15), channel_id=1, source_target_pairs={{0,4},{4,8},{8,12},{12,16},{16,20},{20,24},{24,28},{28,0},{1,5},{5... | collective-permute-start | bytes 147464 | tf_op jit(solution)/shard_map/ppermute | solution.py:367
  2.4 2.9 %collective-permute-start.1 = (f32[3,16,256]{2,1,0:T(8,128)S(1)}, f32[3,16,256]{2,1,0:T(8,128)S(1)}, u32[]{:S(2)}, u32[]{:S(2)}) collective-permute-start(f32[3,16,256]{2,1,0:T(8,128)S(1)} %get-tuple-element.16), channel_id=1, source_target_pairs={{0,28},{4,0},{8,4},{12,8},{16,12},{20,16},{24,20},{28,24},{1,29},{... | collective-permute-start | bytes 147464 | tf_op jit(solution)/shard_map/ppermute | solution.py:367
  5.4 2.3 %collective-permute-start.2 = (f32[3,16,256]{2,1,0:T(8,128)S(1)}, f32[3,16,256]{2,1,0:T(8,128)S(1)}, u32[]{:S(2)}, u32[]{:S(2)}) collective-permute-start(f32[3,16,256]{2,1,0:T(8,128)S(1)} %get-tuple-element.17), channel_id=1, source_target_pairs={{0,1},{1,2},{2,3},{3,0},{4,5},{5,6},{6,7},{7,4},{8,9},{9,10},{10,1... | collective-permute-start | bytes 147464 | tf_op jit(solution)/shard_map/ppermute | solution.py:367
  7.6 2.0 %collective-permute-start.3 = (f32[3,16,256]{2,1,0:T(8,128)S(1)}, f32[3,16,256]{2,1,0:T(8,128)S(1)}, u32[]{:S(2)}, u32[]{:S(2)}) collective-permute-start(f32[3,16,256]{2,1,0:T(8,128)S(1)} %get-tuple-element.18), channel_id=1, source_target_pairs={{0,3},{1,0},{2,1},{3,2},{4,7},{5,4},{6,5},{7,6},{8,11},{9,8},{10,9... | collective-permute-start | bytes 147464 | tf_op jit(solution)/shard_map/ppermute | solution.py:367
  9.7 0.0 copy-done.2
  9.7 0.0 copy-done.5
  9.7 0.0 copy-done.6
  9.7 0.0 copy-done.7
  9.7 0.8 %pack.1 = (bf16[8,208,128]{2,1,0:T(8,128)(2,1)}, s32[1,3,1,8]{3,2,1,0:T(1,128)S(1)}, s32[1,3,1,8]{3,2,1,0:T(1,128)S(1)}) custom-call(bf16[8,192,128]{2,1,0:T(8,128)(2,1)S(1)} %bitcast.13, bf16[3,8,192]{2,1,0:T(8,128)(2,1)S(1)} %bitcast.15, s32[1,3,1,8]{3,2,1,0:T(1,128)S(1)} %bitcast.17, s32[1,3,1,8]{3,2,1,0:T(1,128)S(1)} %bitcast.18), custom_call_target="tpu_custom_call" | custom-call | tf_op jit(solution)/shard_map/pack/pallas_call | solution.py:355
  10.5 0.0 copy-start.4
  10.5 3.6 %all-to-all-start = ((bf16[8,208,128]{2,1,0:T(8,128)(2,1)}), bf16[8,208,128]{2,1,0:T(8,128)(2,1)S(1)}, u32[]{:S(2)}, u32[]{:S(2)}) async-start(bf16[8,208,128]{2,1,0:T(8,128)(2,1)} %get-tuple-element.22), calls=%async_computation | async-start | bytes 851968 | tf_op jit(solution)/shard_map/all_to_all | solution.py:376
  14.1 0.0 collective-permute-done.x_before
  14.2 0.0 collective-permute-done.1.x_after
  14.2 0.0 collective-permute-done.2.y_before
  14.2 0.0 collective-permute-done.3.y_after
  14.2 0.0 copy-done.1
  14.2 0.0 copy-done.4
  14.2 0.0 copy-start.3
  14.2 1.5 %predict.1 = (f32[2,784,128]{2,1,0:T(8,128)S(1)}, bf16[4,16,128]{2,1,0:T(8,128)(2,1)S(1)}, bf16[4,16,128]{2,1,0:T(8,128)(2,1)S(1)}) custom-call(s32[1,3,1,8]{3,2,1,0:T(1,128)S(1)} %get-tuple-element.14.table, f32[768,256]{1,0:T(8,128)S(1)} %bitcast.12, f32[3,16,256]{2,1,0:T(8,128)S(1)} %collective-permute-done.x_before, ...), custom_call_target="tpu_custom_call" | custom-call | tf_op jit(solution)/shard_map/predict/pallas_call | solution.py:377
  15.7 0.5 %collective-permute-start.4 = (bf16[4,16,128]{2,1,0:T(8,128)(2,1)S(1)}, bf16[4,16,128]{2,1,0:T(8,128)(2,1)S(1)}, u32[]{:S(2)}, u32[]{:S(2)}) collective-permute-start(bf16[4,16,128]{2,1,0:T(8,128)(2,1)S(1)} %get-tuple-element.21.give), channel_id=1, source_target_pairs={{0,4},{4,0},{8,12},{12,8},{16,20},{20,16},{24,28},{28,24},{1,5},{5... | collective-permute-start | bytes 49160 | tf_op jit(solution)/shard_map/ppermute | solution.py:370
  16.2 0.8 %collective-permute-done.4.first = bf16[4,16,128]{2,1,0:T(8,128)(2,1)S(1)} collective-permute-done((bf16[4,16,128]{2,1,0:T(8,128)(2,1)S(1)}, bf16[4,16,128]{2,1,0:T(8,128)(2,1)S(1)}, u32[]{:S(2)}, u32[]{:S(2)}) %collective-permute-start.4) | collective-permute-done | bytes 16416 | tf_op jit(solution)/shard_map/ppermute | solution.py:370
  17.0 1.9 %collective-permute-start.5 = (bf16[2,16,128]{2,1,0:T(8,128)(2,1)S(1)}, bf16[2,16,128]{2,1,0:T(8,128)(2,1)S(1)}, u32[]{:S(2)}, u32[]{:S(2)}) collective-permute-start(bf16[2,16,128]{2,1,0:T(8,128)(2,1)S(1)} %pad_maximum_fusion), channel_id=1, source_target_pairs={{0,8},{4,12},{8,0},{12,4},{16,24},{20,28},{24,16},{28,20},{1,9},{5... | collective-permute-start | bytes 24584 | tf_op jit(solution)/shard_map/ppermute | solution.py:370
  18.9 1.5 %collective-permute-start.6 = (bf16[2,16,128]{2,1,0:T(8,128)(2,1)S(1)}, bf16[2,16,128]{2,1,0:T(8,128)(2,1)S(1)}, u32[]{:S(2)}, u32[]{:S(2)}) collective-permute-start(bf16[2,16,128]{2,1,0:T(8,128)(2,1)S(1)} %pad_maximum_fusion.1), channel_id=1, source_target_pairs={{0,16},{4,20},{8,24},{12,28},{16,0},{20,4},{24,8},{28,12},{1,17},{... | collective-permute-start | bytes 24584 | tf_op jit(solution)/shard_map/ppermute | solution.py:370
  20.4 0.1 collective-permute-start.7
  20.5 2.4 %all-to-all-done.blocks = bf16[8,208,128]{2,1,0:T(8,128)(2,1)S(1)} async-done(((bf16[8,208,128]{2,1,0:T(8,128)(2,1)}), bf16[8,208,128]{2,1,0:T(8,128)(2,1)S(1)}, u32[]{:S(2)}, u32[]{:S(2)}) %all-to-all-start) | async-done | bytes 426016 | tf_op jit(solution)/shard_map/all_to_all | solution.py:376
  22.9 0.0 copy-done.3
  22.9 2.2 %spread.1 = (f32[768,256]{1,0:T(8,128)}, f32[8,128]{1,0:T(8,128)S(1)}) custom-call(s32[1,3,1,8]{3,2,1,0:T(1,128)S(1)} %get-tuple-element.14.table, f32[2,784,128]{2,1,0:T(8,128)S(1)} %get-tuple-element.19.before, bf16[4,16,128]{2,1,0:T(8,128)(2,1)S(1)} %get-tuple-element.20.keep, bf16[4,16,128]{2,1,0:T(8,128)(2,1)S(1)} %get-tuple-element.21.give, ...), custom_call_target="tpu_custom_call" | custom-call | flops 100000000 | bytes 4000000 | tf_op jit(solution)/shard_map/spread/pallas_call | solution.py:388
  25.1 0.0 collective-permute-done.5.rest_0_
  25.1 0.0 collective-permute-done.6.rest_1_
  25.1 0.0 collective-permute-done.7.rest_2_
  25.1 1.3 %owner.1 = f32[3,8,192]{2,1,0:T(8,128)} custom-call(s32[1,3,1,8]{3,2,1,0:T(1,128)S(1)} %get-tuple-element.24.table, f32[8,128]{1,0:T(8,128)S(1)} %get-tuple-element.25.token, bf16[3,8,192]{2,1,0:T(8,128)(2,1)S(1)} %bitcast.16, bf16[8,192,128]{2,1,0:T(8,128)(2,1)S(1)} %bitcast.14, bf16[4,16,128]{2,1,0:T(8,128)(2,1)S(1)} %get-tuple-element.20.keep, ...), custom_call_target="tpu_custom_call" | custom-call | tf_op jit(solution)/shard_map/owner/pallas_call | solution.py:404
  (5 shorter events, 0.0 us)
Async XLA Ops:
  0.6 1.1 %copy-start = (f32[3,16,16,256]{3,2,1,0:T(8,128)S(1)}, f32[3,16,16,256]{3,2,1,0:T(8,128)}, u32[]{:S(2)}) copy-start(f32[3,16,16,256]{3,2,1,0:T(8,128)} %param.7) | copy-start | bytes 2359300
  1.8 7.9 %copy-start.2 = (bf16[1,1,8,3,64,128]{5,4,3,2,1,0:T(8,128)(2,1)S(1)}, bf16[1,1,8,3,64,128]{5,4,3,2,1,0:T(8,128)(2,1)}, u32[]{:S(2)}) copy-start(bf16[1,1,8,3,64,128]{5,4,3,2,1,0:T(8,128)(2,1)} %param.8) | copy-start | bytes 1179652
  1.8 7.9 %copy-start.5 = (bf16[1,1,8,3,192]{4,2,3,1,0:T(8,128)(2,1)S(1)}, bf16[1,1,8,3,192]{4,2,3,1,0:T(8,128)(2,1)}, u32[]{:S(2)}) copy-start(bf16[1,1,8,3,192]{4,2,3,1,0:T(8,128)(2,1)} %param.9) | copy-start | bytes 27652
  1.8 7.9 %copy-start.6 = (s32[1,1,8,3]{2,1,3,0:T(1,128)S(1)}, s32[1,1,8,3]{2,1,3,0:T(1,128)}, u32[]{:S(2)}) copy-start(s32[1,1,8,3]{2,1,3,0:T(1,128)} %param.11) | copy-start | bytes 292
  1.8 7.9 %copy-start.7 = (s32[1,1,8,3]{2,1,3,0:T(1,128)S(1)}, s32[1,1,8,3]{2,1,3,0:T(1,128)}, u32[]{:S(2)}) copy-start(s32[1,1,8,3]{2,1,3,0:T(1,128)} %param.10) | copy-start | bytes 292
  1.9 12.3 %copy-start.1 = (f32[3,16,16,256]{3,2,1,0:T(8,128)S(1)}, f32[3,16,16,256]{3,2,1,0:T(8,128)}, u32[]{:S(2)}) copy-start(f32[3,16,16,256]{3,2,1,0:T(8,128)} %param.7) | copy-start | bytes 2359300
  1.9 12.2 %collective-permute-start = (f32[3,16,256]{2,1,0:T(8,128)S(1)}, f32[3,16,256]{2,1,0:T(8,128)S(1)}, u32[]{:S(2)}, u32[]{:S(2)}) collective-permute-start(f32[3,16,256]{2,1,0:T(8,128)S(1)} %get-tuple-element.15), channel_id=1, source_target_pairs={{0,4},{4,8},{8,12},{12,16},{16,20},{20,24},{24,28},{28,0},{1,5},{5... | collective-permute-start | bytes 147464 | tf_op jit(solution)/shard_map/ppermute | solution.py:367
  2.4 11.7 %collective-permute-start.1 = (f32[3,16,256]{2,1,0:T(8,128)S(1)}, f32[3,16,256]{2,1,0:T(8,128)S(1)}, u32[]{:S(2)}, u32[]{:S(2)}) collective-permute-start(f32[3,16,256]{2,1,0:T(8,128)S(1)} %get-tuple-element.16), channel_id=1, source_target_pairs={{0,28},{4,0},{8,4},{12,8},{16,12},{20,16},{24,20},{28,24},{1,29},{... | collective-permute-start | bytes 147464 | tf_op jit(solution)/shard_map/ppermute | solution.py:367
  5.4 8.8 %collective-permute-start.2 = (f32[3,16,256]{2,1,0:T(8,128)S(1)}, f32[3,16,256]{2,1,0:T(8,128)S(1)}, u32[]{:S(2)}, u32[]{:S(2)}) collective-permute-start(f32[3,16,256]{2,1,0:T(8,128)S(1)} %get-tuple-element.17), channel_id=1, source_target_pairs={{0,1},{1,2},{2,3},{3,0},{4,5},{5,6},{6,7},{7,4},{8,9},{9,10},{10,1... | collective-permute-start | bytes 147464 | tf_op jit(solution)/shard_map/ppermute | solution.py:367
  7.6 6.5 %collective-permute-start.3 = (f32[3,16,256]{2,1,0:T(8,128)S(1)}, f32[3,16,256]{2,1,0:T(8,128)S(1)}, u32[]{:S(2)}, u32[]{:S(2)}) collective-permute-start(f32[3,16,256]{2,1,0:T(8,128)S(1)} %get-tuple-element.18), channel_id=1, source_target_pairs={{0,3},{1,0},{2,1},{3,2},{4,7},{5,4},{6,5},{7,6},{8,11},{9,8},{10,9... | collective-permute-start | bytes 147464 | tf_op jit(solution)/shard_map/ppermute | solution.py:367
  10.5 3.7 %copy-start.4 = (bf16[1024,128]{1,0:T(8,128)(2,1)S(1)}, bf16[1024,128]{1,0:T(8,128)(2,1)}, u32[]{:S(2)}) copy-start(bf16[1024,128]{1,0:T(8,128)(2,1)} %constant.4.clone.gathers) | copy-start | bytes 786436
  10.5 12.4 %all-to-all-start = ((bf16[8,208,128]{2,1,0:T(8,128)(2,1)}), bf16[8,208,128]{2,1,0:T(8,128)(2,1)S(1)}, u32[]{:S(2)}, u32[]{:S(2)}) async-start(bf16[8,208,128]{2,1,0:T(8,128)(2,1)} %get-tuple-element.22), calls=%async_computation | async-start | bytes 851968 | tf_op jit(solution)/shard_map/all_to_all | solution.py:376
  14.2 8.7 %copy-start.3 = (bf16[128,1024]{1,0:T(8,128)(2,1)S(1)}, bf16[128,1024]{1,0:T(8,128)(2,1)}, u32[]{:S(2)}) copy-start(bf16[128,1024]{1,0:T(8,128)(2,1)} %constant.5.clone.scatters) | copy-start | bytes 786436
  15.7 1.3 %collective-permute-start.4 = (bf16[4,16,128]{2,1,0:T(8,128)(2,1)S(1)}, bf16[4,16,128]{2,1,0:T(8,128)(2,1)S(1)}, u32[]{:S(2)}, u32[]{:S(2)}) collective-permute-start(bf16[4,16,128]{2,1,0:T(8,128)(2,1)S(1)} %get-tuple-element.21.give), channel_id=1, source_target_pairs={{0,4},{4,0},{8,12},{12,8},{16,20},{20,16},{24,28},{28,24},{1,5},{5... | collective-permute-start | bytes 49160 | tf_op jit(solution)/shard_map/ppermute | solution.py:370
  17.0 8.1 %collective-permute-start.5 = (bf16[2,16,128]{2,1,0:T(8,128)(2,1)S(1)}, bf16[2,16,128]{2,1,0:T(8,128)(2,1)S(1)}, u32[]{:S(2)}, u32[]{:S(2)}) collective-permute-start(bf16[2,16,128]{2,1,0:T(8,128)(2,1)S(1)} %pad_maximum_fusion), channel_id=1, source_target_pairs={{0,8},{4,12},{8,0},{12,4},{16,24},{20,28},{24,16},{28,20},{1,9},{5... | collective-permute-start | bytes 24584 | tf_op jit(solution)/shard_map/ppermute | solution.py:370
  18.9 6.2 %collective-permute-start.6 = (bf16[2,16,128]{2,1,0:T(8,128)(2,1)S(1)}, bf16[2,16,128]{2,1,0:T(8,128)(2,1)S(1)}, u32[]{:S(2)}, u32[]{:S(2)}) collective-permute-start(bf16[2,16,128]{2,1,0:T(8,128)(2,1)S(1)} %pad_maximum_fusion.1), channel_id=1, source_target_pairs={{0,16},{4,20},{8,24},{12,28},{16,0},{20,4},{24,8},{28,12},{1,17},{... | collective-permute-start | bytes 24584 | tf_op jit(solution)/shard_map/ppermute | solution.py:370
  20.4 4.7 %collective-permute-start.7 = (bf16[2,16,128]{2,1,0:T(8,128)(2,1)S(1)}, bf16[2,16,128]{2,1,0:T(8,128)(2,1)S(1)}, u32[]{:S(2)}, u32[]{:S(2)}) collective-permute-start(bf16[2,16,128]{2,1,0:T(8,128)(2,1)S(1)} %pad_maximum_fusion.2), channel_id=1, source_target_pairs={{0,24},{4,28},{8,16},{12,20},{16,8},{20,12},{24,0},{28,4},{1,25},{... | collective-permute-start | bytes 24584 | tf_op jit(solution)/shard_map/ppermute | solution.py:370

commit v5 on v4

--- a/solution.py
+++ b/solution.py
@@ -31,7 +31,7 @@
         lax.fori_loop(0, count, step, 0)
 
 
-def faces_kernel(dims, vel, x_first, x_last, y_first, y_last, held, sems):
+def faces_kernel(dims, vel, y_first, y_last, held, sems):
     size_x, size_y = dims
     halves = held.shape[0]
     moves = [
@@ -45,17 +45,15 @@
         moves[part].wait()
         lanes = pl.ds(part * 128, 128)
         for c in range(3):
-            x_first[c, :, lanes] = held[part, pl.ds(c * plane, size_y), :]
-            x_last[c, :, lanes] = held[part, pl.ds(c * plane + plane - size_y, size_y), :]
             y_first[c, :, lanes] = held[part, pl.ds(c * plane, size_x, stride=size_y), :]
             y_last[c, :, lanes] = held[part, pl.ds(c * plane + size_y - 1, size_x, stride=size_y), :]
 
 
-def pack_kernel(dims, w, t, slots, own, chunk, slots_out, own_out, rows, sem):
+def pack_kernel(dims, w, t, slots, own, chunk, slots_out, own_out, rows, packed, sems):
     slots_out[...] = slots[...]
     own_out[...] = own[...]
     count_d, width = dims
-    move_w = pltpu.make_async_copy(w, chunk.at[:, pl.ds(0, width), :], sem)
+    move_w = pltpu.make_async_copy(w, chunk.at[:, pl.ds(0, width), :], sems.at[0])
     move_w.start()
     rows[...] = jnp.zeros_like(rows)
     rest = jnp.zeros((count_d, 256 - width), F32)
@@ -63,7 +61,10 @@
         values = t[c].astype(F32)
         rows[pl.ds(c, count_d, stride=16), :] = values[:, 0:128]
         rows[pl.ds(8 + c, count_d, stride=16), :] = jnp.concatenate([values[:, 128:width], rest], axis=1)
-    chunk[:, width : width + 16, :] = rows[...].astype(BF16).reshape(count_d, 16, 128)
+    packed[...] = rows[...].astype(BF16).reshape(count_d, 16, 128)
+    move_t = pltpu.make_async_copy(packed, chunk.at[:, pl.ds(width, 16), :], sems.at[1])
+    move_t.start()
+    move_t.wait()
     move_w.wait()
 
 
@@ -124,25 +125,19 @@
     col = lax.broadcasted_iota(jnp.int32, (size_y, size_z), 1)
 
     def stencil(x):
-        center, fore, back, right, left, top, bottom = [], [], [], [], [], [], []
+        center = [vel[pl.ds((c * size_x + x) * size_y, size_y), :] for c in range(3)]
         for c in range(3):
             base = (c * size_x + x) * size_y
-            here = vel[pl.ds(base, size_y), :]
-            center.append(here)
-            fore.append(x_after[c] if x == size_x - 1 else vel[pl.ds(base + size_y, size_y), :])
-            back.append(x_before[c] if x == 0 else vel[pl.ds(base - size_y, size_y), :])
-            right.append(
-                jnp.where(row == size_y - 1, y_after[c, pl.ds(x, 1), :], pltpu.roll(here, size_y - 1, 0))
-            )
-            left.append(jnp.where(row == 0, y_before[c, pl.ds(x, 1), :], pltpu.roll(here, 1, 0)))
-            top.append(jnp.where(col == size_z - 1, 0.0, pltpu.roll(here, size_z - 1, 1)))
-            bottom.append(jnp.where(col == 0, 0.0, pltpu.roll(here, 1, 1)))
-        for c in range(3):
-            total = (
-                (fore[c] + back[c]) - center[0] * (fore[c] - back[c])
-                + (right[c] + left[c]) - center[1] * (right[c] - left[c])
-                + (top[c] + bottom[c]) - center[2] * (top[c] - bottom[c])
-            )
+            here = center[c]
+            fore = x_after[c] if x == size_x - 1 else vel[pl.ds(base + size_y, size_y), :]
+            back = x_before[c] if x == 0 else vel[pl.ds(base - size_y, size_y), :]
+            total = (fore + back) - center[0] * (fore - back)
+            right = jnp.where(row == size_y - 1, y_after[c, pl.ds(x, 1), :], pltpu.roll(here, size_y - 1, 0))
+            left = jnp.where(row == 0, y_before[c, pl.ds(x, 1), :], pltpu.roll(here, 1, 0))
+            total = total + ((right + left) - center[1] * (right - left))
+            top = jnp.where(col == size_z - 1, 0.0, pltpu.roll(here, size_z - 1, 1))
+            bottom = jnp.where(col == 0, 0.0, pltpu.roll(here, 1, 1))
+            total = total + ((top + bottom) - center[2] * (top - bottom))
             base = 8 + (c * size_x + x) * size_y
             result = (1.0 - 6.0 * time_step * viscosity) * center[c] + (0.5 * time_step) * total
             for part in range(halves):
@@ -178,7 +173,8 @@
 
 
 def spread_kernel(
-    dims, table, before, keep, give, blocks, scatters, out, token, field, stage, chosen, slots, sems,
+    dims, table, own_table, before, keep, give, blocks, scatters, out, live_out, field, stage, chosen,
+    slots, own, sems,
 ):
     size_x, size_y, size_z, count_d, count_s, width = dims
     cells = 3 * size_x * size_y
@@ -186,9 +182,10 @@
     me = lax.axis_index("gx")
     move_field = pltpu.make_async_copy(before, field, sems.at[0])
     move_slots = pltpu.make_async_copy(table, slots, sems.at[1])
+    move_own = pltpu.make_async_copy(own_table, own, sems.at[2])
     move_slots.start()
+    move_own.start()
     move_field.start()
-    token[...] = jnp.zeros_like(token)
     low_lane, low_sub = low_halves()
     group = 8 if count_d % 8 == 0 else count_d
     high = keep.shape[1]
@@ -233,6 +230,16 @@
                 for (k, at), total in zip(spots, sums):
                     field[k, at, :] = total
 
+    row = lax.broadcasted_iota(jnp.int32, (group, width), 0)
+    column_slot = lax.broadcasted_iota(jnp.int32, (group, width), 1) // (width // count_s)
+
+    def mark_live(k):
+        live = jnp.full((group, width), -1, jnp.int32)
+        for g in range(group):
+            for s in range(count_s):
+                live = jnp.where((row == g) & (column_slot == s), own[0, s, 0, k * group + g], live)
+        live_out[pl.ds(k * group, group), :] = live
+
     def batch(k):
         owners = [me ^ (k * group + g) for g in range(group)]
         products = [
@@ -241,11 +248,13 @@
         ]
         if count_d == group:
             move_slots.wait()
+            move_own.wait()
         forces = [force(owners[g], products[g]) for g in range(group)]
         for g in range(group):
             chosen[pl.ds(g * high, high), :] = jnp.dot(
                 forces[g], blocks[owners[g], 0:width, :], preferred_element_type=F32
             )
+        mark_live(k)
         rows = chosen[...] * (time_step * spread_gain)
         upper = rows.astype(BF16)
         lower = (rows - upper.astype(F32)).astype(BF16)
@@ -260,11 +269,12 @@
 
     if count_d != group:
         move_slots.wait()
+        move_own.wait()
         move_field.wait()
     each(count_d // group, batch)
     moves = [
         pltpu.make_async_copy(
-            field.at[part, pl.ds(8, cells), :], out.at[:, pl.ds(part * 128, 128)], sems.at[2 + part]
+            field.at[part, pl.ds(8, cells), :], out.at[:, pl.ds(part * 128, 128)], sems.at[3 + part]
         )
         for part in range(halves)
     ]
@@ -274,23 +284,18 @@
         move.wait()
 
 
-def owner_kernel(dims, table, token, targets, block_w, keep, first, *rest):
+def owner_kernel(dims, live, targets, block_w, keep, first, *rest):
     size_x, size_y, size_z, count_d, count_s, width = dims
-    received, (out, picked, slots, sem) = rest[:-4], rest[-4:]
+    received, (out, picked) = rest[:-2], rest[-2:]
     me = lax.axis_index("gx")
-    move = pltpu.make_async_copy(table, slots, sem)
-    move.start()
     group = 8 if count_d % 8 == 0 else count_d
     slot_of = lax.broadcasted_iota(jnp.int32, (8, width), 1) // (width // count_s)
     row = lax.broadcasted_iota(jnp.int32, (group, width), 0)
-    column_slot = lax.broadcasted_iota(jnp.int32, (group, width), 1) // (width // count_s)
     picked[0] = keep[0]
     picked[1] = first[0]
     for k, pair in enumerate(received):
         picked[2 * k + 2] = pair[0]
         picked[2 * k + 3] = pair[1]
-    if count_d != group:
-        move.wait()
 
     def batch(k):
         products = [
@@ -300,20 +305,15 @@
             )
             for g in range(group)
         ]
-        if count_d == group:
-            move.wait()
         interp = [jnp.zeros((group, width), F32) for c in range(3)]
-        live = jnp.full((group, width), -1, jnp.int32)
         for g in range(group):
             lines = select_slots(products[g], slot_of, count_s)
             for c in range(3):
                 interp[c] = jnp.where(row == g, lines[c : c + 1], interp[c])
-            for s in range(count_s):
-                live = jnp.where((row == g) & (column_slot == s), slots[0, s, 0, k * group + g], live)
         for c in range(3):
             at = pl.ds(k * group, group)
             target = targets[c, at, :].astype(F32)
-            out[c, at, :] = jnp.where(live >= 0, (target - interp[c]) / time_step, 0.0)
+            out[c, at, :] = jnp.where(live[at, :] >= 0, (target - interp[c]) / time_step, 0.0)
 
     each(count_d // group, batch)
 
@@ -333,18 +333,18 @@
     high = -(-count_s * 4 // 16) * 16
     anywhere = pl.BlockSpec(memory_space=pl.ANY)
     inside = pl.BlockSpec(memory_space=VMEM)
-    face_x = jax.ShapeDtypeStruct((3, size_y, size_z), F32)
     face_y = jax.ShapeDtypeStruct((3, size_x, size_z), F32)
     half = jax.ShapeDtypeStruct((count_d // 2, high, 128), BF16)
     padded = (size_z // 128, cells + 16, 128)
     params = pltpu.CompilerParams(vmem_limit_bytes=24 * 2**20)
     table = jax.ShapeDtypeStruct(slots.shape, jnp.int32)
     staged = (pltpu.SMEM(slots.shape, jnp.int32), pltpu.SemaphoreType.DMA)
-    x_first, x_last, y_first, y_last = pl.pallas_call(
+    x_first, x_last = velocity[:, 0], velocity[:, size_x - 1]
+    y_first, y_last = pl.pallas_call(
         functools.partial(faces_kernel, (size_x, size_y)),
-        out_shape=(face_x, face_x, face_y, face_y),
+        out_shape=(face_y, face_y),
         in_specs=[anywhere],
-        out_specs=(inside,) * 4,
+        out_specs=(inside,) * 2,
         scratch_shapes=[
             VMEM((size_z // 128, cells, 128), F32),
             pltpu.SemaphoreType.DMA((size_z // 128,)),
@@ -355,9 +355,13 @@
     chunk, slots, own = pl.pallas_call(
         functools.partial(pack_kernel, (count_d, width)),
         out_shape=(jax.ShapeDtypeStruct((count_d, width + 16, 128), BF16), table, table),
-        in_specs=[anywhere, inside, inside, inside],
-        out_specs=(inside,) * 3,
-        scratch_shapes=[VMEM((count_d * 16, 128), F32), pltpu.SemaphoreType.DMA],
+        in_specs=[inside, inside, inside, inside],
+        out_specs=(anywhere, inside, inside),
+        scratch_shapes=[
+            VMEM((count_d * 16, 128), F32),
+            VMEM((count_d, 16, 128), BF16),
+            pltpu.SemaphoreType.DMA((2,)),
+        ],
         compiler_params=params,
         name="pack",
     )(block_w, wanted, slots, own)
@@ -385,31 +389,32 @@
     )(slots, vel, x_before, x_after, y_before, y_after, jnp.asarray(shifts()))
     first = swap(give, 1)
     received = [swap(jnp.stack([keep[k], first[k]]), 2 * k) for k in range(1, count_d // 2)]
-    out, token = pl.pallas_call(
+    out, live = pl.pallas_call(
         functools.partial(spread_kernel, dims),
-        out_shape=(jax.ShapeDtypeStruct((cells, size_z), F32), jax.ShapeDtypeStruct((8, 128), F32)),
-        in_specs=[inside] * 6,
+        out_shape=(jax.ShapeDtypeStruct((cells, size_z), F32), jax.ShapeDtypeStruct((count_d, width), jnp.int32)),
+        in_specs=[inside] * 7,
         out_specs=(anywhere, inside),
         scratch_shapes=[
             VMEM(padded, F32),
             VMEM((group * high * 8, 128), F32),
             VMEM((group * high, 128), F32),
             staged[0],
-            pltpu.SemaphoreType.DMA((2 + size_z // 128,)),
+            staged[0],
+            pltpu.SemaphoreType.DMA((3 + size_z // 128,)),
         ],
         compiler_params=params,
         cost_estimate=pl.CostEstimate(flops=10**8, bytes_accessed=4 * 10**6, transcendentals=0),
         name="spread",
-    )(slots, field, keep, give, arrived, jnp.asarray(shifts().T))
+    )(slots, own, field, keep, give, arrived, jnp.asarray(shifts().T))
     force = pl.pallas_call(
         functools.partial(owner_kernel, dims),
         out_shape=jax.ShapeDtypeStruct((3, count_d, width), F32),
-        in_specs=[inside] * (5 + count_d // 2),
+        in_specs=[inside] * (4 + count_d // 2),
         out_specs=inside,
-        scratch_shapes=[VMEM((count_d, high, 128), BF16), *staged],
+        scratch_shapes=[VMEM((count_d, high, 128), BF16)],
         compiler_params=params,
         name="owner",
-    )(own, token, wanted, block_w, keep, first, *received)
+    )(live, wanted, block_w, keep, first, *received)
     return out.reshape(velocity.shape), jnp.transpose(force, (1, 0, 2))[None, None]
 
 

time: 26.7 us -> 25.9 us (0.970)
  starting transfers between devices: 15.3 us -> 14.9 us
  Pallas kernels: 5.93 us -> 5.54 us
    ppermute x4, starting transfers between devices: 7.75 us -> 6.82 us  [ring(): return lax.ppermute(x, axis, [(i, (i + step) % size) for i in range(size)])]
    all_to_all x1, starting transfers between devices: 3.61 us -> 4.05 us  [shards(): lax.all_to_all(chunk, 'gx', split_axis=0, concat_axis=0, tiled=True)]
    pallas_call x1, Pallas kernels: 1.32 us -> 0.94 us  [shards(): pl.pallas_call(functools.partial(owner_kernel, dims), out_shape=jax.Shape...]
  transfers between devices with their start and end apart: 9 -> 9, of which waited for: 2 -> 2; matrix products, arithmetic and copies ran while one was open for 0% -> 0% of each run, Pallas kernels for 17% -> 18%
where the time goes in v5:
time: 25.9 us; the launch traced here: 25.6 us
  starting transfers between devices  14.9 us (58%)
  Pallas kernels  5.54 us (21%)
  waiting for transfers between devices  3.19 us (12%)
  local copies, waits for them, and re-layouts  1.17 us (5%)
  between operations  0.79 us (3%)
    ppermute x4, starting transfers between devices, ring(): return lax.ppermute(x, axis, [(i, (i + step) % size) for i in range(size)])  6.82 us
    ppermute x4, starting transfers between devices, swap(): lax.ppermute(x, 'gx', [(i, i ^ mask) for i in range(lax.axis_size('gx'))])  4.05 us
    all_to_all x1, starting transfers between devices, shards(): lax.all_to_all(chunk, 'gx', split_axis=0, concat_axis=0, tiled=True)  4.05 us
    all_to_all x1, waiting for transfers between devices, shards(): lax.all_to_all(chunk, 'gx', split_axis=0, concat_axis=0, tiled=True)  2.34 us
    pallas_call x1, Pallas kernels, shards(): pl.pallas_call(functools.partial(spread_kernel, dims), out_shape=(jax.Sha...  2.23 us
    pallas_call x1, Pallas kernels, shards(): pl.pallas_call(functools.partial(predict_kernel, dims), out_shape=(jax.Sh...  1.49 us
    unnamed x16, local copies, waits for them, and re-layouts  1.16 us
    pallas_call x1, Pallas kernels, shards(): pl.pallas_call(functools.partial(owner_kernel, dims), out_shape=jax.Shape...  0.94 us
  transfers between devices with their start and end apart: 9, of which 2 were waited for; matrix products, arithmetic and copies ran while one was open for 0% of the time, Pallas kernels for 18%

profile of v5, /device:TPU:0, one launch (start us, length us, event | category | flops | bytes accessed | tf_op | source)
XLA Modules:
  0.0 25.6 jit_solution(13523294925458874457)
XLA Ops:
  0.6 0.0 copy-start
  0.6 1.1 %copy-done = f32[3,16,16,256]{3,2,1,0:T(8,128)S(1)} copy-done((f32[3,16,16,256]{3,2,1,0:T(8,128)S(1)}, f32[3,16,16,256]{3,2,1,0:T(8,128)}, u32[]{:S(2)}) %copy-start) | copy-done | bytes 786456
  1.8 0.0 copy-start.2
  1.8 0.0 copy-start.5
  1.8 0.0 copy-start.6
  1.8 0.0 copy-start.7
  1.8 0.1 faces.1
  1.9 0.0 copy-start.1
  1.9 3.1 %collective-permute-start.2 = (f32[3,16,256]{2,1,0:T(8,128)S(1)}, f32[3,16,256]{2,1,0:T(8,128)S(1)}, u32[]{:S(2)}, u32[]{:S(2)}) collective-permute-start(f32[3,16,256]{2,1,0:T(8,128)S(1)} %get-tuple-element.14), channel_id=1, source_target_pairs={{0,1},{1,2},{2,3},{3,0},{4,5},{5,6},{6,7},{7,4},{8,9},{9,10},{10,1... | collective-permute-start | bytes 147464 | tf_op jit(solution)/shard_map/ppermute | solution.py:371
  5.0 2.1 %collective-permute-start.3 = (f32[3,16,256]{2,1,0:T(8,128)S(1)}, f32[3,16,256]{2,1,0:T(8,128)S(1)}, u32[]{:S(2)}, u32[]{:S(2)}) collective-permute-start(f32[3,16,256]{2,1,0:T(8,128)S(1)} %get-tuple-element.15), channel_id=1, source_target_pairs={{0,3},{1,0},{2,1},{3,2},{4,7},{5,4},{6,5},{7,6},{8,11},{9,8},{10,9... | collective-permute-start | bytes 147464 | tf_op jit(solution)/shard_map/ppermute | solution.py:371
  7.1 1.7 %collective-permute-start.1 = (f32[3,16,256]{2,1,0:T(8,128)S(1)}, f32[3,16,256]{2,1,0:T(8,128)S(1)}, u32[]{:S(2)}, u32[]{:S(2)}) collective-permute-start(f32[3,16,256]{2,1,0:T(8,128)S(1)} %get-tuple-element.22), channel_id=1, source_target_pairs={{0,28},{4,0},{8,4},{12,8},{16,12},{20,16},{24,20},{28,24},{1,29},{... | collective-permute-start | bytes 147464 | tf_op jit(solution)/shard_map/ppermute | solution.py:371
  8.7 0.0 collective-permute-start
  8.7 0.0 copy-done.2
  8.7 0.0 copy-done.5
  8.8 0.0 copy-done.6
  8.8 0.0 copy-done.7
  8.8 0.8 %pack.1 = (bf16[8,208,128]{2,1,0:T(8,128)(2,1)}, s32[1,3,1,8]{3,2,1,0:T(1,128)S(1)}, s32[1,3,1,8]{3,2,1,0:T(1,128)S(1)}) custom-call(bf16[8,192,128]{2,1,0:T(8,128)(2,1)S(1)} %bitcast.21, bf16[3,8,192]{2,1,0:T(8,128)(2,1)S(1)} %bitcast.23, s32[1,3,1,8]{3,2,1,0:T(1,128)S(1)} %bitcast.25, s32[1,3,1,8]{3,2,1,0:T(1,128)S(1)} %bitcast.26), custom_call_target="tpu_custom_call" | custom-call | tf_op jit(solution)/shard_map/pack/pallas_call | solution.py:355
  9.6 0.0 copy-start.4
  9.6 4.0 %all-to-all-start = ((bf16[8,208,128]{2,1,0:T(8,128)(2,1)}), bf16[8,208,128]{2,1,0:T(8,128)(2,1)S(1)}, u32[]{:S(2)}, u32[]{:S(2)}) async-start(bf16[8,208,128]{2,1,0:T(8,128)(2,1)} %get-tuple-element.19), calls=%async_computation | async-start | bytes 851968 | tf_op jit(solution)/shard_map/all_to_all | solution.py:380
  13.6 0.0 collective-permute-done.2.y_before
  13.6 0.0 collective-permute-done.3.y_after
  13.6 0.0 collective-permute-done.1.x_after
  13.6 0.0 collective-permute-done.x_before
  13.6 0.0 copy-done.1
  13.7 0.0 copy-done.4
  13.7 0.0 copy-start.3
  13.7 1.5 %predict.1 = (f32[2,784,128]{2,1,0:T(8,128)S(1)}, bf16[4,16,128]{2,1,0:T(8,128)(2,1)S(1)}, bf16[4,16,128]{2,1,0:T(8,128)(2,1)S(1)}) custom-call(s32[1,3,1,8]{3,2,1,0:T(1,128)S(1)} %get-tuple-element.12.table, f32[768,256]{1,0:T(8,128)S(1)} %bitcast.20, f32[3,16,256]{2,1,0:T(8,128)S(1)} %collective-permute-done.x_before, ...), custom_call_target="tpu_custom_call" | custom-call | tf_op jit(solution)/shard_map/predict/pallas_call | solution.py:381
  15.2 0.6 %collective-permute-start.4 = (bf16[4,16,128]{2,1,0:T(8,128)(2,1)S(1)}, bf16[4,16,128]{2,1,0:T(8,128)(2,1)S(1)}, u32[]{:S(2)}, u32[]{:S(2)}) collective-permute-start(bf16[4,16,128]{2,1,0:T(8,128)(2,1)S(1)} %get-tuple-element.18.give), channel_id=1, source_target_pairs={{0,4},{4,0},{8,12},{12,8},{16,20},{20,16},{24,28},{28,24},{1,5},{5... | collective-permute-start | bytes 49160 | tf_op jit(solution)/shard_map/ppermute | solution.py:374
  15.7 0.8 %collective-permute-done.4.first = bf16[4,16,128]{2,1,0:T(8,128)(2,1)S(1)} collective-permute-done((bf16[4,16,128]{2,1,0:T(8,128)(2,1)S(1)}, bf16[4,16,128]{2,1,0:T(8,128)(2,1)S(1)}, u32[]{:S(2)}, u32[]{:S(2)}) %collective-permute-start.4) | collective-permute-done | bytes 16416 | tf_op jit(solution)/shard_map/ppermute | solution.py:374
  16.6 1.9 %collective-permute-start.5 = (bf16[2,16,128]{2,1,0:T(8,128)(2,1)S(1)}, bf16[2,16,128]{2,1,0:T(8,128)(2,1)S(1)}, u32[]{:S(2)}, u32[]{:S(2)}) collective-permute-start(bf16[2,16,128]{2,1,0:T(8,128)(2,1)S(1)} %pad_maximum_fusion), channel_id=1, source_target_pairs={{0,8},{4,12},{8,0},{12,4},{16,24},{20,28},{24,16},{28,20},{1,9},{5... | collective-permute-start | bytes 24584 | tf_op jit(solution)/shard_map/ppermute | solution.py:374
  18.5 1.5 %collective-permute-start.6 = (bf16[2,16,128]{2,1,0:T(8,128)(2,1)S(1)}, bf16[2,16,128]{2,1,0:T(8,128)(2,1)S(1)}, u32[]{:S(2)}, u32[]{:S(2)}) collective-permute-start(bf16[2,16,128]{2,1,0:T(8,128)(2,1)S(1)} %pad_maximum_fusion.1), channel_id=1, source_target_pairs={{0,16},{4,20},{8,24},{12,28},{16,0},{20,4},{24,8},{28,12},{1,17},{... | collective-permute-start | bytes 24584 | tf_op jit(solution)/shard_map/ppermute | solution.py:374
  19.9 0.2 collective-permute-start.7
  20.1 2.3 %all-to-all-done.blocks = bf16[8,208,128]{2,1,0:T(8,128)(2,1)S(1)} async-done(((bf16[8,208,128]{2,1,0:T(8,128)(2,1)}), bf16[8,208,128]{2,1,0:T(8,128)(2,1)S(1)}, u32[]{:S(2)}, u32[]{:S(2)}) %all-to-all-start) | async-done | bytes 426016 | tf_op jit(solution)/shard_map/all_to_all | solution.py:380
  22.4 0.0 copy-done.3
  22.4 2.2 %spread.1 = (f32[768,256]{1,0:T(8,128)}, s32[8,192]{1,0:T(8,128)S(1)}) custom-call(s32[1,3,1,8]{3,2,1,0:T(1,128)S(1)} %get-tuple-element.12.table, s32[1,3,1,8]{3,2,1,0:T(1,128)S(1)} %get-tuple-element.13.own_table, f32[2,784,128]{2,1,0:T(8,128)S(1)} %get-tuple-element.16.before, bf16[4,16,128]{2,1,0:T(8,128)(2,1)S(1)} %get-tuple-element.17.keep, ...), custom_call_target="tpu_custom_call" | custom-call | flops 100000000 | bytes 4000000 | tf_op jit(solution)/shard_map/spread/pallas_call | solution.py:392
  24.7 0.0 collective-permute-done.5.rest_0_
  24.7 0.0 collective-permute-done.6.rest_1_
  24.7 0.0 collective-permute-done.7.rest_2_
  24.7 0.9 %owner.1 = f32[3,8,192]{2,1,0:T(8,128)} custom-call(s32[8,192]{1,0:T(8,128)S(1)} %get-tuple-element.21.live, bf16[3,8,192]{2,1,0:T(8,128)(2,1)S(1)} %bitcast.24, bf16[8,192,128]{2,1,0:T(8,128)(2,1)S(1)} %bitcast.22, bf16[4,16,128]{2,1,0:T(8,128)(2,1)S(1)} %get-tuple-element.17.keep, bf16[4,16,128]{2,1,0:T(8,128)(2,1)S(1)} %collective-permute-done.4.first, ...), custom_call_target="tpu_custom_call" | custom-call | tf_op jit(solution)/shard_map/owner/pallas_call | solution.py:409
  (6 shorter events, 0.0 us)
Async XLA Ops:
  0.6 1.1 %copy-start = (f32[3,16,16,256]{3,2,1,0:T(8,128)S(1)}, f32[3,16,16,256]{3,2,1,0:T(8,128)}, u32[]{:S(2)}) copy-start(f32[3,16,16,256]{3,2,1,0:T(8,128)} %param.7) | copy-start | bytes 2359300
  1.8 7.0 %copy-start.2 = (bf16[1,1,8,3,64,128]{5,4,3,2,1,0:T(8,128)(2,1)S(1)}, bf16[1,1,8,3,64,128]{5,4,3,2,1,0:T(8,128)(2,1)}, u32[]{:S(2)}) copy-start(bf16[1,1,8,3,64,128]{5,4,3,2,1,0:T(8,128)(2,1)} %param.8) | copy-start | bytes 1179652
  1.8 7.0 %copy-start.5 = (bf16[1,1,8,3,192]{4,2,3,1,0:T(8,128)(2,1)S(1)}, bf16[1,1,8,3,192]{4,2,3,1,0:T(8,128)(2,1)}, u32[]{:S(2)}) copy-start(bf16[1,1,8,3,192]{4,2,3,1,0:T(8,128)(2,1)} %param.9) | copy-start | bytes 27652
  1.8 7.0 %copy-start.6 = (s32[1,1,8,3]{2,1,3,0:T(1,128)S(1)}, s32[1,1,8,3]{2,1,3,0:T(1,128)}, u32[]{:S(2)}) copy-start(s32[1,1,8,3]{2,1,3,0:T(1,128)} %param.11) | copy-start | bytes 292
  1.8 7.0 %copy-start.7 = (s32[1,1,8,3]{2,1,3,0:T(1,128)S(1)}, s32[1,1,8,3]{2,1,3,0:T(1,128)}, u32[]{:S(2)}) copy-start(s32[1,1,8,3]{2,1,3,0:T(1,128)} %param.10) | copy-start | bytes 292
  1.9 11.8 %copy-start.1 = (f32[3,16,16,256]{3,2,1,0:T(8,128)S(1)}, f32[3,16,16,256]{3,2,1,0:T(8,128)}, u32[]{:S(2)}) copy-start(f32[3,16,16,256]{3,2,1,0:T(8,128)} %param.7) | copy-start | bytes 2359300
  1.9 11.7 %collective-permute-start.2 = (f32[3,16,256]{2,1,0:T(8,128)S(1)}, f32[3,16,256]{2,1,0:T(8,128)S(1)}, u32[]{:S(2)}, u32[]{:S(2)}) collective-permute-start(f32[3,16,256]{2,1,0:T(8,128)S(1)} %get-tuple-element.14), channel_id=1, source_target_pairs={{0,1},{1,2},{2,3},{3,0},{4,5},{5,6},{6,7},{7,4},{8,9},{9,10},{10,1... | collective-permute-start | bytes 147464 | tf_op jit(solution)/shard_map/ppermute | solution.py:371
  5.0 8.6 %collective-permute-start.3 = (f32[3,16,256]{2,1,0:T(8,128)S(1)}, f32[3,16,256]{2,1,0:T(8,128)S(1)}, u32[]{:S(2)}, u32[]{:S(2)}) collective-permute-start(f32[3,16,256]{2,1,0:T(8,128)S(1)} %get-tuple-element.15), channel_id=1, source_target_pairs={{0,3},{1,0},{2,1},{3,2},{4,7},{5,4},{6,5},{7,6},{8,11},{9,8},{10,9... | collective-permute-start | bytes 147464 | tf_op jit(solution)/shard_map/ppermute | solution.py:371
  7.1 6.5 %collective-permute-start.1 = (f32[3,16,256]{2,1,0:T(8,128)S(1)}, f32[3,16,256]{2,1,0:T(8,128)S(1)}, u32[]{:S(2)}, u32[]{:S(2)}) collective-permute-start(f32[3,16,256]{2,1,0:T(8,128)S(1)} %get-tuple-element.22), channel_id=1, source_target_pairs={{0,28},{4,0},{8,4},{12,8},{16,12},{20,16},{24,20},{28,24},{1,29},{... | collective-permute-start | bytes 147464 | tf_op jit(solution)/shard_map/ppermute | solution.py:371
  8.7 4.9 %collective-permute-start = (f32[3,16,256]{2,1,0:T(8,128)S(1)}, f32[3,16,256]{2,1,0:T(8,128)S(1)}, u32[]{:S(2)}, u32[]{:S(2)}) collective-permute-start(f32[3,16,256]{2,1,0:T(8,128)S(1)} %get-tuple-element.23), channel_id=1, source_target_pairs={{0,4},{4,8},{8,12},{12,16},{16,20},{20,24},{24,28},{28,0},{1,5},{5... | collective-permute-start | bytes 147464 | tf_op jit(solution)/shard_map/ppermute | solution.py:371
  9.6 4.1 %copy-start.4 = (bf16[1024,128]{1,0:T(8,128)(2,1)S(1)}, bf16[1024,128]{1,0:T(8,128)(2,1)}, u32[]{:S(2)}) copy-start(bf16[1024,128]{1,0:T(8,128)(2,1)} %constant.4.clone.gathers) | copy-start | bytes 786436
  9.6 12.9 %all-to-all-start = ((bf16[8,208,128]{2,1,0:T(8,128)(2,1)}), bf16[8,208,128]{2,1,0:T(8,128)(2,1)S(1)}, u32[]{:S(2)}, u32[]{:S(2)}) async-start(bf16[8,208,128]{2,1,0:T(8,128)(2,1)} %get-tuple-element.19), calls=%async_computation | async-start | bytes 851968 | tf_op jit(solution)/shard_map/all_to_all | solution.py:380
  13.7 8.8 %copy-start.3 = (bf16[128,1024]{1,0:T(8,128)(2,1)S(1)}, bf16[128,1024]{1,0:T(8,128)(2,1)}, u32[]{:S(2)}) copy-start(bf16[128,1024]{1,0:T(8,128)(2,1)} %constant.5.clone.scatters) | copy-start | bytes 786436
  15.2 1.4 %collective-permute-start.4 = (bf16[4,16,128]{2,1,0:T(8,128)(2,1)S(1)}, bf16[4,16,128]{2,1,0:T(8,128)(2,1)S(1)}, u32[]{:S(2)}, u32[]{:S(2)}) collective-permute-start(bf16[4,16,128]{2,1,0:T(8,128)(2,1)S(1)} %get-tuple-element.18.give), channel_id=1, source_target_pairs={{0,4},{4,0},{8,12},{12,8},{16,20},{20,16},{24,28},{28,24},{1,5},{5... | collective-permute-start | bytes 49160 | tf_op jit(solution)/shard_map/ppermute | solution.py:374
  16.6 8.1 %collective-permute-start.5 = (bf16[2,16,128]{2,1,0:T(8,128)(2,1)S(1)}, bf16[2,16,128]{2,1,0:T(8,128)(2,1)S(1)}, u32[]{:S(2)}, u32[]{:S(2)}) collective-permute-start(bf16[2,16,128]{2,1,0:T(8,128)(2,1)S(1)} %pad_maximum_fusion), channel_id=1, source_target_pairs={{0,8},{4,12},{8,0},{12,4},{16,24},{20,28},{24,16},{28,20},{1,9},{5... | collective-permute-start | bytes 24584 | tf_op jit(solution)/shard_map/ppermute | solution.py:374
  18.5 6.2 %collective-permute-start.6 = (bf16[2,16,128]{2,1,0:T(8,128)(2,1)S(1)}, bf16[2,16,128]{2,1,0:T(8,128)(2,1)S(1)}, u32[]{:S(2)}, u32[]{:S(2)}) collective-permute-start(bf16[2,16,128]{2,1,0:T(8,128)(2,1)S(1)} %pad_maximum_fusion.1), channel_id=1, source_target_pairs={{0,16},{4,20},{8,24},{12,28},{16,0},{20,4},{24,8},{28,12},{1,17},{... | collective-permute-start | bytes 24584 | tf_op jit(solution)/shard_map/ppermute | solution.py:374
  19.9 4.8 %collective-permute-start.7 = (bf16[2,16,128]{2,1,0:T(8,128)(2,1)S(1)}, bf16[2,16,128]{2,1,0:T(8,128)(2,1)S(1)}, u32[]{:S(2)}, u32[]{:S(2)}) collective-permute-start(bf16[2,16,128]{2,1,0:T(8,128)(2,1)S(1)} %pad_maximum_fusion.2), channel_id=1, source_target_pairs={{0,24},{4,28},{8,16},{12,20},{16,8},{20,12},{24,0},{28,4},{1,25},{... | collective-permute-start | bytes 24584 | tf_op jit(solution)/shard_map/ppermute | solution.py:374

commit v6 on v5

--- a/solution.py
+++ b/solution.py
@@ -258,8 +258,8 @@
         rows = chosen[...] * (time_step * spread_gain)
         upper = rows.astype(BF16)
         lower = (rows - upper.astype(F32)).astype(BF16)
-        pieces = jnp.dot(upper, scatters[...], preferred_element_type=F32)
-        pieces = pieces + jnp.dot(lower, scatters[...], preferred_element_type=F32)
+        both = jnp.concatenate([upper, lower], axis=1)
+        pieces = jnp.dot(both, scatters[...], preferred_element_type=F32)
         for r in range(8):
             stage[pl.ds(r, lines, stride=8), :] = pieces[:, r * 128 : r * 128 + 128]
         if count_d == group:
@@ -312,7 +312,7 @@
                 interp[c] = jnp.where(row == g, lines[c : c + 1], interp[c])
         for c in range(3):
             at = pl.ds(k * group, group)
-            target = targets[c, at, :].astype(F32)
+            target = (targets[c] if count_d == group else targets[c, at, :]).astype(F32)
             out[c, at, :] = jnp.where(live[at, :] >= 0, (target - interp[c]) / time_step, 0.0)
 
     each(count_d // group, batch)
@@ -405,7 +405,7 @@
         compiler_params=params,
         cost_estimate=pl.CostEstimate(flops=10**8, bytes_accessed=4 * 10**6, transcendentals=0),
         name="spread",
-    )(slots, own, field, keep, give, arrived, jnp.asarray(shifts().T))
+    )(slots, own, field, keep, give, arrived, jnp.asarray(np.tile(shifts().T, (2, 1))))
     force = pl.pallas_call(
         functools.partial(owner_kernel, dims),
         out_shape=jax.ShapeDtypeStruct((3, count_d, width), F32),

time: 25.9 us -> 25.8 us (level)
  transfers between devices with their start and end apart: 9 -> 9, of which waited for: 2 -> 2; matrix products, arithmetic and copies ran while one was open for 0% -> 0% of each run, Pallas kernels for 18% -> 17%
where the time goes in v6:
time: 25.8 us; the launch traced here: 25.6 us
  starting transfers between devices  14.9 us (58%)
  Pallas kernels  5.46 us (21%)
  waiting for transfers between devices  3.19 us (12%)
  local copies, waits for them, and re-layouts  1.17 us (5%)
  between operations  0.79 us (3%)
    ppermute x4, starting transfers between devices, ring(): return lax.ppermute(x, axis, [(i, (i + step) % size) for i in range(size)])  6.82 us
    ppermute x4, starting transfers between devices, swap(): lax.ppermute(x, 'gx', [(i, i ^ mask) for i in range(lax.axis_size('gx'))])  4.05 us
    all_to_all x1, starting transfers between devices, shards(): lax.all_to_all(chunk, 'gx', split_axis=0, concat_axis=0, tiled=True)  4.05 us
    all_to_all x1, waiting for transfers between devices, shards(): lax.all_to_all(chunk, 'gx', split_axis=0, concat_axis=0, tiled=True)  2.34 us
    pallas_call x1, Pallas kernels, shards(): pl.pallas_call(functools.partial(spread_kernel, dims), out_shape=(jax.Sha...  2.14 us
    pallas_call x1, Pallas kernels, shards(): pl.pallas_call(functools.partial(predict_kernel, dims), out_shape=(jax.Sh...  1.49 us
    unnamed x16, local copies, waits for them, and re-layouts  1.16 us
    pallas_call x1, Pallas kernels, shards(): pl.pallas_call(functools.partial(owner_kernel, dims), out_shape=jax.Shape...  0.94 us
  transfers between devices with their start and end apart: 9, of which 2 were waited for; matrix products, arithmetic and copies ran while one was open for 0% of the time, Pallas kernels for 17%

profile of v6, /device:TPU:0, one launch (start us, length us, event | category | flops | bytes accessed | tf_op | source)
XLA Modules:
  0.0 25.6 jit_solution(15832001992087139923)
XLA Ops:
  0.6 0.0 copy-start
  0.6 1.1 %copy-done = f32[3,16,16,256]{3,2,1,0:T(8,128)S(1)} copy-done((f32[3,16,16,256]{3,2,1,0:T(8,128)S(1)}, f32[3,16,16,256]{3,2,1,0:T(8,128)}, u32[]{:S(2)}) %copy-start) | copy-done | bytes 786456
  1.8 0.0 copy-start.2
  1.8 0.0 copy-start.5
  1.8 0.0 copy-start.6
  1.8 0.0 copy-start.7
  1.8 0.1 faces.1
  1.9 0.0 copy-start.1
  1.9 3.1 %collective-permute-start.2 = (f32[3,16,256]{2,1,0:T(8,128)S(1)}, f32[3,16,256]{2,1,0:T(8,128)S(1)}, u32[]{:S(2)}, u32[]{:S(2)}) collective-permute-start(f32[3,16,256]{2,1,0:T(8,128)S(1)} %get-tuple-element.14), channel_id=1, source_target_pairs={{0,1},{1,2},{2,3},{3,0},{4,5},{5,6},{6,7},{7,4},{8,9},{9,10},{10,1... | collective-permute-start | bytes 147464 | tf_op jit(solution)/shard_map/ppermute | solution.py:371
  5.0 2.1 %collective-permute-start.3 = (f32[3,16,256]{2,1,0:T(8,128)S(1)}, f32[3,16,256]{2,1,0:T(8,128)S(1)}, u32[]{:S(2)}, u32[]{:S(2)}) collective-permute-start(f32[3,16,256]{2,1,0:T(8,128)S(1)} %get-tuple-element.15), channel_id=1, source_target_pairs={{0,3},{1,0},{2,1},{3,2},{4,7},{5,4},{6,5},{7,6},{8,11},{9,8},{10,9... | collective-permute-start | bytes 147464 | tf_op jit(solution)/shard_map/ppermute | solution.py:371
  7.1 1.7 %collective-permute-start.1 = (f32[3,16,256]{2,1,0:T(8,128)S(1)}, f32[3,16,256]{2,1,0:T(8,128)S(1)}, u32[]{:S(2)}, u32[]{:S(2)}) collective-permute-start(f32[3,16,256]{2,1,0:T(8,128)S(1)} %get-tuple-element.22), channel_id=1, source_target_pairs={{0,28},{4,0},{8,4},{12,8},{16,12},{20,16},{24,20},{28,24},{1,29},{... | collective-permute-start | bytes 147464 | tf_op jit(solution)/shard_map/ppermute | solution.py:371
  8.7 0.0 collective-permute-start
  8.7 0.0 copy-done.2
  8.7 0.0 copy-done.5
  8.8 0.0 copy-done.6
  8.8 0.0 copy-done.7
  8.8 0.8 %pack.1 = (bf16[8,208,128]{2,1,0:T(8,128)(2,1)}, s32[1,3,1,8]{3,2,1,0:T(1,128)S(1)}, s32[1,3,1,8]{3,2,1,0:T(1,128)S(1)}) custom-call(bf16[8,192,128]{2,1,0:T(8,128)(2,1)S(1)} %bitcast.21, bf16[3,8,192]{2,1,0:T(8,128)(2,1)S(1)} %bitcast.23, s32[1,3,1,8]{3,2,1,0:T(1,128)S(1)} %bitcast.25, s32[1,3,1,8]{3,2,1,0:T(1,128)S(1)} %bitcast.26), custom_call_target="tpu_custom_call" | custom-call | tf_op jit(solution)/shard_map/pack/pallas_call | solution.py:355
  9.6 0.0 copy-start.4
  9.6 4.0 %all-to-all-start = ((bf16[8,208,128]{2,1,0:T(8,128)(2,1)}), bf16[8,208,128]{2,1,0:T(8,128)(2,1)S(1)}, u32[]{:S(2)}, u32[]{:S(2)}) async-start(bf16[8,208,128]{2,1,0:T(8,128)(2,1)} %get-tuple-element.19), calls=%async_computation | async-start | bytes 851968 | tf_op jit(solution)/shard_map/all_to_all | solution.py:380
  13.6 0.0 collective-permute-done.2.y_before
  13.6 0.0 collective-permute-done.3.y_after
  13.6 0.0 collective-permute-done.1.x_after
  13.6 0.0 collective-permute-done.x_before
  13.6 0.0 copy-done.1
  13.7 0.0 copy-done.4
  13.7 0.0 copy-start.3
  13.7 1.5 %predict.1 = (f32[2,784,128]{2,1,0:T(8,128)S(1)}, bf16[4,16,128]{2,1,0:T(8,128)(2,1)S(1)}, bf16[4,16,128]{2,1,0:T(8,128)(2,1)S(1)}) custom-call(s32[1,3,1,8]{3,2,1,0:T(1,128)S(1)} %get-tuple-element.12.table, f32[768,256]{1,0:T(8,128)S(1)} %bitcast.20, f32[3,16,256]{2,1,0:T(8,128)S(1)} %collective-permute-done.x_before, ...), custom_call_target="tpu_custom_call" | custom-call | tf_op jit(solution)/shard_map/predict/pallas_call | solution.py:381
  15.2 0.6 %collective-permute-start.4 = (bf16[4,16,128]{2,1,0:T(8,128)(2,1)S(1)}, bf16[4,16,128]{2,1,0:T(8,128)(2,1)S(1)}, u32[]{:S(2)}, u32[]{:S(2)}) collective-permute-start(bf16[4,16,128]{2,1,0:T(8,128)(2,1)S(1)} %get-tuple-element.18.give), channel_id=1, source_target_pairs={{0,4},{4,0},{8,12},{12,8},{16,20},{20,16},{24,28},{28,24},{1,5},{5... | collective-permute-start | bytes 49160 | tf_op jit(solution)/shard_map/ppermute | solution.py:374
  15.7 0.8 %collective-permute-done.4.first = bf16[4,16,128]{2,1,0:T(8,128)(2,1)S(1)} collective-permute-done((bf16[4,16,128]{2,1,0:T(8,128)(2,1)S(1)}, bf16[4,16,128]{2,1,0:T(8,128)(2,1)S(1)}, u32[]{:S(2)}, u32[]{:S(2)}) %collective-permute-start.4) | collective-permute-done | bytes 16416 | tf_op jit(solution)/shard_map/ppermute | solution.py:374
  16.6 1.9 %collective-permute-start.5 = (bf16[2,16,128]{2,1,0:T(8,128)(2,1)S(1)}, bf16[2,16,128]{2,1,0:T(8,128)(2,1)S(1)}, u32[]{:S(2)}, u32[]{:S(2)}) collective-permute-start(bf16[2,16,128]{2,1,0:T(8,128)(2,1)S(1)} %pad_maximum_fusion), channel_id=1, source_target_pairs={{0,8},{4,12},{8,0},{12,4},{16,24},{20,28},{24,16},{28,20},{1,9},{5... | collective-permute-start | bytes 24584 | tf_op jit(solution)/shard_map/ppermute | solution.py:374
  18.5 1.5 %collective-permute-start.6 = (bf16[2,16,128]{2,1,0:T(8,128)(2,1)S(1)}, bf16[2,16,128]{2,1,0:T(8,128)(2,1)S(1)}, u32[]{:S(2)}, u32[]{:S(2)}) collective-permute-start(bf16[2,16,128]{2,1,0:T(8,128)(2,1)S(1)} %pad_maximum_fusion.1), channel_id=1, source_target_pairs={{0,16},{4,20},{8,24},{12,28},{16,0},{20,4},{24,8},{28,12},{1,17},{... | collective-permute-start | bytes 24584 | tf_op jit(solution)/shard_map/ppermute | solution.py:374
  19.9 0.2 collective-permute-start.7
  20.1 2.3 %all-to-all-done.blocks = bf16[8,208,128]{2,1,0:T(8,128)(2,1)S(1)} async-done(((bf16[8,208,128]{2,1,0:T(8,128)(2,1)}), bf16[8,208,128]{2,1,0:T(8,128)(2,1)S(1)}, u32[]{:S(2)}, u32[]{:S(2)}) %all-to-all-start) | async-done | bytes 426016 | tf_op jit(solution)/shard_map/all_to_all | solution.py:380
  22.4 0.0 copy-done.3
  22.4 2.1 %spread.1 = (f32[768,256]{1,0:T(8,128)}, s32[8,192]{1,0:T(8,128)S(1)}) custom-call(s32[1,3,1,8]{3,2,1,0:T(1,128)S(1)} %get-tuple-element.12.table, s32[1,3,1,8]{3,2,1,0:T(1,128)S(1)} %get-tuple-element.13.own_table, f32[2,784,128]{2,1,0:T(8,128)S(1)} %get-tuple-element.16.before, bf16[4,16,128]{2,1,0:T(8,128)(2,1)S(1)} %get-tuple-element.17.keep, ...), custom_call_target="tpu_custom_call" | custom-call | flops 100000000 | bytes 4000000 | tf_op jit(solution)/shard_map/spread/pallas_call | solution.py:392
  24.6 0.0 collective-permute-done.5.rest_0_
  24.6 0.0 collective-permute-done.6.rest_1_
  24.6 0.0 collective-permute-done.7.rest_2_
  24.6 0.9 %owner.1 = f32[3,8,192]{2,1,0:T(8,128)} custom-call(s32[8,192]{1,0:T(8,128)S(1)} %get-tuple-element.21.live, bf16[3,8,192]{2,1,0:T(8,128)(2,1)S(1)} %bitcast.24, bf16[8,192,128]{2,1,0:T(8,128)(2,1)S(1)} %bitcast.22, bf16[4,16,128]{2,1,0:T(8,128)(2,1)S(1)} %get-tuple-element.17.keep, bf16[4,16,128]{2,1,0:T(8,128)(2,1)S(1)} %collective-permute-done.4.first, ...), custom_call_target="tpu_custom_call" | custom-call | tf_op jit(solution)/shard_map/owner/pallas_call | solution.py:409
  (6 shorter events, 0.0 us)
Async XLA Ops:
  0.6 1.1 %copy-start = (f32[3,16,16,256]{3,2,1,0:T(8,128)S(1)}, f32[3,16,16,256]{3,2,1,0:T(8,128)}, u32[]{:S(2)}) copy-start(f32[3,16,16,256]{3,2,1,0:T(8,128)} %param.7) | copy-start | bytes 2359300
  1.8 7.0 %copy-start.2 = (bf16[1,1,8,3,64,128]{5,4,3,2,1,0:T(8,128)(2,1)S(1)}, bf16[1,1,8,3,64,128]{5,4,3,2,1,0:T(8,128)(2,1)}, u32[]{:S(2)}) copy-start(bf16[1,1,8,3,64,128]{5,4,3,2,1,0:T(8,128)(2,1)} %param.8) | copy-start | bytes 1179652
  1.8 7.0 %copy-start.5 = (bf16[1,1,8,3,192]{4,2,3,1,0:T(8,128)(2,1)S(1)}, bf16[1,1,8,3,192]{4,2,3,1,0:T(8,128)(2,1)}, u32[]{:S(2)}) copy-start(bf16[1,1,8,3,192]{4,2,3,1,0:T(8,128)(2,1)} %param.9) | copy-start | bytes 27652
  1.8 7.0 %copy-start.6 = (s32[1,1,8,3]{2,1,3,0:T(1,128)S(1)}, s32[1,1,8,3]{2,1,3,0:T(1,128)}, u32[]{:S(2)}) copy-start(s32[1,1,8,3]{2,1,3,0:T(1,128)} %param.11) | copy-start | bytes 292
  1.8 7.0 %copy-start.7 = (s32[1,1,8,3]{2,1,3,0:T(1,128)S(1)}, s32[1,1,8,3]{2,1,3,0:T(1,128)}, u32[]{:S(2)}) copy-start(s32[1,1,8,3]{2,1,3,0:T(1,128)} %param.10) | copy-start | bytes 292
  1.9 11.8 %copy-start.1 = (f32[3,16,16,256]{3,2,1,0:T(8,128)S(1)}, f32[3,16,16,256]{3,2,1,0:T(8,128)}, u32[]{:S(2)}) copy-start(f32[3,16,16,256]{3,2,1,0:T(8,128)} %param.7) | copy-start | bytes 2359300
  1.9 11.7 %collective-permute-start.2 = (f32[3,16,256]{2,1,0:T(8,128)S(1)}, f32[3,16,256]{2,1,0:T(8,128)S(1)}, u32[]{:S(2)}, u32[]{:S(2)}) collective-permute-start(f32[3,16,256]{2,1,0:T(8,128)S(1)} %get-tuple-element.14), channel_id=1, source_target_pairs={{0,1},{1,2},{2,3},{3,0},{4,5},{5,6},{6,7},{7,4},{8,9},{9,10},{10,1... | collective-permute-start | bytes 147464 | tf_op jit(solution)/shard_map/ppermute | solution.py:371
  5.0 8.6 %collective-permute-start.3 = (f32[3,16,256]{2,1,0:T(8,128)S(1)}, f32[3,16,256]{2,1,0:T(8,128)S(1)}, u32[]{:S(2)}, u32[]{:S(2)}) collective-permute-start(f32[3,16,256]{2,1,0:T(8,128)S(1)} %get-tuple-element.15), channel_id=1, source_target_pairs={{0,3},{1,0},{2,1},{3,2},{4,7},{5,4},{6,5},{7,6},{8,11},{9,8},{10,9... | collective-permute-start | bytes 147464 | tf_op jit(solution)/shard_map/ppermute | solution.py:371
  7.1 6.5 %collective-permute-start.1 = (f32[3,16,256]{2,1,0:T(8,128)S(1)}, f32[3,16,256]{2,1,0:T(8,128)S(1)}, u32[]{:S(2)}, u32[]{:S(2)}) collective-permute-start(f32[3,16,256]{2,1,0:T(8,128)S(1)} %get-tuple-element.22), channel_id=1, source_target_pairs={{0,28},{4,0},{8,4},{12,8},{16,12},{20,16},{24,20},{28,24},{1,29},{... | collective-permute-start | bytes 147464 | tf_op jit(solution)/shard_map/ppermute | solution.py:371
  8.7 4.9 %collective-permute-start = (f32[3,16,256]{2,1,0:T(8,128)S(1)}, f32[3,16,256]{2,1,0:T(8,128)S(1)}, u32[]{:S(2)}, u32[]{:S(2)}) collective-permute-start(f32[3,16,256]{2,1,0:T(8,128)S(1)} %get-tuple-element.23), channel_id=1, source_target_pairs={{0,4},{4,8},{8,12},{12,16},{16,20},{20,24},{24,28},{28,0},{1,5},{5... | collective-permute-start | bytes 147464 | tf_op jit(solution)/shard_map/ppermute | solution.py:371
  9.6 4.1 %copy-start.4 = (bf16[1024,128]{1,0:T(8,128)(2,1)S(1)}, bf16[1024,128]{1,0:T(8,128)(2,1)}, u32[]{:S(2)}) copy-start(bf16[1024,128]{1,0:T(8,128)(2,1)} %constant.4.clone.gathers) | copy-start | bytes 786436
  9.6 12.9 %all-to-all-start = ((bf16[8,208,128]{2,1,0:T(8,128)(2,1)}), bf16[8,208,128]{2,1,0:T(8,128)(2,1)S(1)}, u32[]{:S(2)}, u32[]{:S(2)}) async-start(bf16[8,208,128]{2,1,0:T(8,128)(2,1)} %get-tuple-element.19), calls=%async_computation | async-start | bytes 851968 | tf_op jit(solution)/shard_map/all_to_all | solution.py:380
  13.7 8.8 %copy-start.3 = (bf16[256,1024]{1,0:T(8,128)(2,1)S(1)}, bf16[256,1024]{1,0:T(8,128)(2,1)}, u32[]{:S(2)}) copy-start(bf16[256,1024]{1,0:T(8,128)(2,1)} %constant.5.clone.scatters) | copy-start | bytes 1572868
  15.2 1.4 %collective-permute-start.4 = (bf16[4,16,128]{2,1,0:T(8,128)(2,1)S(1)}, bf16[4,16,128]{2,1,0:T(8,128)(2,1)S(1)}, u32[]{:S(2)}, u32[]{:S(2)}) collective-permute-start(bf16[4,16,128]{2,1,0:T(8,128)(2,1)S(1)} %get-tuple-element.18.give), channel_id=1, source_target_pairs={{0,4},{4,0},{8,12},{12,8},{16,20},{20,16},{24,28},{28,24},{1,5},{5... | collective-permute-start | bytes 49160 | tf_op jit(solution)/shard_map/ppermute | solution.py:374
  16.6 8.0 %collective-permute-start.5 = (bf16[2,16,128]{2,1,0:T(8,128)(2,1)S(1)}, bf16[2,16,128]{2,1,0:T(8,128)(2,1)S(1)}, u32[]{:S(2)}, u32[]{:S(2)}) collective-permute-start(bf16[2,16,128]{2,1,0:T(8,128)(2,1)S(1)} %pad_maximum_fusion), channel_id=1, source_target_pairs={{0,8},{4,12},{8,0},{12,4},{16,24},{20,28},{24,16},{28,20},{1,9},{5... | collective-permute-start | bytes 24584 | tf_op jit(solution)/shard_map/ppermute | solution.py:374
  18.5 6.1 %collective-permute-start.6 = (bf16[2,16,128]{2,1,0:T(8,128)(2,1)S(1)}, bf16[2,16,128]{2,1,0:T(8,128)(2,1)S(1)}, u32[]{:S(2)}, u32[]{:S(2)}) collective-permute-start(bf16[2,16,128]{2,1,0:T(8,128)(2,1)S(1)} %pad_maximum_fusion.1), channel_id=1, source_target_pairs={{0,16},{4,20},{8,24},{12,28},{16,0},{20,4},{24,8},{28,12},{1,17},{... | collective-permute-start | bytes 24584 | tf_op jit(solution)/shard_map/ppermute | solution.py:374
  19.9 4.7 %collective-permute-start.7 = (bf16[2,16,128]{2,1,0:T(8,128)(2,1)S(1)}, bf16[2,16,128]{2,1,0:T(8,128)(2,1)S(1)}, u32[]{:S(2)}, u32[]{:S(2)}) collective-permute-start(bf16[2,16,128]{2,1,0:T(8,128)(2,1)S(1)} %pad_maximum_fusion.2), channel_id=1, source_target_pairs={{0,24},{4,28},{8,16},{12,20},{16,8},{20,12},{24,0},{28,4},{1,25},{... | collective-permute-start | bytes 24584 | tf_op jit(solution)/shard_map/ppermute | solution.py:374
